TPU v7x, 32 devices: a whole 2x2x4 slice. The times are simulated.
32 devices in a mesh: fsdp: 4 (over y, x), ctx: 4 (over z), tp: 2 (over core).
Axes of the slice: x: 2, y: 2, z: 4, core: 2. Of those that a mesh axis runs over, the one named last changes fastest.
Arguments:
- tokens: bfloat16 [4, 768, 2048], P('fsdp', 'ctx'), may hold values from -6 to 6
- out_grad: bfloat16 [4, 768, 2048], P('fsdp', 'ctx'), may hold values from -6 to 6
- lengths: int32 [4, 2], P('fsdp'), may hold values from 192 to 576, as said below
- w_query: bfloat16 [2048, 2048], P(('fsdp', 'ctx'), 'tp'), may hold values from -0.015625 to 0.015625
- w_key: bfloat16 [2048, 2048], P(('fsdp', 'ctx'), 'tp'), may hold values from -0.125 to 0.125
- w_value: bfloat16 [2048, 2048], P(('fsdp', 'ctx'), 'tp'), may hold values from -0.125 to 0.125
- w_out: bfloat16 [2048, 2048], P(('fsdp', 'ctx'), 'tp'), may hold values from -4 to 4
- w_gate: bfloat16 [2048, 5120], P(('fsdp', 'ctx'), 'tp'), may hold values from -0.125 to 0.125
- w_up: bfloat16 [2048, 5120], P(('fsdp', 'ctx'), 'tp'), may hold values from -0.125 to 0.125
- w_down: bfloat16 [2048, 5120], P(('fsdp', 'ctx'), 'tp'), may hold values from -0.125 to 0.125
- gain_attn: bfloat16 [2048], P(('fsdp', 'ctx')), may hold values from 0.5 to 1.5
- gain_ffn: bfloat16 [2048], P(('fsdp', 'ctx')), may hold values from 0.5 to 1.5
- bias_table: bfloat16 [32, 32], P('tp'), may hold values from -4 to 4
- clip_limit: float32 [32], P('tp'), may hold values from 0.5 to 6
Outputs:
- mixed_out: bfloat16 [4, 768, 2048], P('fsdp', 'ctx')
- grad_tokens: bfloat16 [4, 768, 2048], P('fsdp', 'ctx')
- grad_w_query: float32 [2048, 2048], P(('fsdp', 'ctx'), 'tp')
- grad_w_key: float32 [2048, 2048], P(('fsdp', 'ctx'), 'tp')
- grad_w_value: float32 [2048, 2048], P(('fsdp', 'ctx'), 'tp')
- grad_w_out: float32 [2048, 2048], P(('fsdp', 'ctx'), 'tp')
- grad_w_gate: float32 [2048, 5120], P(('fsdp', 'ctx'), 'tp')
- grad_w_up: float32 [2048, 5120], P(('fsdp', 'ctx'), 'tp')
- grad_w_down: float32 [2048, 5120], P(('fsdp', 'ctx'), 'tp')
- grad_gain_attn: float32 [2048], P(('fsdp', 'ctx'))
- grad_gain_ffn: float32 [2048], P(('fsdp', 'ctx'))
- grad_table: float32 [32, 32], P('tp')
- head_peaks: float32 [32], P('tp')
- clipped_query: bfloat16 [2048, 2048], P(('fsdp', 'ctx'), 'tp')
- clipped_key: bfloat16 [2048, 2048], P(('fsdp', 'ctx'), 'tp')
Inputs may be any that keep to these rules, and one draw needn't show every extreme that they name: Each group holds two sequences packed from its first position, of lengths[g, 0] and lengths[g, 1], whose sum is at most 768; the rest is padding. Some group's first sequence has exactly 576.
All inputs are finite; a program needn't handle non-finite values.
Results may differ from a plain program's by a relative error of at most 0.024.
Values may be sent and summed in bfloat16 or wider, within the bound.
No kernel may reach another device: no remote copies, remote signals or barrier semaphores. Data moves between devices by JAX's collectives and lax.ppermute only.
A program may use at most 256 MiB of HBM per device.

v0:
```python
import math

import jax
import jax.numpy as jnp
from jax import lax
from jax.sharding import PartitionSpec as P

DK = 64
BUCKETS = 32


THRESHOLDS = (12, 16, 23, 32, 46, 64, 91)
NEGATIVE = -1e30
EPSILON = 1e-06
ROWS_CONTRACT = (((0,), (0,)), ((), ()))
COLS_CONTRACT = (((1,), (1,)), ((), ()))


def bucket_of(offset):
    distance = jnp.abs(offset)
    beyond = 8 + sum(((distance >= threshold).astype(jnp.int32) for threshold in THRESHOLDS))
    within = jnp.where(distance < 8, distance, beyond)
    return within + jnp.where(offset > 0, BUCKETS // 2, 0)


def segment_of(place, length_pair):
    first_end = length_pair[0]
    second_end = length_pair[0] + length_pair[1]
    return (place >= first_end).astype(jnp.int32) + (place >= second_end).astype(jnp.int32)


def normalize(values, gain_row):
    return (
        values * lax.rsqrt(jnp.mean(values * values, axis=-1, keepdims=True) + EPSILON) * gain_row
    )


def gelu_tanh(values):
    return jax.nn.gelu(values, approximate=True)


def outer_sum(left_side, right_side):
    return lax.dot_general(left_side, right_side, ROWS_CONTRACT, preferred_element_type=jnp.float32)


def against(left_side, right_side):
    return lax.dot_general(left_side, right_side, COLS_CONTRACT, preferred_element_type=jnp.float32)


def expand_bias(table_in, first_offset, query_count, key_count):
    diagonals = query_count + key_count - 1
    offsets = first_offset - (query_count - 1) + jnp.arange(diagonals, dtype=jnp.int32)
    onehot = (
        bucket_of(offsets)[:, None] == jnp.arange(table_in.shape[1], dtype=jnp.int32)[None, :]
    ).astype(jnp.float32)
    values = jnp.dot(table_in, onehot.T, precision=lax.Precision.HIGHEST)
    padded = jnp.pad(values, ((0, 0), (0, 1)))
    repeated = jnp.tile(padded, (1, query_count))[:, : query_count * diagonals]
    repeated = repeated.reshape(table_in.shape[0], query_count, diagonals)
    return repeated[:, :, query_count - 1 : query_count - 1 + key_count]


def shards(
    tokens,
    out_grad,
    lengths,
    w_query,
    w_key,
    w_value,
    w_out,
    w_gate,
    w_up,
    w_down,
    gain_attn,
    gain_ffn,
    bias_table,
    clip_limit,
):
    local_rows = tokens.shape[1]
    heads_here = bias_table.shape[0]
    slots_all = local_rows * lax.axis_size("ctx")
    key_block = math.gcd(slots_all, 512)
    block_count = slots_all // key_block
    first_row = lax.axis_index("ctx") * local_rows
    length_pair = lengths[0]
    row_place = first_row + jnp.arange(local_rows, dtype=jnp.int32)
    row_segment = segment_of(row_place, length_pair)
    row_valid = row_segment < 2
    inputs = tokens[0].astype(jnp.float32)
    bias_float = bias_table.astype(jnp.float32)
    gathered = (
        lax.all_gather(w_query, ("fsdp", "ctx"), axis=0, tiled=True),
        lax.all_gather(w_key, ("fsdp", "ctx"), axis=0, tiled=True),
        lax.all_gather(w_value, ("fsdp", "ctx"), axis=0, tiled=True),
        lax.all_gather(w_out, ("fsdp", "ctx"), axis=0, tiled=True),
        lax.all_gather(w_gate, ("fsdp", "ctx"), axis=0, tiled=True),
        lax.all_gather(w_up, ("fsdp", "ctx"), axis=0, tiled=True),
        lax.all_gather(w_down, ("fsdp", "ctx"), axis=0, tiled=True),
        lax.all_gather(gain_attn, ("fsdp", "ctx"), axis=0, tiled=True),
        lax.all_gather(gain_ffn, ("fsdp", "ctx"), axis=0, tiled=True),
    )
    (
        query_full,
        key_full,
        value_full,
        out_full,
        gate_full,
        up_full,
        down_full,
        gain_one,
        gain_two,
    ) = gathered
    attn_gain = gain_one.astype(jnp.float32)
    ffn_gain = gain_two.astype(jnp.float32)
    normed = normalize(inputs, attn_gain).astype(jnp.bfloat16)
    queries = jnp.dot(normed, query_full, preferred_element_type=jnp.float32).astype(jnp.bfloat16)
    key_rows = jnp.dot(normed, key_full, preferred_element_type=jnp.float32).astype(jnp.bfloat16)
    value_rows = jnp.dot(normed, value_full, preferred_element_type=jnp.float32).astype(
        jnp.bfloat16
    )
    keys_all, values_all = (
        lax.all_gather(key_rows, "ctx", axis=0, tiled=True),
        lax.all_gather(value_rows, "ctx", axis=0, tiled=True),
    )
    query_heads = queries.reshape(local_rows, heads_here, DK)

    def key_slice(source, key_start):
        return lax.dynamic_slice_in_dim(source, key_start, key_block, 0).reshape(
            key_block, heads_here, DK
        )

    def block_masks(key_start):
        key_segment = segment_of(key_start + jnp.arange(key_block, dtype=jnp.int32), length_pair)
        same_part = row_segment[:, None] == key_segment[None, :]
        both_valid = same_part & row_valid[:, None]
        return (both_valid, same_part)

    def forward_step(running, block_index):
        peak_now, highest, weight_sum, summed = running
        key_start = block_index * key_block
        key_heads = key_slice(keys_all, key_start)
        value_heads = key_slice(values_all, key_start)
        logits = jnp.einsum(
            "qhd,khd->hqk", query_heads, key_heads, preferred_element_type=jnp.float32
        )
        both_valid, same_part = block_masks(key_start)
        peak_now = jnp.maximum(
            peak_now, jnp.max(jnp.where(both_valid[None], logits, NEGATIVE), axis=(1, 2))
        )
        scores = jnp.where(
            same_part[None],
            logits + expand_bias(bias_float, key_start - first_row, local_rows, key_block),
            NEGATIVE,
        )
        new_highest = jnp.maximum(highest, jnp.max(scores, axis=2))
        weights = jnp.exp(scores - new_highest[:, :, None])
        shrink = jnp.exp(highest - new_highest)
        weight_sum = weight_sum * shrink + jnp.sum(weights, axis=2)
        summed = summed * shrink.T[:, :, None] + jnp.einsum(
            "hqk,khd->qhd",
            weights.astype(jnp.bfloat16),
            value_heads,
            preferred_element_type=jnp.float32,
        )
        return ((peak_now, new_highest, weight_sum, summed), None)

    start_state = (
        jnp.full((heads_here,), NEGATIVE, jnp.float32),
        jnp.full((heads_here, local_rows), NEGATIVE, jnp.float32),
        jnp.zeros((heads_here, local_rows), jnp.float32),
        jnp.zeros((local_rows, heads_here, DK), jnp.float32),
    )
    final_state, _ = lax.scan(forward_step, start_state, jnp.arange(block_count))
    peak_now, highest, weight_sum, summed = final_state
    log_total = highest + jnp.log(weight_sum)
    mixed_float = (summed / weight_sum.T[:, :, None]).reshape(local_rows, heads_here * DK)
    mixed_rows = mixed_float.astype(jnp.bfloat16)
    branch = lax.psum(against(mixed_rows, out_full).astype(jnp.bfloat16), "tp").astype(jnp.float32)
    hidden_state = inputs + branch
    normed_ffn = normalize(hidden_state, ffn_gain).astype(jnp.bfloat16)
    gate_pre = jnp.dot(normed_ffn, gate_full, preferred_element_type=jnp.float32)
    upward = jnp.dot(normed_ffn, up_full, preferred_element_type=jnp.float32)
    activated, gelu_back = jax.vjp(gelu_tanh, gate_pre)
    product = (activated * upward).astype(jnp.bfloat16)
    ffn_out = lax.psum(against(product, down_full).astype(jnp.bfloat16), "tp").astype(jnp.float32)
    mixed_out = (hidden_state + ffn_out).astype(jnp.bfloat16)[None]
    head_peaks = lax.pmax(peak_now, ("fsdp", "ctx"))
    factor = jnp.sqrt(clip_limit / jnp.maximum(head_peaks, clip_limit))

    def clipped(weight):
        scaled = (
            weight.astype(jnp.float32).reshape(weight.shape[0], heads_here, DK)
            * factor[None, :, None]
        )
        return scaled.reshape(weight.shape).astype(jnp.bfloat16)

    grad_out = out_grad[0].astype(jnp.float32) * row_valid.astype(jnp.float32)[:, None]
    grad_branch_ffn = grad_out.astype(jnp.bfloat16)
    gathered = (
        lax.all_gather(w_query, ("fsdp", "ctx"), axis=0, tiled=True),
        lax.all_gather(w_key, ("fsdp", "ctx"), axis=0, tiled=True),
        lax.all_gather(w_value, ("fsdp", "ctx"), axis=0, tiled=True),
        lax.all_gather(w_out, ("fsdp", "ctx"), axis=0, tiled=True),
        lax.all_gather(w_gate, ("fsdp", "ctx"), axis=0, tiled=True),
        lax.all_gather(w_up, ("fsdp", "ctx"), axis=0, tiled=True),
        lax.all_gather(w_down, ("fsdp", "ctx"), axis=0, tiled=True),
        lax.all_gather(gain_attn, ("fsdp", "ctx"), axis=0, tiled=True),
        lax.all_gather(gain_ffn, ("fsdp", "ctx"), axis=0, tiled=True),
    )
    (
        query_full,
        key_full,
        value_full,
        out_full,
        gate_full,
        up_full,
        down_full,
        gain_one,
        gain_two,
    ) = gathered
    grad_w_down = outer_sum(grad_branch_ffn, product)
    grad_product = jnp.dot(grad_branch_ffn, down_full, preferred_element_type=jnp.float32)
    grad_gate = gelu_back(grad_product * upward)[0].astype(jnp.bfloat16)
    grad_upward = (grad_product * activated).astype(jnp.bfloat16)
    grad_w_gate = outer_sum(normed_ffn, grad_gate)
    grad_w_up = outer_sum(normed_ffn, grad_upward)
    grad_normed_ffn = lax.psum(
        (against(grad_gate, gate_full) + against(grad_upward, up_full)).astype(jnp.bfloat16), "tp"
    ).astype(jnp.float32)
    _, ffn_norm_back = jax.vjp(normalize, hidden_state, ffn_gain)
    grad_hidden_norm, grad_gain_two = ffn_norm_back(grad_normed_ffn)
    grad_hidden = grad_out + grad_hidden_norm
    ffn_sums = (
        lax.psum_scatter(grad_w_gate, ("fsdp", "ctx"), scatter_dimension=0, tiled=True),
        lax.psum_scatter(grad_w_up, ("fsdp", "ctx"), scatter_dimension=0, tiled=True),
        lax.psum_scatter(grad_w_down, ("fsdp", "ctx"), scatter_dimension=0, tiled=True),
        lax.psum_scatter(grad_gain_two, ("fsdp", "ctx"), scatter_dimension=0, tiled=True),
    )
    grad_branch = grad_hidden.astype(jnp.bfloat16)
    grad_w_out = outer_sum(grad_branch, mixed_rows)
    grad_mixed = jnp.dot(grad_branch, out_full, preferred_element_type=jnp.float32).astype(
        jnp.bfloat16
    )
    grad_heads = grad_mixed.reshape(local_rows, heads_here, DK)
    row_delta = jnp.sum(
        (grad_mixed.astype(jnp.float32) * mixed_float).reshape(local_rows, heads_here, DK), axis=2
    ).T
    keys_all, values_all = (
        lax.all_gather(key_rows, "ctx", axis=0, tiled=True),
        lax.all_gather(value_rows, "ctx", axis=0, tiled=True),
    )

    def backward_step(running, block_index):
        grad_query, grad_bias = running
        key_start = block_index * key_block
        key_heads = key_slice(keys_all, key_start)
        value_heads = key_slice(values_all, key_start)
        logits = jnp.einsum(
            "qhd,khd->hqk", query_heads, key_heads, preferred_element_type=jnp.float32
        )
        both_valid, same_part = block_masks(key_start)

        def place_bias(table_in):
            return expand_bias(table_in, key_start - first_row, local_rows, key_block)

        bias_block, bias_back = jax.vjp(place_bias, bias_float)
        scores = jnp.where(same_part[None], logits + bias_block, NEGATIVE)
        chance = jnp.exp(scores - log_total[:, :, None])
        grad_chance = jnp.einsum(
            "qhd,khd->hqk", grad_heads, value_heads, preferred_element_type=jnp.float32
        )
        grad_scores = chance * (grad_chance - row_delta[:, :, None])
        grad_bias = grad_bias + bias_back(grad_scores)[0]
        rounded = grad_scores.astype(jnp.bfloat16)
        grad_query = grad_query + jnp.einsum(
            "hqk,khd->qhd", rounded, key_heads, preferred_element_type=jnp.float32
        )
        grad_keys = jnp.einsum(
            "hqk,qhd->khd", rounded, query_heads, preferred_element_type=jnp.float32
        ).reshape(key_block, heads_here * DK)
        grad_values = jnp.einsum(
            "hqk,qhd->khd",
            chance.astype(jnp.bfloat16),
            grad_heads,
            preferred_element_type=jnp.float32,
        ).reshape(key_block, heads_here * DK)
        return ((grad_query, grad_bias), jnp.concatenate([grad_keys, grad_values], axis=1))

    back_state = (
        jnp.zeros((local_rows, heads_here, DK), jnp.float32),
        jnp.zeros(bias_float.shape, jnp.float32),
    )
    back_final, pieces = lax.scan(backward_step, back_state, jnp.arange(block_count))
    grad_query, grad_bias = back_final
    key_value_terms = pieces.reshape(slots_all, 2 * heads_here * DK)
    key_value_mine = lax.psum_scatter(
        key_value_terms.astype(jnp.bfloat16), "ctx", scatter_dimension=0, tiled=True
    ).astype(jnp.float32)
    head_width = heads_here * DK
    grad_key_rows = key_value_mine[:, :head_width].astype(jnp.bfloat16)
    grad_value_rows = key_value_mine[:, head_width:].astype(jnp.bfloat16)
    grad_query_rows = grad_query.reshape(local_rows, head_width).astype(jnp.bfloat16)
    grad_w_query = outer_sum(normed, grad_query_rows)
    grad_w_key = outer_sum(normed, grad_key_rows)
    grad_w_value = outer_sum(normed, grad_value_rows)
    grad_normed_part = (
        against(grad_query_rows, query_full)
        + against(grad_key_rows, key_full)
        + against(grad_value_rows, value_full)
    )
    grad_normed = lax.psum(grad_normed_part.astype(jnp.bfloat16), "tp").astype(jnp.float32)
    _, attn_norm_back = jax.vjp(normalize, inputs, attn_gain)
    grad_inputs_norm, grad_gain_one = attn_norm_back(grad_normed)
    grad_tokens = (grad_hidden + grad_inputs_norm).astype(jnp.bfloat16)[None]
    attn_sums = (
        lax.psum_scatter(grad_w_query, ("fsdp", "ctx"), scatter_dimension=0, tiled=True),
        lax.psum_scatter(grad_w_key, ("fsdp", "ctx"), scatter_dimension=0, tiled=True),
        lax.psum_scatter(grad_w_value, ("fsdp", "ctx"), scatter_dimension=0, tiled=True),
        lax.psum_scatter(grad_w_out, ("fsdp", "ctx"), scatter_dimension=0, tiled=True),
        lax.psum_scatter(grad_gain_one, ("fsdp", "ctx"), scatter_dimension=0, tiled=True),
    )
    grad_table = lax.psum(grad_bias, ("fsdp", "ctx"))
    return (
        mixed_out,
        grad_tokens,
        attn_sums[0],
        attn_sums[1],
        attn_sums[2],
        attn_sums[3],
        ffn_sums[0],
        ffn_sums[1],
        ffn_sums[2],
        attn_sums[4],
        ffn_sums[3],
        grad_table,
        head_peaks,
        clipped(w_query),
        clipped(w_key),
    )


def solution(mesh):
    return jax.shard_map(
        shards,
        mesh=mesh,
        in_specs=(
            P("fsdp", "ctx", None),
            P("fsdp", "ctx", None),
            P("fsdp", None),
            P(("fsdp", "ctx"), "tp"),
            P(("fsdp", "ctx"), "tp"),
            P(("fsdp", "ctx"), "tp"),
            P(("fsdp", "ctx"), "tp"),
            P(("fsdp", "ctx"), "tp"),
            P(("fsdp", "ctx"), "tp"),
            P(("fsdp", "ctx"), "tp"),
            P(("fsdp", "ctx")),
            P(("fsdp", "ctx")),
            P("tp", None),
            P("tp"),
        ),
        out_specs=(
            P("fsdp", "ctx", None),
            P("fsdp", "ctx", None),
            P(("fsdp", "ctx"), "tp"),
            P(("fsdp", "ctx"), "tp"),
            P(("fsdp", "ctx"), "tp"),
            P(("fsdp", "ctx"), "tp"),
            P(("fsdp", "ctx"), "tp"),
            P(("fsdp", "ctx"), "tp"),
            P(("fsdp", "ctx"), "tp"),
            P(("fsdp", "ctx")),
            P(("fsdp", "ctx")),
            P("tp", None),
            P("tp"),
            P(("fsdp", "ctx"), "tp"),
            P(("fsdp", "ctx"), "tp"),
        ),
        check_vma=False,
    )
```

profile of v0, /device:TPU:0, one launch (start us, length us, event | category | flops | bytes accessed | tf_op | source)
XLA Modules:
  0.0 3266.2 jit_solution(1591968284427487196)
XLA Ops:
  9.5 42.4 %all-gather = bf16[16,1,128]{2,1,0:T(2,128)(2,1)S(1)} all-gather(bf16[1,1,128]{2,1,0:T(2,128)(2,1)} %bitcast.279), channel_id=1, replica_groups=mesh['fsdp'=4,'ctx'=4,'tp'=2] {'fsdp','ctx'}, dimensions={0}, use_global_device_ids=true | all-gather | bytes 4352 | tf_op jit(solution)/shard_map/all_gather | solution.py:99
  53.3 36.1 %all-gather.12.cloned.1.call-done = bf16[2048,1024]{1,0:T(8,128)(2,1)} async-done(((bf16[128,1024]{1,0:T(8,128)(2,1)}), bf16[2048,1024]{1,0:T(8,128)(2,1)}) %all-gather.12.cloned.1.call-update) | async-done | bytes 4194320 | tf_op jit(solution)/shard_map/all_gather | solution.py:93
  93.5 73.1 %all-gather.18.cloned.1.call-done = bf16[2048,1024]{1,0:T(8,128)(2,1)} async-done(((bf16[128,1024]{1,0:T(8,128)(2,1)}), bf16[2048,1024]{1,0:T(8,128)(2,1)}) %all-gather.18.cloned.1.call-update) | async-done | bytes 4194320 | tf_op jit(solution)/shard_map/all_gather | solution.py:94
  173.4 70.5 %all-gather.16.cloned.1.call-done = bf16[2048,1024]{1,0:T(8,128)(2,1)} async-done(((bf16[128,1024]{1,0:T(8,128)(2,1)}), bf16[2048,1024]{1,0:T(8,128)(2,1)}) %all-gather.16.cloned.1.call-update) | async-done | bytes 4194320 | tf_op jit(solution)/shard_map/all_gather | solution.py:92
  248.1 33.5 %all-gather.14.cloned.1.call-done = bf16[768,1024]{1,0:T(8,128)(2,1)} async-done(((bf16[192,1024]{1,0:T(8,128)(2,1)}), bf16[768,1024]{1,0:T(8,128)(2,1)}) %all-gather.14.cloned.1.call-update) | async-done | bytes 1572880 | tf_op jit(solution)/shard_map/all_gather | solution.py:122
  284.2 35.3 %all-gather.20.cloned.1.call-done = bf16[768,1024]{1,0:T(8,128)(2,1)} async-done(((bf16[192,1024]{1,0:T(8,128)(2,1)}), bf16[768,1024]{1,0:T(8,128)(2,1)}) %all-gather.20.cloned.1.call-update) | async-done | bytes 1572880 | tf_op jit(solution)/shard_map/all_gather | solution.py:123
  322.2 113.7 %while.40 = (s32[]{:T(128)}, f32[16]{0:T(128)S(1)}, f32[16,192]{1,0:T(8,128)S(1)}, f32[16,192]{1,0:T(8,128)S(1)}, f32[192,16,64]{0,2,1:T(8,128)}, /*index=5*/s32...) while((s32[]{:T(128)}, f32[16]{0:T(128)S(1)}, ...), condition=%wide.region_5.6_spmd.clone.clone.clone, body=%wide.region_1.5_spmd.clone.clone.clone.sunk | while | flops 211887136 | bytes 56698664 | solution.py:173
  341.9 9.0 reshape.426
  367.9 6.9 tile.41
  380.0 9.0 reshape.426
  417.8 9.0 reshape.426
  445.0 38.4 %all-gather.1 = bf16[16,1,128]{2,1,0:T(2,128)(2,1)S(1)} all-gather(bf16[1,1,128]{2,1,0:T(2,128)(2,1)S(1)} %bitcast.280), channel_id=1, replica_groups=mesh['fsdp'=4,'ctx'=4,'tp'=2] {'fsdp','ctx'}, dimensions={0}, use_global_device_ids=true | all-gather | bytes 4352 | tf_op jit(solution)/shard_map/all_gather | solution.py:100
  486.1 111.0 %all-gather.24.cloned.1.call-done = bf16[2048,2560]{1,0:T(8,128)(2,1)} async-done(((bf16[128,2560]{1,0:T(8,128)(2,1)}), bf16[2048,2560]{1,0:T(8,128)(2,1)}) %all-gather.24.cloned.1.call-update) | async-done | bytes 10485776 | tf_op jit(solution)/shard_map/all_gather | solution.py:96
  597.1 7.5 fusion.126
  604.7 126.0 %all-gather.26.cloned.1.call-done = bf16[2048,2560]{1,0:T(8,128)(2,1)} async-done(((bf16[128,2560]{1,0:T(8,128)(2,1)}), bf16[2048,2560]{1,0:T(8,128)(2,1)}) %all-gather.26.cloned.1.call-update) | async-done | bytes 10485776 | tf_op jit(solution)/shard_map/all_gather | solution.py:97
  730.7 7.4 fusion.127
  738.1 125.9 %all-gather.28.cloned.1.call-done = bf16[2048,2560]{1,0:T(8,128)(2,1)} async-done(((bf16[128,2560]{1,0:T(8,128)(2,1)}), bf16[2048,2560]{1,0:T(8,128)(2,1)}) %all-gather.28.cloned.1.call-update) | async-done | bytes 10485776 | tf_op jit(solution)/shard_map/all_gather | solution.py:98
  864.0 10.0 multiply_convert_fusion
  874.0 8.3 fusion.128
  888.1 16.2 all-reduce.14.cloned.1.call-done
  914.1 211.5 %while.41 = (s32[]{:T(128)}, f32[192,16,64]{0,2,1:T(8,128)}, f32[16,32]{1,0:T(8,128)S(1)}, bf16[3,256,2048]{2,1,0:T(8,128)(2,1)}, s32[3]{0:T(128)S(1)}, /*index=...) while((s32[]{:T(128)}, f32[192,16,64]{0,2,1:T(8,128)}, ...), condition=%wide.region_14.15_spmd.clone.clone.clone, body=%wide.region_12.14_spmd.clone.clone.clone.sunk | while | flops 519054112 | bytes 127876632 | solution.py:293
  922.3 6.3 tile.43
  934.0 8.9 reshape.427
  959.6 6.6 reshape.428
  971.5 6.4 reshape.429
  992.4 6.3 tile.43
  1004.1 8.9 reshape.427
  1029.8 6.6 reshape.428
  1041.7 6.4 reshape.429
  1063.0 6.3 tile.43
  1074.7 8.9 reshape.427
  1100.3 6.6 reshape.428
  1112.2 6.4 reshape.429
  1126.9 8.5 convolution_convert_fusion
  1137.8 49.5 %reduce-scatter.9.cloned.1.call-done = bf16[192,2048]{1,0:T(8,128)(2,1)} async-done(((bf16[768,2048]{1,0:T(8,128)(2,1)}), bf16[192,2048]{1,0:T(8,128)(2,1)}) %reduce-scatter.9.cloned.1.call-update) | async-done | bytes 786448 | tf_op jit(solution)/shard_map/reduce_scatter | solution.py:296
  1195.1 6.5 fusion.96
  1220.1 11.4 fusion.130
  1231.5 11.4 fusion.131
  1243.0 10.0 fusion.105
  1254.8 44.2 %pmax.7 = f32[16]{0:T(128)S(1)} all-reduce(f32[16]{0:T(128)S(1)} %copy-done.41), channel_id=1, replica_groups=mesh['fsdp'=4,'ctx'=4,'tp'=2] {'fsdp','ctx'}, use_global_device_ids=true, to_apply=%region_30.31 | all-reduce | flops 16 | bytes 128 | tf_op jit(solution)/shard_map/pmax | solution.py:187
  1303.0 77.8 %all-reduce.6 = (f32[2048]{0:T(1024)S(1)}, f32[2048]{0:T(1024)S(1)}, f32[16,32]{1,0:T(8,128)}) all-reduce(f32[2048]{0:T(1024)S(1)} %get-tuple-element.771, f32[2048]{0:T(1024)S(1)} %copy-done.37, f32[16,32]{1,0:T(8,128)S(1)} %get-tuple-element.397), channel_id=10, replica_groups=mesh['fsdp'=4,'ctx'=4,'tp'=2] {'fsdp','ctx'}, use_global_device_ids=true, to_apply=%region_26.27.clone | all-reduce | flops 4608 | bytes 36864
  1385.8 18.3 reduce-scatter.17.cloned.1.call-done
  1404.1 182.7 %reduce-scatter.11.cloned.1.call-done = f32[128,1024]{1,0:T(8,128)} async-done(((f32[2048,1024]{1,0:T(8,128)}), f32[128,1024]{1,0:T(8,128)}) %reduce-scatter.11.cloned.1.call-update) | async-done | bytes 524304 | tf_op jit(solution)/shard_map/reduce_scatter | solution.py:316
  1586.8 182.7 %reduce-scatter.13.cloned.1.call-done = f32[128,1024]{1,0:T(8,128)} async-done(((f32[2048,1024]{1,0:T(8,128)}), f32[128,1024]{1,0:T(8,128)}) %reduce-scatter.13.cloned.1.call-update) | async-done | bytes 524304 | tf_op jit(solution)/shard_map/reduce_scatter | solution.py:317
  1769.5 182.7 %reduce-scatter.15.cloned.1.call-done = f32[128,1024]{1,0:T(8,128)} async-done(((f32[2048,1024]{1,0:T(8,128)}), f32[128,1024]{1,0:T(8,128)}) %reduce-scatter.15.cloned.1.call-update) | async-done | bytes 524304 | tf_op jit(solution)/shard_map/reduce_scatter | solution.py:318
  1952.1 434.2 %reduce-scatter.19.cloned.1.call-done = f32[128,2560]{1,0:T(8,128)} async-done(((f32[2048,2560]{1,0:T(8,128)}), f32[128,2560]{1,0:T(8,128)}) %reduce-scatter.19.cloned.1.call-update) | async-done | bytes 1310736 | tf_op jit(solution)/shard_map/reduce_scatter | solution.py:234
  2386.3 436.4 %reduce-scatter.21.cloned.1.call-done = f32[128,2560]{1,0:T(8,128)} async-done(((f32[2048,2560]{1,0:T(8,128)}), f32[128,2560]{1,0:T(8,128)}) %reduce-scatter.21.cloned.1.call-update) | async-done | bytes 1310736 | tf_op jit(solution)/shard_map/reduce_scatter | solution.py:235
  2822.7 436.2 %reduce-scatter.23.cloned.1.call-done = f32[128,2560]{1,0:T(8,128)} async-done(((f32[2048,2560]{1,0:T(8,128)}), f32[128,2560]{1,0:T(8,128)}) %reduce-scatter.23.cloned.1.call-update) | async-done | bytes 1310736 | tf_op jit(solution)/shard_map/reduce_scatter | solution.py:236
  (327 shorter events, 291.5 us)
Async XLA Ops:
  7.2 82.2 %copy-start.1 = (bf16[1,192,2048]{2,1,0:T(8,128)(2,1)S(1)}, bf16[1,192,2048]{2,1,0:T(8,128)(2,1)}, u32[]{:S(2)}) copy-start(bf16[1,192,2048]{2,1,0:T(8,128)(2,1)} %param.18) | copy-start | bytes 2359300
  7.2 82.2 %all-gather.12.cloned.1.call-start = ((), (), s32[]{:S(2)}) async-start(), calls=%async_computation.8 | async-start | bytes 4456448 | tf_op jit(solution)/shard_map/all_gather | solution.py:93
  7.9 158.7 %all-gather.18.cloned.1.call-start = ((), (), s32[]{:S(2)}) async-start(), calls=%async_computation.11 | async-start | bytes 4456448 | tf_op jit(solution)/shard_map/all_gather | solution.py:94
  8.7 235.2 %all-gather.16.cloned.1.call-start = ((), (), s32[]{:S(2)}) async-start(), calls=%async_computation.10 | async-start | bytes 4456448 | tf_op jit(solution)/shard_map/all_gather | solution.py:92
  9.4 272.2 %all-gather.14.cloned.1.call-start = ((), (), s32[]{:S(2)}) async-start(), calls=%async_computation.9 | async-start | bytes 1966080 | tf_op jit(solution)/shard_map/all_gather | solution.py:122
  51.9 192.0 %copy-start.20 = (f32[16,1,128]{2,1,0:T(1,128)}, f32[16,1,128]{2,1,0:T(1,128)S(1)}, u32[]{:S(2)}) copy-start(f32[16,1,128]{2,1,0:T(1,128)S(1)} %convert_element_type.401) | copy-start | bytes 24580
  53.3 40.1 %copy-start.42 = (f32[192]{0:T(256)}, f32[192]{0:T(256)S(1)}, u32[]{:S(2)}) copy-start(f32[192]{0:T(256)S(1)} %fusion.81) | copy-start | bytes 2308
  53.3 190.6 %copy-start.30 = (f32[192]{0:T(256)}, f32[192]{0:T(256)S(1)}, u32[]{:S(2)}) copy-start(f32[192]{0:T(256)S(1)} %fusion.112) | copy-start | bytes 2308
  93.4 78.0 %copy-start.32 = (s32[1,2]{1,0:T(1,128)S(1)}, s32[1,2]{1,0:T(1,128)}, u32[]{:S(2)}) copy-start(s32[1,2]{1,0:T(1,128)} %param.20) | copy-start | bytes 28
  93.4 78.6 %copy-start.44 = (bf16[16,32]{1,0:T(8,128)(2,1)S(1)}, bf16[16,32]{1,0:T(8,128)(2,1)}, u32[]{:S(2)}) copy-start(bf16[16,32]{1,0:T(8,128)(2,1)} %param.30) | copy-start | bytes 3076
  93.4 226.2 %all-gather.20.cloned.1.call-start = ((), (), s32[]{:S(2)}) async-start(), calls=%async_computation.12 | async-start | bytes 1966080 | tf_op jit(solution)/shard_map/all_gather | solution.py:123
  170.6 266.7 %all-gather.22.cloned.1.call-start = ((), (), s32[]{:S(2)}) async-start(), calls=%async_computation.13 | async-start | bytes 4456448 | tf_op jit(solution)/shard_map/all_gather | solution.py:95
  171.1 313.0 %all-reduce.12.cloned.1.call-start = ((), (), s32[]{:S(2)}) async-start(), calls=%async_computation.14 | async-start | bytes 1572864 | tf_op jit(solution)/shard_map/psum | solution.py:178
  435.9 7.0 copy-start.40
  442.9 41.3 %copy-start.2 = (bf16[1,192,2048]{2,1,0:T(8,128)(2,1)S(1)}, bf16[1,192,2048]{2,1,0:T(8,128)(2,1)}, u32[]{:S(2)}) copy-start(bf16[1,192,2048]{2,1,0:T(8,128)(2,1)} %param.18) | copy-start | bytes 2359300
  442.9 154.3 %all-gather.24.cloned.1.call-start = ((), (), s32[]{:S(2)}) async-start(), calls=%async_computation.15 | async-start | bytes 11141120 | tf_op jit(solution)/shard_map/all_gather | solution.py:96
  443.6 287.0 %all-gather.26.cloned.1.call-start = ((), (), s32[]{:S(2)}) async-start(), calls=%async_computation.16 | async-start | bytes 11141120 | tf_op jit(solution)/shard_map/all_gather | solution.py:97
  444.4 419.7 %all-gather.28.cloned.1.call-start = ((), (), s32[]{:S(2)}) async-start(), calls=%async_computation.17 | async-start | bytes 11141120 | tf_op jit(solution)/shard_map/all_gather | solution.py:98
  445.0 459.4 %all-reduce.14.cloned.1.call-start = ((), (), s32[]{:S(2)}) async-start(), calls=%async_computation.18 | async-start | bytes 1572864 | tf_op jit(solution)/shard_map/psum | solution.py:227
  483.5 423.4 %copy-start.27 = (f32[16,1,128]{2,1,0:T(1,128)}, f32[16,1,128]{2,1,0:T(1,128)S(1)}, u32[]{:S(2)}) copy-start(f32[16,1,128]{2,1,0:T(1,128)S(1)} %convert_element_type.402) | copy-start | bytes 24580
  484.1 422.7 %copy-start.33 = (f32[192]{0:T(256)}, f32[192]{0:T(256)S(1)}, u32[]{:S(2)}) copy-start(f32[192]{0:T(256)S(1)} %compare_convert_fusion.8) | copy-start | bytes 2308
  485.8 421.1 %copy-start.35 = (f32[192]{0:T(256)}, f32[192]{0:T(256)S(1)}, u32[]{:S(2)}) copy-start(f32[192]{0:T(256)S(1)} %fusion.113) | copy-start | bytes 2308
  486.1 244.6 %copy-start.13 = (bf16[192,2048]{1,0:T(8,128)(2,1)}, bf16[192,2048]{1,0:T(8,128)(2,1)S(1)}, u32[]{:S(2)}) copy-start(bf16[192,2048]{1,0:T(8,128)(2,1)S(1)} %multiply_convert_fusion.2) | copy-start | bytes 2359300
  604.7 259.4 %copy-start.9 = (bf16[1,192,2048]{2,1,0:T(8,128)(2,1)S(1)}, bf16[1,192,2048]{2,1,0:T(8,128)(2,1)}, u32[]{:S(2)}) copy-start(bf16[1,192,2048]{2,1,0:T(8,128)(2,1)} %param.19) | copy-start | bytes 2359300
  874.0 8.3 copy-start.25
  874.0 8.3 copy-start.24
  874.0 8.3 copy-start.46
  886.8 300.5 %reduce-scatter.9.cloned.1.call-start = ((), (), s32[]{:S(2)}) async-start(), calls=%async_computation.19 | async-start | bytes 3932160 | tf_op jit(solution)/shard_map/reduce_scatter | solution.py:296
  888.1 18.8 copy-start.26
  906.9 4.6 copy-start.38
  917.6 25.3 copy-start
  987.8 25.3 copy-start
  1058.3 25.3 copy-start
  1125.7 175.4 %all-reduce.16.cloned.1.call-start = ((), (), s32[]{:S(2)}) async-start(), calls=%async_computation.27 | async-start | bytes 3145728 | tf_op jit(solution)/shard_map/psum | solution.py:185
  1126.9 8.5 copy-start.6
  1126.9 9.4 copy-start.17
  1193.8 210.3 %reduce-scatter.17.cloned.1.call-start = ((), (), s32[]{:S(2)}) async-start(), calls=%async_computation.23 | async-start | bytes 8912896 | tf_op jit(solution)/shard_map/reduce_scatter | solution.py:319
  1201.7 385.2 %reduce-scatter.11.cloned.1.call-start = ((), (), s32[]{:S(2)}) async-start(), calls=%async_computation.20 | async-start | bytes 8912896 | tf_op jit(solution)/shard_map/reduce_scatter | solution.py:316
  1208.2 561.3 %reduce-scatter.13.cloned.1.call-start = ((), (), s32[]{:S(2)}) async-start(), calls=%async_computation.21 | async-start | bytes 8912896 | tf_op jit(solution)/shard_map/reduce_scatter | solution.py:317
  1213.9 738.2 %reduce-scatter.15.cloned.1.call-start = ((), (), s32[]{:S(2)}) async-start(), calls=%async_computation.22 | async-start | bytes 8912896 | tf_op jit(solution)/shard_map/reduce_scatter | solution.py:318
  1219.8 1166.5 %reduce-scatter.19.cloned.1.call-start = ((), (), s32[]{:S(2)}) async-start(), calls=%async_computation.24 | async-start | bytes 22282240 | tf_op jit(solution)/shard_map/reduce_scatter | solution.py:234
  1231.4 1591.3 %reduce-scatter.21.cloned.1.call-start = ((), (), s32[]{:S(2)}) async-start(), calls=%async_computation.25 | async-start | bytes 22282240 | tf_op jit(solution)/shard_map/reduce_scatter | solution.py:235
  1242.9 2016.0 %reduce-scatter.23.cloned.1.call-start = ((), (), s32[]{:S(2)}) async-start(), calls=%async_computation.26 | async-start | bytes 22282240 | tf_op jit(solution)/shard_map/reduce_scatter | solution.py:236
  1252.9 46.1 %copy-start.47 = (f32[16]{0:T(128)S(1)}, f32[16]{0:T(128)}, u32[]{:S(2)}) copy-start(f32[16]{0:T(128)} %param.31) | copy-start | bytes 196
  1253.0 46.2 %copy-start.22 = (bf16[128,1024]{1,0:T(8,128)(2,1)S(1)}, bf16[128,1024]{1,0:T(8,128)(2,1)}, u32[]{:S(2)}) copy-start(bf16[128,1024]{1,0:T(8,128)(2,1)} %param.22) | copy-start | bytes 786436
  1253.0 50.0 %copy-start.37 = (f32[2048]{0:T(1024)S(1)}, f32[2048]{0:T(1024)}, u32[]{:S(2)}) copy-start(f32[2048]{0:T(1024)} %get-tuple-element.769) | copy-start | bytes 24580
  1253.0 129.0 %copy-start.43 = (f32[192]{0:T(256)S(1)}, f32[192]{0:T(256)}, u32[]{:S(2)}) copy-start(f32[192]{0:T(256)} %copy-done.42) | copy-start | bytes 2308
  1299.0 86.8 %copy-start.49 = (f32[16]{0:T(128)}, f32[16]{0:T(128)S(1)}, u32[]{:S(2)}) copy-start(f32[16]{0:T(128)S(1)} %pmax.7) | copy-start | bytes 196
  (28 other events, 66.6 us)
Sparse Core Ops, SparseCore 0:
  10.8 78.5 all-gather.11
  92.2 74.3 all-gather.17
  169.3 74.4 all-gather.15
  245.9 35.6 all-gather.13
  283.6 35.9 all-gather.19
  322.2 74.7 all-gather.21
  443.0 17.5 all-reduce.11
  463.7 133.3 all-gather.23
  600.3 130.3 all-gather.25
  733.6 130.3 all-gather.27
  886.9 17.3 all-reduce.13
  1125.8 61.4 reduce-scatter.8
  1193.9 20.4 all-reduce.15
  1217.3 186.8 reduce-scatter.16
  1407.0 179.8 reduce-scatter.10
  1589.6 179.8 reduce-scatter.12
  1772.3 179.7 reduce-scatter.14
  1955.0 431.2 reduce-scatter.18
  2389.3 433.3 reduce-scatter.20
  2825.6 433.3 reduce-scatter.22
where the time goes:
time: 3270 us
  waiting for transfers between devices  2560 us (78%)
  local copies, waits for them, and re-layouts  261 us (8%)
  blocking collectives  203 us (6%)
  matrix products  186 us (6%)
  other arithmetic  38 us (1%)
    reduce_scatter x1, waiting for transfers between devices, shards(): lax.psum_scatter(grad_w_up, ('fsdp', 'ctx'), scatter_dimension=0, tiled=T...  436 us
    reduce_scatter x1, waiting for transfers between devices, shards(): lax.psum_scatter(grad_w_down, ('fsdp', 'ctx'), scatter_dimension=0, tiled...  436 us
    reduce_scatter x1, waiting for transfers between devices, shards(): lax.psum_scatter(grad_w_gate, ('fsdp', 'ctx'), scatter_dimension=0, tiled...  434 us
    reduce_scatter x1, waiting for transfers between devices, shards(): lax.psum_scatter(grad_w_key, ('fsdp', 'ctx'), scatter_dimension=0, tiled=...  183 us
    reduce_scatter x1, waiting for transfers between devices, shards(): lax.psum_scatter(grad_w_query, ('fsdp', 'ctx'), scatter_dimension=0, tile...  183 us
    reduce_scatter x1, waiting for transfers between devices, shards(): lax.psum_scatter(grad_w_value, ('fsdp', 'ctx'), scatter_dimension=0, tile...  183 us
    all_gather x1, waiting for transfers between devices, shards(): lax.all_gather(w_up, ('fsdp', 'ctx'), axis=0, tiled=True)  126 us
    all_gather x1, waiting for transfers between devices, shards(): lax.all_gather(w_down, ('fsdp', 'ctx'), axis=0, tiled=True)  126 us
  transfers between devices with their start and end apart: 20, of which 17 were waited for; matrix products, arithmetic and copies ran while one was open for 7% of the time, Pallas kernels for 0%

commit v1 on v0

v1 whole, which is shorter than its diff:
```python
import functools

import jax
import jax.numpy as jnp
from jax import lax
from jax.experimental import pallas as pl
from jax.experimental.pallas import tpu as pltpu
from jax.sharding import PartitionSpec as P

DK = 64
BUCKETS = 32
THRESHOLDS = (12, 16, 23, 32, 46, 64, 91)
NEGATIVE = -1e30
EPSILON = 1e-06
QUERY_BLOCK = 256
NEAR = 512
VMEM_LIMIT = 48 * 1024 * 1024
LOW = jnp.bfloat16
WIDE = jnp.float32


def bucket_of(offset):
    distance = jnp.abs(offset)
    beyond = 8 + sum(((distance >= threshold).astype(jnp.int32) for threshold in THRESHOLDS))
    within = jnp.where(distance < 8, distance, beyond)
    return within + jnp.where(offset > 0, BUCKETS // 2, 0)


def contract(left, right, left_dim, right_dim):
    return lax.dot_general(
        left, right, (((left_dim,), (right_dim,)), ((), ())), preferred_element_type=WIDE
    )


def places(meta_ref, count, half):
    here, core = meta_ref[0], meta_ref[1]
    for side in range(2):
        for back in range(count):
            block = lax.rem(here - back + count, count) * 2 + (core if side == 0 else 1 - core)
            yield (side * count + back) * half, pl.multiple_of(block * half, half)


def segments_down(meta_ref, shape):
    place = lax.broadcasted_iota(jnp.int32, shape, 0)
    return (place >= meta_ref[2]).astype(jnp.int32) + (place >= meta_ref[3]).astype(jnp.int32)


def segments_across(meta_ref, first, width):
    place = first + lax.broadcasted_iota(jnp.int32, (1, width), 1)
    return (place >= meta_ref[2]).astype(jnp.int32) + (place >= meta_ref[3]).astype(jnp.int32)


def forward_kernel(
    meta_ref, rows_ref, bias_ref, mixed_ref, log_ref, peak_ref, home_ref, flip_ref, part_ref, *, count, half, heads
):
    slots, width, block = 2 * count * half, heads * DK, QUERY_BLOCK
    for source, target in places(meta_ref, count, half):
        home_ref[pl.ds(target, half), :] = rows_ref[source : source + half, :]
    part_ref[...] = segments_down(meta_ref, (slots, block))
    log_ref[...] = jnp.zeros_like(log_ref)
    peak_ref[...] = jnp.full(peak_ref.shape, NEGATIVE, WIDE)
    for head in range(heads):
        at = head * DK
        keys = home_ref[:, width + at : width + at + DK]
        queries_flip = home_ref[:, at : at + DK].T
        values_flip = home_ref[:, 2 * width + at : 2 * width + at + DK].T
        peak = jnp.full((1, block), NEGATIVE, WIDE)
        for step in range(slots // block):
            first = step * block
            across = segments_across(meta_ref, first, block)
            logits = contract(keys, queries_flip[:, first : first + block], 1, 0)
            logits = jnp.where(part_ref[...] == across, logits, NEGATIVE)
            tops = jnp.max(logits, axis=0, keepdims=True)
            peak = jnp.maximum(peak, jnp.where(across < 2, tops, NEGATIVE))
            start = slots - block - first
            scores = logits + bias_ref[head, start : start + slots, :]
            highest = jnp.max(scores, axis=0, keepdims=True)
            weights = jnp.exp(scores - highest)
            total = jnp.sum(weights, axis=0, keepdims=True)
            mixed = contract(values_flip, weights.astype(LOW), 1, 0)
            flip_ref[at : at + DK, first : first + block] = mixed / total
            log_ref[head : head + 1, first : first + block] = highest + jnp.log(total)
        peak_ref[head : head + 1, :] = jnp.broadcast_to(
            jnp.max(peak, axis=1, keepdims=True), (1, peak_ref.shape[1])
        )
    home_ref[:, :width] = flip_ref[...].T.astype(LOW)
    for source, target in places(meta_ref, count, half):
        mixed_ref[source : source + half, :] = home_ref[pl.ds(target, half), :width]


def backward_kernel(
    meta_ref,
    rows_ref,
    grad_ref,
    log_ref,
    bias_ref,
    out_ref,
    table_ref,
    home_ref,
    grad_home_ref,
    flip_ref,
    part_ref,
    sums_ref,
    down_ref,
    *,
    count,
    half,
    heads,
):
    slots, width, block = 2 * count * half, heads * DK, QUERY_BLOCK
    for source, target in places(meta_ref, count, half):
        home_ref[pl.ds(target, half), :] = rows_ref[source : source + half, :]
        grad_home_ref[pl.ds(target, half), :] = grad_ref[source : source + half, :]
    part_ref[...] = segments_down(meta_ref, (slots, block))
    table_ref[...] = jnp.zeros_like(table_ref)
    lane = lax.broadcasted_iota(jnp.int32, (1, table_ref.shape[1]), 1)
    near = slots - block - (NEAR - block) // 2
    buckets = bucket_of(
        lax.broadcasted_iota(jnp.int32, (NEAR, block), 0)
        + near
        - (slots - block)
        - lax.broadcasted_iota(jnp.int32, (NEAR, block), 1)
    )
    for head in range(heads):
        at = head * DK
        queries = home_ref[:, at : at + DK]
        keys = home_ref[:, width + at : width + at + DK]
        values = home_ref[:, 2 * width + at : 2 * width + at + DK]
        grads = grad_home_ref[:, at : at + DK]
        queries_flip, keys_flip, grads_flip = queries.T, keys.T, grads.T
        sums_ref[...] = jnp.zeros_like(sums_ref)
        for step in range(slots // block):
            first = step * block
            across = segments_across(meta_ref, first, block)
            start = slots - block - first
            logits = contract(keys, queries_flip[:, first : first + block], 1, 0)
            scores = logits + bias_ref[head, start : start + slots, :]
            scores = scores - log_ref[head : head + 1, first : first + block]
            chance = jnp.exp(jnp.where(part_ref[...] == across, scores, NEGATIVE))
            grad_chance = contract(values, grads_flip[:, first : first + block], 1, 0)
            delta = jnp.sum(chance * grad_chance, axis=0, keepdims=True)
            grad_scores = chance * (grad_chance - delta)
            sums_ref[start : start + slots, :] += grad_scores
            rounded = grad_scores.astype(LOW)
            grad_keys = contract(rounded, queries[first : first + block, :], 1, 0)
            grad_values = contract(chance.astype(LOW), grads[first : first + block, :], 1, 0)
            if step == 0:
                down_ref[:, :DK] = grad_keys
                down_ref[:, DK:] = grad_values
            else:
                down_ref[:, :DK] += grad_keys
                down_ref[:, DK:] += grad_values
            flip_ref[at : at + DK, first : first + block] = contract(keys_flip, rounded, 1, 0)
        home_ref[:, width + at : width + at + DK] = down_ref[:, :DK].astype(LOW)
        home_ref[:, 2 * width + at : 2 * width + at + DK] = down_ref[:, DK:].astype(LOW)
        close = sums_ref[near : near + NEAR, :]
        row = jnp.where(lane == BUCKETS // 2 - 1, jnp.sum(sums_ref[:near, :]), 0.0)
        row = row + jnp.where(lane == BUCKETS - 1, jnp.sum(sums_ref[near + NEAR :, :]), 0.0)
        for bucket in range(BUCKETS):
            row = row + jnp.where(lane == bucket, jnp.sum(jnp.where(buckets == bucket, close, 0.0)), 0.0)
        table_ref[head : head + 1, :] = row
    home_ref[:, :width] = flip_ref[...].T.astype(LOW)
    for source, target in places(meta_ref, count, half):
        out_ref[source : source + half, :] = home_ref[pl.ds(target, half), :]


def bias_master(table, slots):
    heads, block = table.shape[0], QUERY_BLOCK
    near = slots - block - (NEAR - block) // 2
    offset = (
        lax.broadcasted_iota(jnp.int32, (NEAR, block), 0)
        + near
        - (slots - block)
        - lax.broadcasted_iota(jnp.int32, (NEAR, block), 1)
    )
    buckets = bucket_of(offset)[None]
    close = jnp.zeros((heads, NEAR, block), WIDE)
    for bucket in range(BUCKETS):
        close = jnp.where(buckets == bucket, table[:, bucket][:, None, None], close)
    after = 2 * slots - block - near - NEAR
    below = jnp.broadcast_to(table[:, BUCKETS // 2 - 1][:, None, None], (heads, near, block))
    above = jnp.broadcast_to(table[:, BUCKETS - 1][:, None, None], (heads, after, block))
    return jnp.concatenate([below, close, above], axis=1)


def whole(memory=pltpu.VMEM):
    return pl.BlockSpec(memory_space=memory)


def attend_forward(meta, rows_in, bias, count, half, heads):
    slots, width, block = 2 * count * half, heads * DK, QUERY_BLOCK
    return pl.pallas_call(
        functools.partial(forward_kernel, count=count, half=half, heads=heads),
        out_shape=(
            jax.ShapeDtypeStruct((slots, width), LOW),
            jax.ShapeDtypeStruct((8, slots), WIDE),
            jax.ShapeDtypeStruct((8, 128), WIDE),
        ),
        in_specs=[whole(pltpu.SMEM), whole(), whole()],
        out_specs=(whole(), whole(), whole()),
        scratch_shapes=[
            pltpu.VMEM((slots, 3 * width), LOW),
            pltpu.VMEM((width, slots), WIDE),
            pltpu.VMEM((slots, block), jnp.int32),
        ],
        compiler_params=pltpu.CompilerParams(vmem_limit_bytes=VMEM_LIMIT),
        cost_estimate=pl.CostEstimate(
            flops=4 * heads * slots * slots * DK,
            bytes_accessed=8 * slots * width + 8 * heads * slots * block,
            transcendentals=heads * slots * slots,
        ),
        name="attend_forward",
    )(meta, rows_in, bias)


def attend_backward(meta, rows_in, grad_in, log_total, bias, count, half, heads):
    slots, width, block = 2 * count * half, heads * DK, QUERY_BLOCK
    return pl.pallas_call(
        functools.partial(backward_kernel, count=count, half=half, heads=heads),
        out_shape=(
            jax.ShapeDtypeStruct((slots, 3 * width), LOW),
            jax.ShapeDtypeStruct((8, 128), WIDE),
        ),
        in_specs=[whole(pltpu.SMEM), whole(), whole(), whole(), whole()],
        out_specs=(whole(), whole()),
        scratch_shapes=[
            pltpu.VMEM((slots, 3 * width), LOW),
            pltpu.VMEM((slots, width), LOW),
            pltpu.VMEM((width, slots), WIDE),
            pltpu.VMEM((slots, block), jnp.int32),
            pltpu.VMEM((2 * slots - block, block), WIDE),
            pltpu.VMEM((slots, 2 * DK), WIDE),
        ],
        compiler_params=pltpu.CompilerParams(vmem_limit_bytes=VMEM_LIMIT),
        cost_estimate=pl.CostEstimate(
            flops=10 * heads * slots * slots * DK,
            bytes_accessed=16 * slots * width + 8 * heads * slots * block,
            transcendentals=heads * slots * slots,
        ),
        name="attend_backward",
    )(meta, rows_in, grad_in, log_total, bias)


def shards(
    tokens,
    out_grad,
    lengths,
    w_query,
    w_key,
    w_value,
    w_out,
    w_gate,
    w_up,
    w_down,
    gain_attn,
    gain_ffn,
    bias_table,
    clip_limit,
):
    groups, count, cores = (lax.axis_size(name) for name in ("fsdp", "ctx", "tp"))
    assert cores == 2
    group, here, core = (lax.axis_index(name) for name in ("fsdp", "ctx", "tp"))
    half = tokens.shape[1] // cores
    slots = tokens.shape[1] * count
    heads = bias_table.shape[0] // count
    head_width = heads * DK
    unit_width = w_gate.shape[1] // count
    weight_rows = w_query.shape[0]

    def around(value, steps):
        return lax.ppermute(value, "ctx", [(i, (i + steps) % count) for i in range(count)])

    def flip(value, mask):
        return lax.ppermute(value, "fsdp", [(i, i ^ mask) for i in range(groups)])

    def swap(value):
        return lax.ppermute(value, "tp", [(0, 1), (1, 0)])

    def ordered(pieces, which, axis):
        total = len(pieces)
        if total > 4:
            stacked = jnp.stack(pieces)
            return jnp.concatenate(
                [lax.dynamic_index_in_dim(stacked, which(n), 0, False) for n in range(total)], axis=axis
            )
        return jnp.concatenate([lax.select_n(which(n), *pieces) for n in range(total)], axis=axis)

    def place_of(n):
        return lax.rem(here - n + count, count)

    def spread(parts, width):
        def block(steps):
            start = lax.rem(here + steps, count) * width
            return jnp.concatenate([lax.dynamic_slice_in_dim(p, start, width, 1) for p in parts], axis=1)

        pieces = [block(0)] + [around(block(k), k) for k in range(1, count)]
        return ordered(pieces, place_of, 0)

    def collect(block, width):
        def rows_of(steps):
            start = lax.rem(here + steps, count) * weight_rows
            return lax.dynamic_slice_in_dim(block, start, weight_rows, 0)

        pieces = [rows_of(0)] + [around(rows_of(k), k) for k in range(1, count)]
        return [
            ordered([p[:, at : at + width] for p in pieces], place_of, 1).astype(WIDE)
            for at in range(0, block.shape[1], width)
        ]

    def gather_weights(block):
        if groups != 4:
            return lax.all_gather(block, "fsdp", axis=0, tiled=True)
        middle = block.shape[0] // 2
        first, second = flip(block, 1), flip(block, 2)
        corner = jnp.concatenate([flip(first[:middle], 2), flip(second[middle:], 1)], axis=0)
        return ordered([block, first, second, corner], lambda n: group ^ n, 0)

    def gather_rows(piece):
        mine = jnp.concatenate([piece] + [around(piece, k) for k in range(1, count)], axis=0)
        return jnp.concatenate([mine, swap(mine)], axis=0)

    def reduce_rows(product_of):
        own = count * half
        theirs = swap(product_of(own, 2 * own).astype(LOW))
        total = product_of(0, own) + theirs.astype(WIDE)
        low = total.astype(LOW)
        result = total[:half]
        for k in range(1, count):
            result = result + around(low[k * half : (k + 1) * half], -k).astype(WIDE)
        return result

    def both_cores(piece):
        other = swap(piece)
        return jnp.where(
            core == 0, jnp.concatenate([piece, other], axis=0), jnp.concatenate([other, piece], axis=0)
        )

    def own_rows(value):
        return lax.dynamic_slice_in_dim(value[0], core * half, half, 0)

    def inverse_norm(value):
        return lax.rsqrt(jnp.mean(value * value, axis=-1, keepdims=True) + EPSILON)

    def norm_back(value, inverse, grad):
        along = jnp.mean(grad * value, axis=-1, keepdims=True)
        return inverse * grad - value * (inverse * inverse * inverse * along)

    ends = (lengths[0, 0], lengths[0, 0] + lengths[0, 1])
    meta = jnp.stack([here, core, ends[0], ends[1]]).astype(jnp.int32)
    attn_gain = gain_attn.astype(WIDE)[:, None]
    ffn_gain = gain_ffn.astype(WIDE)[:, None]

    def scaled(weight, gain):
        return (weight.astype(WIDE) * gain).astype(LOW)

    query_key_value = [scaled(w, attn_gain) for w in (w_query, w_key, w_value)]
    gate_up = [scaled(w, ffn_gain) for w in (w_gate, w_up)]

    attn_columns = gather_weights(spread(query_key_value, head_width))
    inputs = own_rows(tokens).astype(WIDE)
    inverse_one = inverse_norm(inputs)
    normed = gather_rows((inputs * inverse_one).astype(LOW))
    out_columns = gather_weights(spread([w_out], head_width))
    gate_up_columns = lax.all_gather(spread(gate_up, unit_width), "fsdp", axis=0, tiled=True)
    down_columns = lax.all_gather(spread([w_down], unit_width), "fsdp", axis=0, tiled=True)

    row_place = (here * cores + core) * half + jnp.arange(half, dtype=jnp.int32)
    row_valid = (row_place < ends[1])[:, None]
    grad_out = jnp.where(row_valid, own_rows(out_grad).astype(WIDE), 0.0)
    grad_rows = gather_rows(grad_out.astype(LOW))

    my_table = lax.dynamic_slice_in_dim(bias_table, here * heads, heads, 0).astype(WIDE)
    bias = bias_master(my_table, slots)

    projected = contract(normed, attn_columns, 1, 0).astype(LOW)
    mixed, log_total, peaks = attend_forward(meta, projected, bias, count, half, heads)
    hidden = inputs + reduce_rows(lambda a, b: contract(mixed[a:b], out_columns, 1, 1))
    inverse_two = inverse_norm(hidden)
    normed_ffn = gather_rows((hidden * inverse_two).astype(LOW))
    both_pre = contract(normed_ffn, gate_up_columns, 1, 0)
    gate_pre, upward = both_pre[:, :unit_width], both_pre[:, unit_width:]
    activated, gelu_back = jax.vjp(functools.partial(jax.nn.gelu, approximate=True), gate_pre)
    product = (activated * upward).astype(LOW)
    ffn_out = reduce_rows(lambda a, b: contract(product[a:b], down_columns, 1, 1))
    mixed_out = both_cores((hidden + ffn_out).astype(LOW))[None]

    grad_product = contract(grad_rows, down_columns, 1, 0)
    grad_gate = gelu_back(grad_product * upward)[0].astype(LOW)
    grad_upward = (grad_product * activated).astype(LOW)
    grad_both = jnp.concatenate([grad_gate, grad_upward], axis=1)
    grad_normed_ffn = reduce_rows(lambda a, b: contract(grad_both[a:b], gate_up_columns, 1, 1))
    grad_hidden = grad_out + norm_back(hidden, inverse_two, grad_normed_ffn)
    branch_rows = gather_rows(grad_hidden.astype(LOW))

    def sum_groups(left, right):
        terms = contract(left, right, 0, 0).astype(LOW)
        return lax.psum_scatter(terms, "fsdp", scatter_dimension=0, tiled=True)

    (grad_down,) = collect(sum_groups(grad_rows, product), unit_width)
    grad_gate_w, grad_up_w = collect(sum_groups(normed_ffn, grad_both), unit_width)

    grad_mixed = contract(branch_rows, out_columns, 1, 0).astype(LOW)
    grad_projected, table_terms = attend_backward(
        meta, projected, grad_mixed, log_total, bias, count, half, heads
    )
    (grad_out_w,) = collect(sum_groups(branch_rows, mixed), head_width)
    grad_normed = reduce_rows(lambda a, b: contract(grad_projected[a:b], attn_columns, 1, 1))
    grad_tokens = both_cores((grad_hidden + norm_back(inputs, inverse_one, grad_normed)).astype(LOW))[None]
    grad_query_w, grad_key_w, grad_value_w = collect(sum_groups(normed, grad_projected), head_width)

    def gain_terms(weights, grads):
        return sum(jnp.sum(w.astype(WIDE) * g, axis=1) for w, g in zip(weights, grads, strict=True))

    gain_grads = jnp.stack(
        [
            gain_terms((w_query, w_key, w_value), (grad_query_w, grad_key_w, grad_value_w)),
            gain_terms((w_gate, w_up), (grad_gate_w, grad_up_w)),
        ]
    )
    gain_grads = gain_grads + swap(gain_grads)

    small = jnp.concatenate([table_terms[:heads, :BUCKETS], peaks[:heads, :1]], axis=1)
    blank = jnp.concatenate([jnp.zeros((1, BUCKETS), WIDE), jnp.full((1, 1), NEGATIVE, WIDE)], axis=1)
    is_sum = jnp.arange(BUCKETS + 1)[None, :] < BUCKETS
    small = jnp.where(
        (jnp.arange(count * heads) // heads == here)[:, None],
        jnp.tile(small, (count, 1)),
        blank,
    )

    def merge(first, second):
        return jnp.where(is_sum, first + second, jnp.maximum(first, second))

    mask = 1
    while mask < groups:
        small = merge(small, flip(small, mask))
        mask *= 2
    mask = 1
    while mask < count:
        small = merge(small, lax.ppermute(small, "ctx", [(i, i ^ mask) for i in range(count)]))
        mask *= 2
    grad_table, head_peaks = small[:, :BUCKETS], small[:, BUCKETS]
    factor = jnp.sqrt(clip_limit / jnp.maximum(head_peaks, clip_limit))
    factor_row = jnp.repeat(factor, DK)[None, :]

    def clipped(weight):
        return (weight.astype(WIDE) * factor_row).astype(LOW)

    return (
        mixed_out,
        grad_tokens,
        grad_query_w * attn_gain,
        grad_key_w * attn_gain,
        grad_value_w * attn_gain,
        grad_out_w,
        grad_gate_w * ffn_gain,
        grad_up_w * ffn_gain,
        grad_down,
        gain_grads[0],
        gain_grads[1],
        grad_table,
        head_peaks,
        clipped(w_query),
        clipped(w_key),
    )


def solution(mesh):
    rows, weight, gain = P("fsdp", "ctx", None), P(("fsdp", "ctx"), "tp"), P(("fsdp", "ctx"))
    return jax.shard_map(
        shards,
        mesh=mesh,
        in_specs=(rows, rows, P("fsdp", None)) + (weight,) * 7 + (gain, gain, P("tp", None), P("tp")),
        out_specs=(rows, rows) + (weight,) * 7 + (gain, gain, P("tp", None), P("tp"), weight, weight),
        check_vma=False,
    )
```

time: 3270 us -> 662 us (0.20)
  waiting for transfers between devices: 2560 us -> 313 us
  local copies, waits for them, and re-layouts: 261 us -> 25 us
  blocking collectives: 203 us -> 0 us
  starting transfers between devices: 1.27 us -> 141 us
  matrix products: 186 us -> 69.2 us
    reduce_scatter x8 -> x4, waiting for transfers between devices: 1920 us -> 1.18 us  [sum_groups(): return lax.psum_scatter(terms, 'fsdp', scatter_dimension=0, tiled=True)]
    all_gather x9 -> x2, waiting for transfers between devices: 612 us -> 0.01 us  [the longest x1 0.01 us: shards(): lax.all_gather(spread(gate_up, unit_width), 'fsdp', axis=0, tiled=True)]
    ppermute x0 -> x71, waiting for transfers between devices: none -> 312 us  [the longest x48 252 us: around(): lax.ppermute(value, 'ctx', [(i, (i + steps) % count) for i in range(count)])]
    ppermute x0 -> x71, starting transfers between devices: none -> 141 us  [the longest x48 120 us: around(): lax.ppermute(value, 'ctx', [(i, (i + steps) % count) for i in range(count)])]
    dot_general x51 -> x16, matrix products: 186 us -> 69.2 us  [contract(): lax.dot_general(left, right, (((left_dim,), (right_dim,)), ((), ())), pre...]
    reshape x13 -> x0, local copies, waits for them, and re-layouts: 93.7 us -> none  [the longest x9 73.3 us: expand_bias(): repeated = repeated.reshape(table_in.shape[0], query_count, diagonals)]
    all_gather x2 -> x0, blocking collectives: 80.8 us -> none  [the longest x1 42.4 us: shards(): lax.all_gather(gain_attn, ('fsdp', 'ctx'), axis=0, tiled=True)]
    unnamed x1 -> x0, blocking collectives: 77.8 us -> none
  transfers between devices with their start and end apart: 20 -> 77, of which waited for: 17 -> 37; matrix products, arithmetic and copies ran while one was open for 7% -> 20% of each run, Pallas kernels for 0% -> 5%
where the time goes in v1:
time: 662 us; the launch traced here: 651 us
  waiting for transfers between devices  313 us (47%)
  starting transfers between devices  141 us (21%)
  matrix products  69.2 us (10%)
  other arithmetic  55.4 us (8%)
  Pallas kernels  29.5 us (4%)
  local copies, waits for them, and re-layouts  25 us (4%)
  between operations  17.4 us (3%)
    ppermute x48, waiting for transfers between devices, around(): lax.ppermute(value, 'ctx', [(i, (i + steps) % count) for i in range(count)])  252 us
    ppermute x48, starting transfers between devices, around(): lax.ppermute(value, 'ctx', [(i, (i + steps) % count) for i in range(count)])  120 us
    dot_general x16, matrix products, contract(): lax.dot_general(left, right, (((left_dim,), (right_dim,)), ((), ())), pre...  69.2 us
    ppermute x10, waiting for transfers between devices, flip(): return lax.ppermute(value, 'fsdp', [(i, i ^ mask) for i in range(groups)])  54.1 us
    pallas_call x1, Pallas kernels, attend_backward(): pl.pallas_call(functools.partial(backward_kernel, count=count, half=half,...  20.2 us
    ppermute x10, starting transfers between devices, flip(): return lax.ppermute(value, 'fsdp', [(i, i ^ mask) for i in range(groups)])  13.6 us
  transfers between devices with their start and end apart: 77, of which 37 were waited for; matrix products, arithmetic and copies ran while one was open for 20% of the time, Pallas kernels for 5%

profile of v1, /device:TPU:0, one launch (start us, length us, event | category | flops | bytes accessed | tf_op | source)
XLA Modules:
  0.0 651.1 jit_solution(2795719763081905828)
XLA Ops:
  10.4 5.0 collective-permute-start.2
  27.5 4.3 broadcast_compare_fusion.26
  39.1 8.0 %select_select_fusion = f32[4,512,256]{2,1,0:T(8,128)S(1)} fusion(f32[4]{0:T(128)S(1)} %get-tuple-element.26, f32[4]{0:T(128)S(1)} %get-tuple-element.27, f32[4]{0:T(128)S(1)} %copy-done.77, f32[4]{0:T(128)S(1)} %copy-done.78, f32[4]{0:T(128)S(1)} %copy-done.79, f32[4]{0:T(128)S(1)} %copy-done.80, f32[4]{0:T(128)S(1)} %copy-done.81, f32[4]{0:T(128)S(1)} %copy-done.82, ...), kind=kLoop, calls=%fused_computation.21 | loop fusion | flops 16777216 | bytes 6291968 | tf_op jit(solution)/shard_map/jit(_where)/select_n | solution.py:179
  50.1 13.4 %collective-permute-start.11 = (bf16[128,256]{1,0:T(8,128)(2,1)}, bf16[128,256]{1,0:T(8,128)(2,1)S(1)}, u32[]{:S(2)}, u32[]{:S(2)}) collective-permute-start(bf16[128,256]{1,0:T(8,128)(2,1)} %get-tuple-element.171), channel_id=1, source_target_pairs={{0,2},{2,4},{4,6},{6,0},{1,3},{3,5},{5,7},{7,1},{8,10},{10,12},{12... | collective-permute-start | bytes 196616 | tf_op jit(solution)/shard_map/ppermute | solution.py:271
  64.2 8.9 %collective-permute-start.13 = (bf16[128,256]{1,0:T(8,128)(2,1)}, bf16[128,256]{1,0:T(8,128)(2,1)S(1)}, u32[]{:S(2)}, u32[]{:S(2)}) collective-permute-start(bf16[128,256]{1,0:T(8,128)(2,1)} %get-tuple-element.172), channel_id=1, source_target_pairs={{0,6},{2,0},{4,2},{6,4},{1,7},{3,1},{5,3},{7,5},{8,14},{10,8},{12,... | collective-permute-start | bytes 196616 | tf_op jit(solution)/shard_map/ppermute | solution.py:271
  78.0 7.8 %collective-permute-done.12 = bf16[128,256]{1,0:T(8,128)(2,1)S(1)} collective-permute-done((bf16[128,256]{1,0:T(8,128)(2,1)S(1)}, bf16[128,256]{1,0:T(8,128)(2,1)S(1)}, u32[]{:S(2)}, u32[]{:S(2)}) %collective-permute-start.12) | collective-permute-done | bytes 65568 | tf_op jit(solution)/shard_map/ppermute | solution.py:271
  86.8 5.0 collective-permute-start
  91.8 8.3 %collective-permute-done.5 = bf16[128,768]{1,0:T(8,128)(2,1)S(1)} collective-permute-done((bf16[128,768]{1,0:T(8,128)(2,1)S(1)}, bf16[128,768]{1,0:T(8,128)(2,1)S(1)}, u32[]{:S(2)}, u32[]{:S(2)}) %collective-permute-start.5) | collective-permute-done | bytes 196640 | tf_op jit(solution)/shard_map/ppermute | solution.py:271
  103.4 5.5 collective-permute-done.15
  113.9 33.7 %collective-permute-done.16 = bf16[256,256]{1,0:T(8,128)(2,1)S(1)} collective-permute-done((bf16[256,256]{1,0:T(8,128)(2,1)S(1)}, bf16[256,256]{1,0:T(8,128)(2,1)S(1)}, u32[]{:S(2)}, u32[]{:S(2)}) %collective-permute-start.16) | collective-permute-done | bytes 131104 | tf_op jit(solution)/shard_map/ppermute | solution.py:274
  147.6 3.7 collective-permute-done.17
  155.0 7.7 %collective-permute-done.9 = bf16[256,768]{1,0:T(8,128)(2,1)S(1)} collective-permute-done((bf16[256,768]{1,0:T(8,128)(2,1)S(1)}, bf16[256,768]{1,0:T(8,128)(2,1)S(1)}, u32[]{:S(2)}, u32[]{:S(2)}) %collective-permute-start.9) | collective-permute-done | bytes 393248 | tf_op jit(solution)/shard_map/ppermute | solution.py:274
  170.1 9.3 %attend_forward.1 = (bf16[768,256]{1,0:T(8,128)(2,1)S(1)}, f32[8,768]{1,0:T(8,128)S(1)}, f32[8,128]{1,0:T(8,128)S(1)}) custom-call(s32[4]{0:T(128)S(1)} %pad_add_fusion.meta_ref, bf16[768,768]{1,0:T(8,128)(2,1)S(1)} %convolution_convert_fusion.8.rows_ref, f32[4,1280,256]{2,1,0:T(8,128)} %pad_maximum_fusion.bias_ref), custom_call_target="tpu_custom_call" | custom-call | flops 603979776 | bytes 7864320 | tf_op jit(solution)/shard_map/attend_forward/pallas_call | solution.py:192
  195.9 21.6 %collective-permute-done.29 = bf16[128,640]{1,0:T(8,128)(2,1)S(1)} collective-permute-done((bf16[128,640]{1,0:T(8,128)(2,1)S(1)}, bf16[128,640]{1,0:T(8,128)(2,1)S(1)}, u32[]{:S(2)}, u32[]{:S(2)}) %collective-permute-start.29) | collective-permute-done | bytes 163872 | tf_op jit(solution)/shard_map/ppermute | solution.py:271
  217.5 13.5 %collective-permute-start.30 = (bf16[128,640]{1,0:T(8,128)(2,1)S(1)}, bf16[128,640]{1,0:T(8,128)(2,1)S(1)}, u32[]{:S(2)}, u32[]{:S(2)}) collective-permute-start(bf16[128,640]{1,0:T(8,128)(2,1)S(1)} %get-tuple-element.151), channel_id=1, source_target_pairs={{0,4},{2,6},{4,0},{6,2},{1,5},{3,7},{5,1},{7,3},{8,12},{10,14},{12... | collective-permute-start | bytes 491528 | tf_op jit(solution)/shard_map/ppermute | solution.py:271
  232.4 6.2 collective-permute-done.30
  238.6 5.0 collective-permute-start.21
  243.7 3.9 collective-permute-start.20
  251.3 5.0 collective-permute-done.21
  256.3 15.9 %collective-permute-done.20 = bf16[96,2048]{1,0:T(8,128)(2,1)} collective-permute-done((bf16[96,2048]{1,0:T(8,128)(2,1)}, bf16[96,2048]{1,0:T(8,128)(2,1)}, u32[]{:S(2)}, u32[]{:S(2)}) %collective-permute-start.20) | collective-permute-done | bytes 393248 | tf_op jit(solution)/shard_map/ppermute | solution.py:271
  277.0 10.1 %collective-permute-done.24 = bf16[96,2048]{1,0:T(8,128)(2,1)S(1)} collective-permute-done((bf16[96,2048]{1,0:T(8,128)(2,1)S(1)}, bf16[96,2048]{1,0:T(8,128)(2,1)S(1)}, u32[]{:S(2)}, u32[]{:S(2)}) %collective-permute-start.24) | collective-permute-done | bytes 393248 | tf_op jit(solution)/shard_map/ppermute | solution.py:271
  287.1 21.8 %collective-permute-done.23 = bf16[96,2048]{1,0:T(8,128)(2,1)S(1)} collective-permute-done((bf16[96,2048]{1,0:T(8,128)(2,1)S(1)}, bf16[96,2048]{1,0:T(8,128)(2,1)S(1)}, u32[]{:S(2)}, u32[]{:S(2)}) %collective-permute-start.23) | collective-permute-done | bytes 393248 | tf_op jit(solution)/shard_map/ppermute | solution.py:271
  315.4 9.6 %fusion.84 = f32[768,1280]{1,0:T(8,128)} fusion(bf16[768,2048]{1,0:T(8,128)(2,1)} %constant_dynamic-update-slice_fusion.9, bf16[2048,1280]{1,0:T(8,128)(2,1)} %all-gather.3.cloned.1.call-done), kind=kOutput, calls=%fused_computation.364 | convolution fusion | flops 4026531840 | bytes 12320768 | tf_op jit(solution)/shard_map/dot_general | solution.py:30
  325.1 7.7 %multiply_convert_fusion = (bf16[768,640]{1,0:T(8,128)(2,1)S(1)}, bf16[768,640]{1,0:T(8,128)(2,1)S(1)}, bf16[768,640]{1,0:T(8,128)(2,1)S(1)}) fusion(f32[768,1280]{1,0:T(8,128)} %fusion.84, bf16[768,2048]{1,0:T(8,128)(2,1)} %copy-done.74, bf16[2048,640]{1,0:T(8,128)(2,1)} %all-gather.5.cloned.1.call-done), kind=kOutput, calls=%fused_computation.29 | convolution fusion | flops 2026045440 | bytes 12648448 | tf_op jit(solution)/shard_map/dot_general | solution.py:30
  340.9 4.0 convolution_convert_fusion.2
  345.1 3.8 fusion.82
  354.5 5.2 fusion.81
  364.5 8.0 %collective-permute-done.35 = bf16[96,2048]{1,0:T(8,128)(2,1)S(1)} collective-permute-done((bf16[96,2048]{1,0:T(8,128)(2,1)S(1)}, bf16[96,2048]{1,0:T(8,128)(2,1)S(1)}, u32[]{:S(2)}, u32[]{:S(2)}) %collective-permute-start.35) | collective-permute-done | bytes 393248 | tf_op jit(solution)/shard_map/ppermute | solution.py:271
  372.4 15.6 %collective-permute-done.34 = bf16[96,2048]{1,0:T(8,128)(2,1)S(1)} collective-permute-done((bf16[96,2048]{1,0:T(8,128)(2,1)S(1)}, bf16[96,2048]{1,0:T(8,128)(2,1)S(1)}, u32[]{:S(2)}, u32[]{:S(2)}) %collective-permute-start.34) | collective-permute-done | bytes 393248 | tf_op jit(solution)/shard_map/ppermute | solution.py:271
  388.0 9.8 %collective-permute-done.44 = bf16[96,2048]{1,0:T(8,128)(2,1)S(1)} collective-permute-done((bf16[96,2048]{1,0:T(8,128)(2,1)S(1)}, bf16[96,2048]{1,0:T(8,128)(2,1)S(1)}, u32[]{:S(2)}, u32[]{:S(2)}) %collective-permute-start.44) | collective-permute-done | bytes 393248 | tf_op jit(solution)/shard_map/ppermute | solution.py:271
  397.7 23.0 %collective-permute-done.43 = bf16[96,2048]{1,0:T(8,128)(2,1)S(1)} collective-permute-done((bf16[96,2048]{1,0:T(8,128)(2,1)S(1)}, bf16[96,2048]{1,0:T(8,128)(2,1)S(1)}, u32[]{:S(2)}, u32[]{:S(2)}) %collective-permute-start.43) | collective-permute-done | bytes 393248 | tf_op jit(solution)/shard_map/ppermute | solution.py:271
  425.2 10.0 %collective-permute-done.47 = bf16[96,2048]{1,0:T(8,128)(2,1)S(1)} collective-permute-done((bf16[96,2048]{1,0:T(8,128)(2,1)S(1)}, bf16[96,2048]{1,0:T(8,128)(2,1)S(1)}, u32[]{:S(2)}, u32[]{:S(2)}) %collective-permute-start.47) | collective-permute-done | bytes 393248 | tf_op jit(solution)/shard_map/ppermute | solution.py:271
  435.2 21.6 %collective-permute-done.46 = bf16[96,2048]{1,0:T(8,128)(2,1)S(1)} collective-permute-done((bf16[96,2048]{1,0:T(8,128)(2,1)S(1)}, bf16[96,2048]{1,0:T(8,128)(2,1)S(1)}, u32[]{:S(2)}, u32[]{:S(2)}) %collective-permute-start.46) | collective-permute-done | bytes 393248 | tf_op jit(solution)/shard_map/ppermute | solution.py:271
  467.3 20.2 %attend_backward.1 = (bf16[768,768]{1,0:T(8,128)(2,1)S(1)}, f32[8,128]{1,0:T(8,128)S(1)}) custom-call(s32[4]{0:T(128)S(1)} %pad_add_fusion.meta_ref, bf16[768,768]{1,0:T(8,128)(2,1)S(1)} %convolution_convert_fusion.8.rows_ref, bf16[768,256]{1,0:T(8,128)(2,1)S(1)} %convolution_convert_fusion.9.grad_ref, f32[8,768]{1,0:T(8,128)S(1)} %get-tuple-element.21.log_ref, ...), custom_call_target="tpu_custom_call" | custom-call | flops 1509949440 | bytes 9437184 | tf_op jit(solution)/shard_map/attend_backward/pallas_call | solution.py:218
  487.6 4.1 convolution_convert_fusion.1
  492.9 8.8 %convolution_convert_fusion = bf16[2048,1280]{1,0:T(8,128)(2,1)} fusion(bf16[768,2048]{1,0:T(8,128)(2,1)} %constant_dynamic-update-slice_fusion.9, bf16[768,640]{1,0:T(8,128)(2,1)S(1)} %copy-done.96, bf16[768,640]{1,0:T(8,128)(2,1)} %copy-done.97), kind=kOutput, calls=%fused_computation | convolution fusion | flops 4033085440 | bytes 10354688 | tf_op jit(solution)/shard_map/dot_general | solution.py:30
  503.9 4.2 convolution_convert_fusion.5
  515.6 3.7 collective-permute-start.70
  527.5 4.1 fusion.83
  533.7 13.5 %collective-permute-start.51 = (bf16[96,2048]{1,0:T(8,128)(2,1)S(1)}, bf16[96,2048]{1,0:T(8,128)(2,1)S(1)}, u32[]{:S(2)}, u32[]{:S(2)}) collective-permute-start(bf16[96,2048]{1,0:T(8,128)(2,1)S(1)} %get-tuple-element.85), channel_id=1, source_target_pairs={{0,4},{2,6},{4,0},{6,2},{1,5},{3,7},{5,1},{7,3},{8,12},{10,14},{12... | collective-permute-start | bytes 1179656 | tf_op jit(solution)/shard_map/ppermute | solution.py:271
  549.6 5.9 collective-permute-done.52
  555.5 17.4 %collective-permute-done.51 = bf16[96,2048]{1,0:T(8,128)(2,1)S(1)} collective-permute-done((bf16[96,2048]{1,0:T(8,128)(2,1)S(1)}, bf16[96,2048]{1,0:T(8,128)(2,1)S(1)}, u32[]{:S(2)}, u32[]{:S(2)}) %collective-permute-start.51) | collective-permute-done | bytes 393248 | tf_op jit(solution)/shard_map/ppermute | solution.py:271
  574.8 3.8 collective-permute-start.59
  584.8 4.8 collective-permute-done.58
  592.8 8.8 %collective-permute-done.55 = bf16[128,768]{1,0:T(8,128)(2,1)S(1)} collective-permute-done((bf16[128,768]{1,0:T(8,128)(2,1)S(1)}, bf16[128,768]{1,0:T(8,128)(2,1)S(1)}, u32[]{:S(2)}, u32[]{:S(2)}) %collective-permute-start.55) | collective-permute-done | bytes 196640 | tf_op jit(solution)/shard_map/ppermute | solution.py:271
  612.0 7.1 %collective-permute-done.60 = bf16[128,1280]{1,0:T(8,128)(2,1)S(1)} collective-permute-done((bf16[128,1280]{1,0:T(8,128)(2,1)S(1)}, bf16[128,1280]{1,0:T(8,128)(2,1)S(1)}, u32[]{:S(2)}, u32[]{:S(2)}) %collective-permute-start.60) | collective-permute-done | bytes 327712 | tf_op jit(solution)/shard_map/ppermute | solution.py:271
  619.1 5.2 collective-permute-done.62
  624.4 14.6 %collective-permute-done.61 = bf16[128,1280]{1,0:T(8,128)(2,1)S(1)} collective-permute-done((bf16[128,1280]{1,0:T(8,128)(2,1)S(1)}, bf16[128,1280]{1,0:T(8,128)(2,1)S(1)}, u32[]{:S(2)}, u32[]{:S(2)}) %collective-permute-start.61) | collective-permute-done | bytes 327712 | tf_op jit(solution)/shard_map/ppermute | solution.py:271
  (456 shorter events, 165.5 us)
Async XLA Ops:
  7.2 308.2 %all-gather.3.cloned.1.call-start = ((), (), s32[]{:S(2)}) async-start(), calls=%async_computation.4 | async-start | bytes 6553600 | tf_op jit(solution)/shard_map/all_gather | solution.py:364
  10.4 101.5 %collective-permute-start.2 = (bf16[96,2048]{1,0:T(8,128)(2,1)S(1)}, bf16[96,2048]{1,0:T(8,128)(2,1)S(1)}, u32[]{:S(2)}, u32[]{:S(2)}) collective-permute-start(bf16[96,2048]{1,0:T(8,128)(2,1)S(1)} %get-tuple-element.67), channel_id=1, source_target_pairs={{0,6},{2,0},{4,2},{6,4},{1,7},{3,1},{5,3},{7,5},{8,14},{10,8},{12,... | collective-permute-start | bytes 1179656 | tf_op jit(solution)/shard_map/ppermute | solution.py:271
  15.5 97.1 %collective-permute-start.1 = (bf16[96,2048]{1,0:T(8,128)(2,1)S(1)}, bf16[96,2048]{1,0:T(8,128)(2,1)S(1)}, u32[]{:S(2)}, u32[]{:S(2)}) collective-permute-start(bf16[96,2048]{1,0:T(8,128)(2,1)S(1)} %get-tuple-element.67), channel_id=1, source_target_pairs={{0,4},{2,6},{4,0},{6,2},{1,5},{3,7},{5,1},{7,3},{8,12},{10,14},{12... | collective-permute-start | bytes 1179656 | tf_op jit(solution)/shard_map/ppermute | solution.py:271
  17.4 32.7 %collective-permute-start.26 = (bf16[128,1280]{1,0:T(8,128)(2,1)}, bf16[128,1280]{1,0:T(8,128)(2,1)S(1)}, u32[]{:S(2)}, u32[]{:S(2)}) collective-permute-start(bf16[128,1280]{1,0:T(8,128)(2,1)} %pad_maximum_fusion.15), channel_id=1, source_target_pairs={{0,2},{2,4},{4,6},{6,0},{1,3},{3,5},{5,7},{7,1},{8,10},{10,12},{12... | collective-permute-start | bytes 983048 | tf_op jit(solution)/shard_map/ppermute | solution.py:271
  19.2 45.1 %collective-permute-start.27 = (bf16[128,1280]{1,0:T(8,128)(2,1)}, bf16[128,1280]{1,0:T(8,128)(2,1)S(1)}, u32[]{:S(2)}, u32[]{:S(2)}) collective-permute-start(bf16[128,1280]{1,0:T(8,128)(2,1)} %pad_maximum_fusion.16), channel_id=1, source_target_pairs={{0,4},{2,6},{4,0},{6,2},{1,5},{3,7},{5,1},{7,3},{8,12},{10,14},{12... | collective-permute-start | bytes 983048 | tf_op jit(solution)/shard_map/ppermute | solution.py:271
  21.8 51.3 %collective-permute-start.28 = (bf16[128,1280]{1,0:T(8,128)(2,1)}, bf16[128,1280]{1,0:T(8,128)(2,1)S(1)}, u32[]{:S(2)}, u32[]{:S(2)}) collective-permute-start(bf16[128,1280]{1,0:T(8,128)(2,1)} %pad_maximum_fusion.17), channel_id=1, source_target_pairs={{0,6},{2,0},{4,2},{6,4},{1,7},{3,1},{5,3},{7,5},{8,14},{10,8},{12,... | collective-permute-start | bytes 983048 | tf_op jit(solution)/shard_map/ppermute | solution.py:271
  50.1 24.8 %collective-permute-start.11 = (bf16[128,256]{1,0:T(8,128)(2,1)}, bf16[128,256]{1,0:T(8,128)(2,1)S(1)}, u32[]{:S(2)}, u32[]{:S(2)}) collective-permute-start(bf16[128,256]{1,0:T(8,128)(2,1)} %get-tuple-element.171), channel_id=1, source_target_pairs={{0,2},{2,4},{4,6},{6,0},{1,3},{3,5},{5,7},{7,1},{8,10},{10,12},{12... | collective-permute-start | bytes 196616 | tf_op jit(solution)/shard_map/ppermute | solution.py:271
  74.8 250.2 %all-gather.5.cloned.1.call-start = ((), (), s32[]{:S(2)}) async-start(), calls=%async_computation.5 | async-start | bytes 3276800 | tf_op jit(solution)/shard_map/all_gather | solution.py:365
  75.9 24.2 %collective-permute-start.5 = (bf16[128,768]{1,0:T(8,128)(2,1)S(1)}, bf16[128,768]{1,0:T(8,128)(2,1)S(1)}, u32[]{:S(2)}, u32[]{:S(2)}) collective-permute-start(bf16[128,768]{1,0:T(8,128)(2,1)S(1)} %copy-done.68), channel_id=1, source_target_pairs={{0,4},{2,6},{4,0},{6,2},{1,5},{3,7},{5,1},{7,3},{8,12},{10,14},{12... | collective-permute-start | bytes 589832 | tf_op jit(solution)/shard_map/ppermute | solution.py:271
  86.8 26.8 %collective-permute-start = (bf16[96,2048]{1,0:T(8,128)(2,1)S(1)}, bf16[96,2048]{1,0:T(8,128)(2,1)S(1)}, u32[]{:S(2)}, u32[]{:S(2)}) collective-permute-start(bf16[96,2048]{1,0:T(8,128)(2,1)S(1)} %get-tuple-element.67), channel_id=1, source_target_pairs={{0,2},{2,4},{4,6},{6,0},{1,3},{3,5},{5,7},{7,1},{8,10},{10,12},{12... | collective-permute-start | bytes 1179656 | tf_op jit(solution)/shard_map/ppermute | solution.py:271
  108.9 42.4 %collective-permute-start.8 = (bf16[512,768]{1,0:T(8,128)(2,1)S(1)}, bf16[512,768]{1,0:T(8,128)(2,1)S(1)}, u32[]{:S(2)}, u32[]{:S(2)}) collective-permute-start(bf16[512,768]{1,0:T(8,128)(2,1)S(1)} %pad_maximum_fusion.10), channel_id=1, source_target_pairs={{0,16},{8,24},{16,0},{24,8},{1,17},{9,25},{17,1},{25,9},{2,18},{10... | collective-permute-start | bytes 2359304 | tf_op jit(solution)/shard_map/ppermute | solution.py:274
  110.4 43.5 %collective-permute-start.7 = (bf16[512,768]{1,0:T(8,128)(2,1)S(1)}, bf16[512,768]{1,0:T(8,128)(2,1)S(1)}, u32[]{:S(2)}, u32[]{:S(2)}) collective-permute-start(bf16[512,768]{1,0:T(8,128)(2,1)S(1)} %pad_maximum_fusion.10), channel_id=1, source_target_pairs={{0,8},{8,0},{16,24},{24,16},{1,9},{9,1},{17,25},{25,17},{2,10},{10... | collective-permute-start | bytes 2359304 | tf_op jit(solution)/shard_map/ppermute | solution.py:274
  111.9 39.4 %collective-permute-start.17 = (bf16[256,256]{1,0:T(8,128)(2,1)S(1)}, bf16[256,256]{1,0:T(8,128)(2,1)S(1)}, u32[]{:S(2)}, u32[]{:S(2)}) collective-permute-start(bf16[256,256]{1,0:T(8,128)(2,1)S(1)} %slice.366), channel_id=1, source_target_pairs={{0,8},{8,0},{16,24},{24,16},{1,9},{9,1},{17,25},{25,17},{2,10},{10... | collective-permute-start | bytes 393224 | tf_op jit(solution)/shard_map/ppermute | solution.py:274
  112.5 35.1 %collective-permute-start.16 = (bf16[256,256]{1,0:T(8,128)(2,1)S(1)}, bf16[256,256]{1,0:T(8,128)(2,1)S(1)}, u32[]{:S(2)}, u32[]{:S(2)}) collective-permute-start(bf16[256,256]{1,0:T(8,128)(2,1)S(1)} %slice.365), channel_id=1, source_target_pairs={{0,16},{8,24},{16,0},{24,8},{1,17},{9,25},{17,1},{25,9},{2,18},{10... | collective-permute-start | bytes 393224 | tf_op jit(solution)/shard_map/ppermute | solution.py:274
  113.7 51.7 %collective-permute-start.3 = (bf16[384,2048]{1,0:T(8,128)(2,1)S(1)}, bf16[384,2048]{1,0:T(8,128)(2,1)S(1)}, u32[]{:S(2)}, u32[]{:S(2)}) collective-permute-start(bf16[384,2048]{1,0:T(8,128)(2,1)S(1)} %pad_maximum_fusion.4), channel_id=1, source_target_pairs={{0,1},{1,0},{2,3},{3,2},{4,5},{5,4},{6,7},{7,6},{8,9},{9,8},{10,11... | collective-permute-start | bytes 4718600 | tf_op jit(solution)/shard_map/ppermute | solution.py:277
  183.4 60.3 %collective-permute-start.39 = (bf16[96,2048]{1,0:T(8,128)(2,1)}, bf16[96,2048]{1,0:T(8,128)(2,1)S(1)}, u32[]{:S(2)}, u32[]{:S(2)}) collective-permute-start(bf16[96,2048]{1,0:T(8,128)(2,1)} %get-tuple-element.61), channel_id=1, source_target_pairs={{0,6},{2,0},{4,2},{6,4},{1,7},{3,1},{5,3},{7,5},{8,14},{10,8},{12,... | collective-permute-start | bytes 1179656 | tf_op jit(solution)/shard_map/ppermute | solution.py:271
  186.8 62.8 %collective-permute-start.38 = (bf16[96,2048]{1,0:T(8,128)(2,1)}, bf16[96,2048]{1,0:T(8,128)(2,1)}, u32[]{:S(2)}, u32[]{:S(2)}) collective-permute-start(bf16[96,2048]{1,0:T(8,128)(2,1)} %get-tuple-element.61), channel_id=1, source_target_pairs={{0,4},{2,6},{4,0},{6,2},{1,5},{3,7},{5,1},{7,3},{8,12},{10,14},{12... | collective-permute-start | bytes 1179656 | tf_op jit(solution)/shard_map/ppermute | solution.py:271
  188.1 61.5 %collective-permute-start.37 = (bf16[96,2048]{1,0:T(8,128)(2,1)}, bf16[96,2048]{1,0:T(8,128)(2,1)}, u32[]{:S(2)}, u32[]{:S(2)}) collective-permute-start(bf16[96,2048]{1,0:T(8,128)(2,1)} %get-tuple-element.61), channel_id=1, source_target_pairs={{0,2},{2,4},{4,6},{6,0},{1,3},{3,5},{5,7},{7,1},{8,10},{10,12},{12... | collective-permute-start | bytes 1179656 | tf_op jit(solution)/shard_map/ppermute | solution.py:271
  189.3 28.2 %collective-permute-start.29 = (bf16[128,640]{1,0:T(8,128)(2,1)S(1)}, bf16[128,640]{1,0:T(8,128)(2,1)S(1)}, u32[]{:S(2)}, u32[]{:S(2)}) collective-permute-start(bf16[128,640]{1,0:T(8,128)(2,1)S(1)} %get-tuple-element.149), channel_id=1, source_target_pairs={{0,2},{2,4},{4,6},{6,0},{1,3},{3,5},{5,7},{7,1},{8,10},{10,12},{12... | collective-permute-start | bytes 491528 | tf_op jit(solution)/shard_map/ppermute | solution.py:271
  191.9 40.1 %collective-permute-start.31 = (bf16[128,640]{1,0:T(8,128)(2,1)S(1)}, bf16[128,640]{1,0:T(8,128)(2,1)S(1)}, u32[]{:S(2)}, u32[]{:S(2)}) collective-permute-start(bf16[128,640]{1,0:T(8,128)(2,1)S(1)} %get-tuple-element.150), channel_id=1, source_target_pairs={{0,6},{2,0},{4,2},{6,4},{1,7},{3,1},{5,3},{7,5},{8,14},{10,8},{12,... | collective-permute-start | bytes 491528 | tf_op jit(solution)/shard_map/ppermute | solution.py:271
  217.5 21.1 %collective-permute-start.30 = (bf16[128,640]{1,0:T(8,128)(2,1)S(1)}, bf16[128,640]{1,0:T(8,128)(2,1)S(1)}, u32[]{:S(2)}, u32[]{:S(2)}) collective-permute-start(bf16[128,640]{1,0:T(8,128)(2,1)S(1)} %get-tuple-element.151), channel_id=1, source_target_pairs={{0,4},{2,6},{4,0},{6,2},{1,5},{3,7},{5,1},{7,3},{8,12},{10,14},{12... | collective-permute-start | bytes 491528 | tf_op jit(solution)/shard_map/ppermute | solution.py:271
  232.0 19.3 %collective-permute-start.19 = (bf16[96,2048]{1,0:T(8,128)(2,1)}, bf16[96,2048]{1,0:T(8,128)(2,1)}, u32[]{:S(2)}, u32[]{:S(2)}) collective-permute-start(bf16[96,2048]{1,0:T(8,128)(2,1)} %get-tuple-element.92), channel_id=1, source_target_pairs={{0,6},{2,0},{4,2},{6,4},{1,7},{3,1},{5,3},{7,5},{8,14},{10,8},{12,... | collective-permute-start | bytes 1179656 | tf_op jit(solution)/shard_map/ppermute | solution.py:271
  238.6 17.7 %collective-permute-start.21 = (bf16[96,2048]{1,0:T(8,128)(2,1)}, bf16[96,2048]{1,0:T(8,128)(2,1)}, u32[]{:S(2)}, u32[]{:S(2)}) collective-permute-start(bf16[96,2048]{1,0:T(8,128)(2,1)} %get-tuple-element.93), channel_id=1, source_target_pairs={{0,2},{2,4},{4,6},{6,0},{1,3},{3,5},{5,7},{7,1},{8,10},{10,12},{12... | collective-permute-start | bytes 1179656 | tf_op jit(solution)/shard_map/ppermute | solution.py:271
  243.7 28.5 %collective-permute-start.20 = (bf16[96,2048]{1,0:T(8,128)(2,1)}, bf16[96,2048]{1,0:T(8,128)(2,1)}, u32[]{:S(2)}, u32[]{:S(2)}) collective-permute-start(bf16[96,2048]{1,0:T(8,128)(2,1)} %get-tuple-element.94), channel_id=1, source_target_pairs={{0,4},{2,6},{4,0},{6,2},{1,5},{3,7},{5,1},{7,3},{8,12},{10,14},{12... | collective-permute-start | bytes 1179656 | tf_op jit(solution)/shard_map/ppermute | solution.py:271
  249.6 271.7 %reduce-scatter.11.cloned.1.call-start = ((), (), s32[]{:S(2)}) async-start(), calls=%async_computation.9 | async-start | bytes 3276800 | tf_op jit(solution)/shard_map/reduce_scatter | solution.py:397
  251.2 60.1 %collective-permute-start.40 = (bf16[384,2048]{1,0:T(8,128)(2,1)S(1)}, bf16[384,2048]{1,0:T(8,128)(2,1)S(1)}, u32[]{:S(2)}, u32[]{:S(2)}) collective-permute-start(bf16[384,2048]{1,0:T(8,128)(2,1)S(1)} %pad_maximum_fusion.6), channel_id=1, source_target_pairs={{0,1},{1,0},{2,3},{3,2},{4,5},{5,4},{6,7},{7,6},{8,9},{9,8},{10,11... | collective-permute-start | bytes 4718600 | tf_op jit(solution)/shard_map/ppermute | solution.py:277
  275.5 33.4 %collective-permute-start.23 = (bf16[96,2048]{1,0:T(8,128)(2,1)S(1)}, bf16[96,2048]{1,0:T(8,128)(2,1)S(1)}, u32[]{:S(2)}, u32[]{:S(2)}) collective-permute-start(bf16[96,2048]{1,0:T(8,128)(2,1)S(1)} %get-tuple-element.63), channel_id=1, source_target_pairs={{0,4},{2,6},{4,0},{6,2},{1,5},{3,7},{5,1},{7,3},{8,12},{10,14},{12... | collective-permute-start | bytes 1179656 | tf_op jit(solution)/shard_map/ppermute | solution.py:271
  275.5 33.4 %collective-permute-start.22 = (bf16[96,2048]{1,0:T(8,128)(2,1)S(1)}, bf16[96,2048]{1,0:T(8,128)(2,1)S(1)}, u32[]{:S(2)}, u32[]{:S(2)}) collective-permute-start(bf16[96,2048]{1,0:T(8,128)(2,1)S(1)} %get-tuple-element.63), channel_id=1, source_target_pairs={{0,2},{2,4},{4,6},{6,0},{1,3},{3,5},{5,7},{7,1},{8,10},{10,12},{12... | collective-permute-start | bytes 1179656 | tf_op jit(solution)/shard_map/ppermute | solution.py:271
  344.9 228.9 %reduce-scatter.7.cloned.1.call-start = ((), (), s32[]{:S(2)}) async-start(), calls=%async_computation.7 | async-start | bytes 1310720 | tf_op jit(solution)/shard_map/reduce_scatter | solution.py:397
  349.1 23.3 %collective-permute-start.35 = (bf16[96,2048]{1,0:T(8,128)(2,1)S(1)}, bf16[96,2048]{1,0:T(8,128)(2,1)S(1)}, u32[]{:S(2)}, u32[]{:S(2)}) collective-permute-start(bf16[96,2048]{1,0:T(8,128)(2,1)S(1)} %get-tuple-element.90), channel_id=1, source_target_pairs={{0,2},{2,4},{4,6},{6,0},{1,3},{3,5},{5,7},{7,1},{8,10},{10,12},{12... | collective-permute-start | bytes 1179656 | tf_op jit(solution)/shard_map/ppermute | solution.py:271
  351.1 36.9 %collective-permute-start.34 = (bf16[96,2048]{1,0:T(8,128)(2,1)S(1)}, bf16[96,2048]{1,0:T(8,128)(2,1)S(1)}, u32[]{:S(2)}, u32[]{:S(2)}) collective-permute-start(bf16[96,2048]{1,0:T(8,128)(2,1)S(1)} %get-tuple-element.91), channel_id=1, source_target_pairs={{0,4},{2,6},{4,0},{6,2},{1,5},{3,7},{5,1},{7,3},{8,12},{10,14},{12... | collective-permute-start | bytes 1179656 | tf_op jit(solution)/shard_map/ppermute | solution.py:271
  359.9 28.1 %collective-permute-start.42 = (bf16[96,2048]{1,0:T(8,128)(2,1)S(1)}, bf16[96,2048]{1,0:T(8,128)(2,1)S(1)}, u32[]{:S(2)}, u32[]{:S(2)}) collective-permute-start(bf16[96,2048]{1,0:T(8,128)(2,1)S(1)} %get-tuple-element.86), channel_id=1, source_target_pairs={{0,6},{2,0},{4,2},{6,4},{1,7},{3,1},{5,3},{7,5},{8,14},{10,8},{12,... | collective-permute-start | bytes 1179656 | tf_op jit(solution)/shard_map/ppermute | solution.py:271
  361.3 36.5 %collective-permute-start.44 = (bf16[96,2048]{1,0:T(8,128)(2,1)S(1)}, bf16[96,2048]{1,0:T(8,128)(2,1)S(1)}, u32[]{:S(2)}, u32[]{:S(2)}) collective-permute-start(bf16[96,2048]{1,0:T(8,128)(2,1)S(1)} %get-tuple-element.87), channel_id=1, source_target_pairs={{0,2},{2,4},{4,6},{6,0},{1,3},{3,5},{5,7},{7,1},{8,10},{10,12},{12... | collective-permute-start | bytes 1179656 | tf_op jit(solution)/shard_map/ppermute | solution.py:271
  361.9 58.8 %collective-permute-start.43 = (bf16[96,2048]{1,0:T(8,128)(2,1)S(1)}, bf16[96,2048]{1,0:T(8,128)(2,1)S(1)}, u32[]{:S(2)}, u32[]{:S(2)}) collective-permute-start(bf16[96,2048]{1,0:T(8,128)(2,1)S(1)} %get-tuple-element.88), channel_id=1, source_target_pairs={{0,4},{2,6},{4,0},{6,2},{1,5},{3,7},{5,1},{7,3},{8,12},{10,14},{12... | collective-permute-start | bytes 1179656 | tf_op jit(solution)/shard_map/ppermute | solution.py:271
  423.6 33.2 %collective-permute-start.46 = (bf16[96,2048]{1,0:T(8,128)(2,1)S(1)}, bf16[96,2048]{1,0:T(8,128)(2,1)S(1)}, u32[]{:S(2)}, u32[]{:S(2)}) collective-permute-start(bf16[96,2048]{1,0:T(8,128)(2,1)S(1)} %get-tuple-element.58), channel_id=1, source_target_pairs={{0,4},{2,6},{4,0},{6,2},{1,5},{3,7},{5,1},{7,3},{8,12},{10,14},{12... | collective-permute-start | bytes 1179656 | tf_op jit(solution)/shard_map/ppermute | solution.py:271
  423.6 33.2 %collective-permute-start.45 = (bf16[96,2048]{1,0:T(8,128)(2,1)S(1)}, bf16[96,2048]{1,0:T(8,128)(2,1)S(1)}, u32[]{:S(2)}, u32[]{:S(2)}) collective-permute-start(bf16[96,2048]{1,0:T(8,128)(2,1)S(1)} %get-tuple-element.58), channel_id=1, source_target_pairs={{0,2},{2,4},{4,6},{6,0},{1,3},{3,5},{5,7},{7,1},{8,10},{10,12},{12... | collective-permute-start | bytes 1179656 | tf_op jit(solution)/shard_map/ppermute | solution.py:271
  464.3 114.3 %reduce-scatter.5.cloned.1.call-start = ((), (), s32[]{:S(2)}) async-start(), calls=%async_computation.6 | async-start | bytes 3932160 | tf_op jit(solution)/shard_map/reduce_scatter | solution.py:397
  491.7 113.6 %reduce-scatter.9.cloned.1.call-start = ((), (), s32[]{:S(2)}) async-start(), calls=%async_computation.8 | async-start | bytes 6553600 | tf_op jit(solution)/shard_map/reduce_scatter | solution.py:397
  508.1 19.4 %collective-permute-start.49 = (bf16[384,2048]{1,0:T(8,128)(2,1)}, bf16[384,2048]{1,0:T(8,128)(2,1)}, u32[]{:S(2)}, u32[]{:S(2)}) collective-permute-start(bf16[384,2048]{1,0:T(8,128)(2,1)} %convolution_convert_fusion.5), channel_id=1, source_target_pairs={{0,1},{1,0},{2,3},{3,2},{4,5},{5,4},{6,7},{7,6},{8,9},{9,8},{10,11... | collective-permute-start | bytes 4718600 | tf_op jit(solution)/shard_map/ppermute | solution.py:277
  523.5 23.7 %collective-permute-start.65 = (bf16[128,640]{1,0:T(8,128)(2,1)S(1)}, bf16[128,640]{1,0:T(8,128)(2,1)S(1)}, u32[]{:S(2)}, u32[]{:S(2)}) collective-permute-start(bf16[128,640]{1,0:T(8,128)(2,1)S(1)} %get-tuple-element.139), channel_id=1, source_target_pairs={{0,6},{2,0},{4,2},{6,4},{1,7},{3,1},{5,3},{7,5},{8,14},{10,8},{12,... | collective-permute-start | bytes 491528 | tf_op jit(solution)/shard_map/ppermute | solution.py:271
  526.4 20.9 %collective-permute-start.64 = (bf16[128,640]{1,0:T(8,128)(2,1)S(1)}, bf16[128,640]{1,0:T(8,128)(2,1)S(1)}, u32[]{:S(2)}, u32[]{:S(2)}) collective-permute-start(bf16[128,640]{1,0:T(8,128)(2,1)S(1)} %get-tuple-element.140), channel_id=1, source_target_pairs={{0,4},{2,6},{4,0},{6,2},{1,5},{3,7},{5,1},{7,3},{8,12},{10,14},{12... | collective-permute-start | bytes 491528 | tf_op jit(solution)/shard_map/ppermute | solution.py:271
  531.7 17.9 %collective-permute-start.50 = (bf16[96,2048]{1,0:T(8,128)(2,1)S(1)}, bf16[96,2048]{1,0:T(8,128)(2,1)S(1)}, u32[]{:S(2)}, u32[]{:S(2)}) collective-permute-start(bf16[96,2048]{1,0:T(8,128)(2,1)S(1)} %get-tuple-element.83), channel_id=1, source_target_pairs={{0,6},{2,0},{4,2},{6,4},{1,7},{3,1},{5,3},{7,5},{8,14},{10,8},{12,... | collective-permute-start | bytes 1179656 | tf_op jit(solution)/shard_map/ppermute | solution.py:271
  532.1 23.4 %collective-permute-start.52 = (bf16[96,2048]{1,0:T(8,128)(2,1)S(1)}, bf16[96,2048]{1,0:T(8,128)(2,1)S(1)}, u32[]{:S(2)}, u32[]{:S(2)}) collective-permute-start(bf16[96,2048]{1,0:T(8,128)(2,1)S(1)} %get-tuple-element.84), channel_id=1, source_target_pairs={{0,2},{2,4},{4,6},{6,0},{1,3},{3,5},{5,7},{7,1},{8,10},{10,12},{12... | collective-permute-start | bytes 1179656 | tf_op jit(solution)/shard_map/ppermute | solution.py:271
  533.7 39.1 %collective-permute-start.51 = (bf16[96,2048]{1,0:T(8,128)(2,1)S(1)}, bf16[96,2048]{1,0:T(8,128)(2,1)S(1)}, u32[]{:S(2)}, u32[]{:S(2)}) collective-permute-start(bf16[96,2048]{1,0:T(8,128)(2,1)S(1)} %get-tuple-element.85), channel_id=1, source_target_pairs={{0,4},{2,6},{4,0},{6,2},{1,5},{3,7},{5,1},{7,3},{8,12},{10,14},{12... | collective-permute-start | bytes 1179656 | tf_op jit(solution)/shard_map/ppermute | solution.py:271
  573.6 68.7 %collective-permute-start.53 = (bf16[96,2048]{1,0:T(8,128)(2,1)S(1)}, bf16[96,2048]{1,0:T(8,128)(2,1)S(1)}, u32[]{:S(2)}, u32[]{:S(2)}) collective-permute-start(bf16[96,2048]{1,0:T(8,128)(2,1)S(1)} %fusion.23), channel_id=1, source_target_pairs={{0,1},{1,0},{2,3},{3,2},{4,5},{5,4},{6,7},{7,6},{8,9},{9,8},{10,11... | collective-permute-start | bytes 1179656 | tf_op jit(solution)/shard_map/ppermute | solution.py:277
  583.7 18.0 %collective-permute-start.55 = (bf16[128,768]{1,0:T(8,128)(2,1)S(1)}, bf16[128,768]{1,0:T(8,128)(2,1)S(1)}, u32[]{:S(2)}, u32[]{:S(2)}) collective-permute-start(bf16[128,768]{1,0:T(8,128)(2,1)S(1)} %get-tuple-element.127), channel_id=1, source_target_pairs={{0,4},{2,6},{4,0},{6,2},{1,5},{3,7},{5,1},{7,3},{8,12},{10,14},{12... | collective-permute-start | bytes 589832 | tf_op jit(solution)/shard_map/ppermute | solution.py:271
  608.2 16.2 %collective-permute-start.62 = (bf16[128,1280]{1,0:T(8,128)(2,1)S(1)}, bf16[128,1280]{1,0:T(8,128)(2,1)S(1)}, u32[]{:S(2)}, u32[]{:S(2)}) collective-permute-start(bf16[128,1280]{1,0:T(8,128)(2,1)S(1)} %get-tuple-element.108), channel_id=1, source_target_pairs={{0,6},{2,0},{4,2},{6,4},{1,7},{3,1},{5,3},{7,5},{8,14},{10,8},{12,... | collective-permute-start | bytes 983048 | tf_op jit(solution)/shard_map/ppermute | solution.py:271
  610.5 28.5 %collective-permute-start.61 = (bf16[128,1280]{1,0:T(8,128)(2,1)S(1)}, bf16[128,1280]{1,0:T(8,128)(2,1)S(1)}, u32[]{:S(2)}, u32[]{:S(2)}) collective-permute-start(bf16[128,1280]{1,0:T(8,128)(2,1)S(1)} %get-tuple-element.109), channel_id=1, source_target_pairs={{0,4},{2,6},{4,0},{6,2},{1,5},{3,7},{5,1},{7,3},{8,12},{10,14},{12... | collective-permute-start | bytes 983048 | tf_op jit(solution)/shard_map/ppermute | solution.py:271
  (128 other events, 1115.9 us)
Sparse Core Ops, SparseCore 0:
  75.0 87.4 all-gather.2
  249.7 37.8 all-gather.4
  345.0 40.6 reduce-scatter.10
  464.4 29.0 reduce-scatter.6
  496.7 43.9 reduce-scatter.4
  543.8 61.4 reduce-scatter.8

commit v2 on v1

v2 whole, which is shorter than its diff:
```python
import functools
import math

import jax
import jax.numpy as jnp
from jax import lax
from jax.experimental import pallas as pl
from jax.experimental.pallas import tpu as pltpu
from jax.sharding import PartitionSpec as P

DK = 64
BUCKETS = 32
THRESHOLDS = (12, 16, 23, 32, 46, 64, 91)
NEGATIVE = -1e30
EPSILON = 1e-06
QUERY_BLOCK = 256
TILE = 128
VMEM_LIMIT = 48 * 1024 * 1024
LOW = jnp.bfloat16
WIDE = jnp.float32


def lasting(micros):
    return pl.CostEstimate(flops=int(micros * 1.1e9), bytes_accessed=int(micros * 3.3e6), transcendentals=0)


def bucket_of(offset):
    distance = jnp.abs(offset)
    beyond = 8 + sum(((distance >= threshold).astype(jnp.int32) for threshold in THRESHOLDS))
    within = jnp.where(distance < 8, distance, beyond)
    return within + jnp.where(offset > 0, BUCKETS // 2, 0)


def contract(left, right, left_dim, right_dim):
    return lax.dot_general(
        left, right, (((left_dim,), (right_dim,)), ((), ())), preferred_element_type=WIDE
    )


def segments_down(meta_ref, shape):
    place = lax.broadcasted_iota(jnp.int32, shape, 0)
    return (place >= meta_ref[0]).astype(jnp.int32) + (place >= meta_ref[1]).astype(jnp.int32)


def segments_across(meta_ref, first, width):
    place = first + lax.broadcasted_iota(jnp.int32, (1, width), 1)
    return (place >= meta_ref[0]).astype(jnp.int32) + (place >= meta_ref[1]).astype(jnp.int32)


def forward_kernel(
    meta_ref, rows_ref, bias_ref, mixed_ref, log_ref, peak_ref, flip_ref, part_ref, *, slots, heads
):
    width, block = heads * DK, QUERY_BLOCK
    part_ref[...] = segments_down(meta_ref, (slots, block))
    log_ref[...] = jnp.zeros_like(log_ref)
    peak_ref[...] = jnp.full(peak_ref.shape, NEGATIVE, WIDE)
    for head in range(heads):
        at = head * DK
        keys = rows_ref[:, width + at : width + at + DK]
        queries_flip = rows_ref[:, at : at + DK].T
        values_flip = rows_ref[:, 2 * width + at : 2 * width + at + DK].T
        peak = jnp.full((1, block), NEGATIVE, WIDE)
        for step in range(slots // block):
            first = step * block
            across = segments_across(meta_ref, first, block)
            logits = contract(keys, queries_flip[:, first : first + block], 1, 0)
            logits = jnp.where(part_ref[...] == across, logits, NEGATIVE)
            tops = jnp.max(logits, axis=0, keepdims=True)
            peak = jnp.maximum(peak, jnp.where(across < 2, tops, NEGATIVE))
            start = slots - block - first
            scores = logits + bias_ref[head, start : start + slots, :]
            highest = jnp.max(scores, axis=0, keepdims=True)
            weights = jnp.exp(scores - highest)
            total = jnp.sum(weights, axis=0, keepdims=True)
            mixed = contract(values_flip, weights.astype(LOW), 1, 0)
            flip_ref[at : at + DK, first : first + block] = mixed / total
            log_ref[head : head + 1, first : first + block] = highest + jnp.log(total)
        peak_ref[head : head + 1, :] = jnp.broadcast_to(
            jnp.max(peak, axis=1, keepdims=True), (1, peak_ref.shape[1])
        )
    mixed_ref[...] = flip_ref[...].T.astype(LOW)


def backward_kernel(
    meta_ref,
    rows_ref,
    grad_ref,
    log_ref,
    bias_ref,
    out_ref,
    table_ref,
    flip_ref,
    part_ref,
    sums_ref,
    down_ref,
    *,
    slots,
    heads,
):
    width, block = heads * DK, QUERY_BLOCK
    part_ref[...] = segments_down(meta_ref, (slots, block))
    table_ref[...] = jnp.zeros_like(table_ref)
    lane = lax.broadcasted_iota(jnp.int32, (1, table_ref.shape[1]), 1)
    offsets = tile_offsets()
    marks = [bucket_of(offsets + shift * TILE) for shift in (-1, 0, 1)]
    for head in range(heads):
        at = head * DK
        queries = rows_ref[:, at : at + DK]
        keys = rows_ref[:, width + at : width + at + DK]
        values = rows_ref[:, 2 * width + at : 2 * width + at + DK]
        grads = grad_ref[:, at : at + DK]
        queries_flip, keys_flip, grads_flip = queries.T, keys.T, grads.T
        sums_ref[...] = jnp.zeros_like(sums_ref)
        for step in range(slots // block):
            first = step * block
            across = segments_across(meta_ref, first, block)
            start = slots - block - first
            logits = contract(keys, queries_flip[:, first : first + block], 1, 0)
            scores = logits + bias_ref[head, start : start + slots, :]
            scores = scores - log_ref[head : head + 1, first : first + block]
            chance = jnp.exp(jnp.where(part_ref[...] == across, scores, NEGATIVE))
            grad_chance = contract(values, grads_flip[:, first : first + block], 1, 0)
            delta = jnp.sum(chance * grad_chance, axis=0, keepdims=True)
            grad_scores = chance * (grad_chance - delta)
            sums_ref[start : start + slots, :] += grad_scores
            rounded = grad_scores.astype(LOW)
            grad_keys = contract(rounded, queries[first : first + block, :], 1, 0)
            grad_values = contract(chance.astype(LOW), grads[first : first + block, :], 1, 0)
            if step == 0:
                down_ref[:, :DK] = grad_keys
                down_ref[:, DK:] = grad_values
            else:
                down_ref[:, :DK] += grad_keys
                down_ref[:, DK:] += grad_values
            flip_ref[at : at + DK, first : first + block] = contract(keys_flip, rounded, 1, 0)
        out_ref[:, width + at : width + at + DK] = down_ref[:, :DK].astype(LOW)
        out_ref[:, 2 * width + at : 2 * width + at + DK] = down_ref[:, DK:].astype(LOW)
        near = [jnp.zeros((TILE, TILE), WIDE) for _ in marks]
        far = [jnp.zeros((TILE, TILE), WIDE) for _ in range(2)]
        for down in range((2 * slots - block) // TILE):
            for across in range(block // TILE):
                shift = down - (slots - block) // TILE - across
                tile = sums_ref[down * TILE : (down + 1) * TILE, across * TILE : (across + 1) * TILE]
                if abs(shift) < 2:
                    near[shift + 1] = near[shift + 1] + tile
                else:
                    far[int(shift > 0)] = far[int(shift > 0)] + tile
        row = jnp.where(lane == BUCKETS // 2 - 1, jnp.sum(far[0]), 0.0)
        row = row + jnp.where(lane == BUCKETS - 1, jnp.sum(far[1]), 0.0)
        for bucket in range(BUCKETS):
            held = sum(
                jnp.where(mark == bucket, tile, 0.0) for mark, tile in zip(marks, near, strict=True)
            )
            row = row + jnp.where(lane == bucket, jnp.sum(held), 0.0)
        table_ref[head : head + 1, :] = row
    out_ref[:, :width] = flip_ref[...].T.astype(LOW)


def tile_offsets():
    return lax.broadcasted_iota(jnp.int32, (TILE, TILE), 0) - lax.broadcasted_iota(jnp.int32, (TILE, TILE), 1)


def bias_kernel(table_ref, out_ref, *, slots, heads):
    block = QUERY_BLOCK
    offsets = tile_offsets()
    buckets = [bucket_of(offsets + shift * TILE) for shift in (-1, 0, 1)]
    for head in range(heads):
        tiles = []
        for marks in buckets:
            tile = jnp.full((TILE, TILE), table_ref[head, 0], WIDE)
            for bucket in range(1, BUCKETS):
                tile = jnp.where(marks == bucket, table_ref[head, bucket], tile)
            tiles.append(tile)
        for down in range((2 * slots - block) // TILE):
            for across in range(block // TILE):
                shift = down - (slots - block) // TILE - across
                if abs(shift) < 2:
                    tile = tiles[shift + 1]
                else:
                    far = table_ref[head, BUCKETS - 1 if shift > 0 else BUCKETS // 2 - 1]
                    tile = jnp.full((TILE, TILE), far, WIDE)
                out_ref[head, down * TILE : (down + 1) * TILE, across * TILE : (across + 1) * TILE] = tile


def bias_master(table, slots):
    heads = table.shape[0]
    shape = (heads, 2 * slots - QUERY_BLOCK, QUERY_BLOCK)
    return pl.pallas_call(
        functools.partial(bias_kernel, slots=slots, heads=heads),
        out_shape=jax.ShapeDtypeStruct(shape, WIDE),
        in_specs=[whole(pltpu.SMEM)],
        out_specs=whole(),
        compiler_params=pltpu.CompilerParams(vmem_limit_bytes=VMEM_LIMIT),
        cost_estimate=lasting(2),
        name="bias_master",
    )(table)


def whole(memory=pltpu.VMEM):
    return pl.BlockSpec(memory_space=memory)


def attend_forward(meta, rows_in, bias, slots, heads):
    width, block = heads * DK, QUERY_BLOCK
    return pl.pallas_call(
        functools.partial(forward_kernel, slots=slots, heads=heads),
        out_shape=(
            jax.ShapeDtypeStruct((slots, width), LOW),
            jax.ShapeDtypeStruct((8, slots), WIDE),
            jax.ShapeDtypeStruct((8, 128), WIDE),
        ),
        in_specs=[whole(pltpu.SMEM), whole(), whole()],
        out_specs=(whole(), whole(), whole()),
        scratch_shapes=[
            pltpu.VMEM((width, slots), WIDE),
            pltpu.VMEM((slots, block), jnp.int32),
        ],
        compiler_params=pltpu.CompilerParams(vmem_limit_bytes=VMEM_LIMIT),
        cost_estimate=lasting(10),
        name="attend_forward",
    )(meta, rows_in, bias)


def attend_backward(meta, rows_in, grad_in, log_total, bias, slots, heads):
    width, block = heads * DK, QUERY_BLOCK
    return pl.pallas_call(
        functools.partial(backward_kernel, slots=slots, heads=heads),
        out_shape=(
            jax.ShapeDtypeStruct((slots, 3 * width), LOW),
            jax.ShapeDtypeStruct((8, 128), WIDE),
        ),
        in_specs=[whole(pltpu.SMEM), whole(), whole(), whole(), whole()],
        out_specs=(whole(), whole()),
        scratch_shapes=[
            pltpu.VMEM((width, slots), WIDE),
            pltpu.VMEM((slots, block), jnp.int32),
            pltpu.VMEM((2 * slots - block, block), WIDE),
            pltpu.VMEM((slots, 2 * DK), WIDE),
        ],
        compiler_params=pltpu.CompilerParams(vmem_limit_bytes=VMEM_LIMIT),
        cost_estimate=lasting(15),
        name="attend_backward",
    )(meta, rows_in, grad_in, log_total, bias)


def gelu_with_slope(value):
    scale = math.sqrt(2.0 / math.pi)
    square = value * value
    bend = jnp.tanh(scale * (value + 0.044715 * value * square))
    active = 0.5 * value * (1.0 + bend)
    slope = 0.5 * (1.0 + bend) + 0.5 * value * (1.0 - bend * bend) * (scale * (1.0 + 3 * 0.044715 * square))
    return active, slope


def ffn_kernel(
    place_ref, rows_ref, grad_ref, *refs, count, units, tile
):
    gates, ups, downs = (refs[n * count : (n + 1) * count] for n in range(3))
    product_ref, both_ref, terms_ref = refs[3 * count :]
    depth = gates[0].shape[0]
    spans = [pl.ds(pl.multiple_of((place_ref[0] ^ n) * depth, depth), depth) for n in range(count)]

    def step(index, carry):
        rows = pl.ds(pl.multiple_of(index * tile, tile), tile)
        def columns_of(source, pieces):
            return sum(
                contract(source[rows, span], piece[...], 1, 0) for span, piece in zip(spans, pieces, strict=True)
            )

        gate_pre, upward = columns_of(rows_ref, gates), columns_of(rows_ref, ups)
        grad_product = columns_of(grad_ref, downs)
        active, slope = gelu_with_slope(gate_pre)
        product_ref[rows, :] = (active * upward).astype(LOW)
        both_ref[rows, :units] = (grad_product * upward * slope).astype(LOW)
        both_ref[rows, units:] = (grad_product * active).astype(LOW)
        for span, gate, up in zip(spans, gates, ups, strict=True):
            terms = contract(both_ref[rows, :units], gate[...], 1, 1)
            terms_ref[rows, span] = (terms + contract(both_ref[rows, units:], up[...], 1, 1)).astype(LOW)
        return carry

    lax.fori_loop(0, rows_ref.shape[0] // tile, step, 0)


def ffn_both_ways(place, rows_in, grad_in, gates, ups, downs):
    slots, model = rows_in.shape
    units = downs[0].shape[1]
    return pl.pallas_call(
        functools.partial(ffn_kernel, count=len(downs), units=units, tile=256),
        out_shape=(
            jax.ShapeDtypeStruct((slots, units), LOW),
            jax.ShapeDtypeStruct((slots, 2 * units), LOW),
            jax.ShapeDtypeStruct((slots, model), LOW),
        ),
        in_specs=[whole(pltpu.SMEM)] + [whole()] * (2 + 3 * len(downs)),
        out_specs=(whole(), whole(), whole()),
        compiler_params=pltpu.CompilerParams(vmem_limit_bytes=VMEM_LIMIT),
        cost_estimate=lasting(19),
        name="ffn_both_ways",
    )(place, rows_in, grad_in, *gates, *ups, *downs)


def ffn_out_kernel(place_ref, product_ref, *refs):
    pieces, terms_ref = refs[:-1], refs[-1]
    depth = pieces[0].shape[0]
    for n, piece in enumerate(pieces):
        span = pl.ds(pl.multiple_of((place_ref[0] ^ n) * depth, depth), depth)
        terms_ref[:, span] = contract(product_ref[...], piece[...], 1, 1).astype(LOW)


def ffn_out(place, product, pieces):
    slots, units = product.shape
    model = pieces[0].shape[0] * len(pieces)
    return pl.pallas_call(
        ffn_out_kernel,
        out_shape=jax.ShapeDtypeStruct((slots, model), LOW),
        in_specs=[whole(pltpu.SMEM)] + [whole()] * (1 + len(pieces)),
        out_specs=whole(),
        compiler_params=pltpu.CompilerParams(vmem_limit_bytes=VMEM_LIMIT),
        cost_estimate=lasting(5),
        name="ffn_out",
    )(place, product, *pieces)


def shards(
    tokens,
    out_grad,
    lengths,
    w_query,
    w_key,
    w_value,
    w_out,
    w_gate,
    w_up,
    w_down,
    gain_attn,
    gain_ffn,
    bias_table,
    clip_limit,
):
    groups, count, cores = (lax.axis_size(name) for name in ("fsdp", "ctx", "tp"))
    assert cores == 2
    group, here, core = (lax.axis_index(name) for name in ("fsdp", "ctx", "tp"))
    half = tokens.shape[1] // cores
    slots = tokens.shape[1] * count
    heads = bias_table.shape[0] // count
    head_width = heads * DK
    unit_width = w_gate.shape[1] // count
    weight_rows = w_query.shape[0]

    def flip(value, mask):
        return lax.ppermute(value, "fsdp", [(i, i ^ mask) for i in range(groups)])

    def swap(value):
        return lax.ppermute(value, "tp", [(0, 1), (1, 0)])

    def spread(parts, width):
        blocks = [
            jnp.concatenate([p[:, n * width : (n + 1) * width] for p in parts], axis=1) for n in range(count)
        ]
        return lax.all_to_all(jnp.concatenate(blocks, axis=0), "ctx", 0, 0, tiled=True)

    def return_rows(block):
        return lax.all_to_all(block, "ctx", 0, 0, tiled=True)

    def collect(rows, width):
        blocks = [rows[n * weight_rows : (n + 1) * weight_rows] for n in range(count)]
        return [
            jnp.concatenate([b[:, at : at + width] for b in blocks], axis=1).astype(WIDE)
            for at in range(0, rows.shape[1], width)
        ]

    def pieces_of(block):
        return [block] + [flip(block, n) for n in range(1, groups)]

    def assemble(pieces):
        rows = pieces[0].shape[0]
        result = jnp.zeros((groups * rows, pieces[0].shape[1]), LOW)
        for n, piece in enumerate(pieces):
            mask, start, part = piece if isinstance(piece, tuple) else (n, 0, piece)
            result = lax.dynamic_update_slice_in_dim(result, part, (group ^ mask) * rows + start, 0)
        return result

    def gather_quickly(block):
        if groups != 4:
            pieces = pieces_of(block)
            return assemble(pieces), pieces[-1]
        middle = block.shape[0] // 2
        first, second = flip(block, 1), flip(block, 2)
        low, high = flip(first[:middle], 2), flip(second[middle:], 1)
        return assemble([block, first, second, (3, 0, low), (3, middle, high)]), second

    def reduce_weights(terms):
        rows = terms.shape[0] // groups

        def block(mask):
            return lax.dynamic_slice_in_dim(terms, (group ^ mask) * rows, rows, 0)

        total = block(0).astype(WIDE)
        for mask in range(1, groups):
            total = total + flip(block(mask), mask).astype(WIDE)
        return total.astype(LOW)

    def after(value, *earlier):
        return lax.optimization_barrier((value, *earlier))[0]

    def together(*values):
        return lax.optimization_barrier(values)

    def gather_rows(piece):
        return lax.all_gather(piece, ("ctx", "tp"), axis=0, tiled=True)

    def reduce_rows(terms):
        return lax.psum_scatter(terms.astype(LOW), ("ctx", "tp"), scatter_dimension=0, tiled=True).astype(WIDE)

    def feed_forward(place, rows_in, grad_in, gate, up, down):
        if unit_width % 128 == 0:
            return ffn_both_ways(place, rows_in, grad_in, gate, up, down)
        gate, up, down = (assemble(pieces) for pieces in (gate, up, down))
        upward = contract(rows_in, up, 1, 0)
        active, slope = gelu_with_slope(contract(rows_in, gate, 1, 0))
        grad_product = contract(grad_in, down, 1, 0)
        product = (active * upward).astype(LOW)
        both = jnp.concatenate([grad_product * upward * slope, grad_product * active], axis=1).astype(LOW)
        terms = contract(both[:, :unit_width], gate, 1, 1) + contract(both[:, unit_width:], up, 1, 1)
        return product, both, terms.astype(LOW)

    def feed_forward_out(place, product, down):
        if unit_width % 128 == 0:
            return ffn_out(place, product, down)
        return contract(product, assemble(down), 1, 1).astype(LOW)

    def both_cores(piece):
        other = swap(piece)
        return jnp.where(
            core == 0, jnp.concatenate([piece, other], axis=0), jnp.concatenate([other, piece], axis=0)
        )

    def own_rows(value):
        return lax.dynamic_slice_in_dim(value[0], core * half, half, 0)

    def inverse_norm(value):
        return lax.rsqrt(jnp.mean(value * value, axis=-1, keepdims=True) + EPSILON)

    def norm_back(value, inverse, grad):
        along = jnp.mean(grad * value, axis=-1, keepdims=True)
        return inverse * grad - value * (inverse * inverse * inverse * along)

    ends = (lengths[0, 0], lengths[0, 0] + lengths[0, 1])
    meta = jnp.stack(ends).astype(jnp.int32)
    attn_gain = gain_attn.astype(WIDE)[:, None]
    ffn_gain = gain_ffn.astype(WIDE)[:, None]

    def scaled(weight, gain):
        return (weight.astype(WIDE) * gain).astype(LOW)

    query_key_value = [scaled(w, attn_gain) for w in (w_query, w_key, w_value)]
    inputs = own_rows(tokens).astype(WIDE)
    inverse_one = inverse_norm(inputs)
    row_place = (here * cores + core) * half + jnp.arange(half, dtype=jnp.int32)
    row_valid = (row_place < ends[1])[:, None]
    grad_out = jnp.where(row_valid, own_rows(out_grad).astype(WIDE), 0.0)
    my_table = lax.dynamic_slice_in_dim(bias_table, here * heads, heads, 0).astype(WIDE)

    bias = bias_master(my_table, slots)
    attn_mine = after(spread(query_key_value, head_width), bias)
    normed_rows = gather_rows(after((inputs * inverse_one).astype(LOW), attn_mine))
    attn_columns, arrived = gather_quickly(attn_mine)
    out_mine = spread([after(w_out, attn_mine)], head_width)
    normed = after(normed_rows, attn_columns, out_mine)
    out_pieces = pieces_of(after(out_mine, attn_columns))
    grad_rows = gather_rows(after(grad_out.astype(LOW), arrived))

    projected = contract(normed, attn_columns, 1, 0).astype(LOW)
    gate_mine = spread([scaled(after(w_gate, normed), ffn_gain)], unit_width)
    mixed, log_total, peaks = attend_forward(meta, projected, bias, slots, heads)
    branch_terms = contract(mixed, assemble(out_pieces), 1, 1).astype(LOW)
    branch_terms = after(branch_terms, gate_mine, grad_rows)
    up_mine = spread([scaled(after(w_up, gate_mine), ffn_gain)], unit_width)
    down_mine = spread([after(w_down, up_mine)], unit_width)
    gate_pieces = pieces_of(gate_mine)
    up_pieces = pieces_of(after(up_mine, *gate_pieces))
    branch = after(reduce_rows(branch_terms), down_mine, *up_pieces)
    down_pieces = pieces_of(after(down_mine, *up_pieces))
    hidden = inputs + branch
    inverse_two = inverse_norm(hidden)
    normed_ffn = gather_rows((hidden * inverse_two).astype(LOW))

    def sum_groups(left, right):
        return reduce_weights(contract(left, right, 0, 0).astype(LOW))

    place = group.astype(jnp.int32)[None]
    product, grad_both, ffn_terms = feed_forward(place, normed_ffn, grad_rows, gate_pieces, up_pieces, down_pieces)
    grad_normed_ffn = reduce_rows(ffn_terms)
    down_sum = sum_groups(after(grad_rows, ffn_terms), product)
    gate_up_terms = contract(after(normed_ffn, ffn_terms), grad_both, 0, 0).astype(LOW)
    out_terms = feed_forward_out(place, after(product, ffn_terms), down_pieces)
    gate_up_sum = reduce_weights(gate_up_terms)
    grad_normed_ffn = after(grad_normed_ffn, down_sum, gate_up_terms, out_terms)
    grad_hidden = grad_out + norm_back(hidden, inverse_two, grad_normed_ffn)
    branch_low = grad_hidden.astype(LOW)
    branch_rows, down_back, gate_up_sum = together(
        gather_rows(branch_low), return_rows(after(down_sum, branch_low)), gate_up_sum
    )

    grad_mixed = contract(branch_rows, assemble(out_pieces), 1, 0).astype(LOW)
    ffn_out_sum = reduce_rows(after(out_terms, branch_rows))
    grad_projected, table_terms = attend_backward(
        meta, projected, grad_mixed, log_total, bias, slots, heads
    )
    out_sum = sum_groups(branch_rows, after(mixed, grad_mixed))
    grad_projected, out_sum = together(grad_projected, out_sum)
    attn_terms = contract(normed, grad_projected, 0, 0).astype(LOW)
    attn_sum = reduce_weights(attn_terms)
    grad_normed = reduce_rows(contract(after(grad_projected, attn_terms), attn_columns, 1, 1))
    gate_up_back = return_rows(after(gate_up_sum, grad_mixed))
    gate_up_back, out_sum = together(gate_up_back, out_sum)
    attn_sum, out_back = together(attn_sum, return_rows(out_sum))
    attn_back = return_rows(attn_sum)
    grad_query_w, grad_key_w, grad_value_w = collect(attn_back, head_width)
    (grad_out_w,) = collect(out_back, head_width)
    (grad_down,) = collect(down_back, unit_width)
    grad_gate_w, grad_up_w = collect(gate_up_back, unit_width)
    mixed_out = both_cores((hidden + ffn_out_sum).astype(LOW))[None]
    grad_tokens = both_cores((grad_hidden + norm_back(inputs, inverse_one, grad_normed)).astype(LOW))[None]

    def gain_terms(weights, grads):
        return sum(jnp.sum(w.astype(WIDE) * g, axis=1) for w, g in zip(weights, grads, strict=True))

    gain_grads = jnp.stack(
        [
            gain_terms((w_query, w_key, w_value), (grad_query_w, grad_key_w, grad_value_w)),
            gain_terms((w_gate, w_up), (grad_gate_w, grad_up_w)),
        ]
    )
    gain_grads = gain_grads + swap(gain_grads)

    table_terms = after(table_terms, attn_sum)
    small = jnp.concatenate([table_terms[:heads, :BUCKETS], peaks[:heads, :1]], axis=1)
    blank = jnp.concatenate([jnp.zeros((1, BUCKETS), WIDE), jnp.full((1, 1), NEGATIVE, WIDE)], axis=1)
    is_sum = jnp.arange(BUCKETS + 1)[None, :] < BUCKETS
    small = jnp.where(
        (jnp.arange(count * heads) // heads == here)[:, None],
        jnp.tile(small, (count, 1)),
        blank,
    )

    def merge(first, second):
        return jnp.where(is_sum, first + second, jnp.maximum(first, second))

    mask = 1
    while mask < groups:
        small = merge(small, flip(small, mask))
        mask *= 2
    mask = 1
    while mask < count:
        small = merge(small, lax.ppermute(small, "ctx", [(i, i ^ mask) for i in range(count)]))
        mask *= 2
    grad_table, head_peaks = small[:, :BUCKETS], small[:, BUCKETS]
    factor = jnp.sqrt(clip_limit / jnp.maximum(head_peaks, clip_limit))
    factor_row = jnp.repeat(factor, DK)[None, :]

    def clipped(weight):
        return (weight.astype(WIDE) * factor_row).astype(LOW)

    return (
        mixed_out,
        grad_tokens,
        grad_query_w * attn_gain,
        grad_key_w * attn_gain,
        grad_value_w * attn_gain,
        grad_out_w,
        grad_gate_w * ffn_gain,
        grad_up_w * ffn_gain,
        grad_down,
        gain_grads[0],
        gain_grads[1],
        grad_table,
        head_peaks,
        clipped(w_query),
        clipped(w_key),
    )


def solution(mesh):
    rows, weight, gain = P("fsdp", "ctx", None), P(("fsdp", "ctx"), "tp"), P(("fsdp", "ctx"))
    return jax.shard_map(
        shards,
        mesh=mesh,
        in_specs=(rows, rows, P("fsdp", None)) + (weight,) * 7 + (gain, gain, P("tp", None), P("tp")),
        out_specs=(rows, rows) + (weight,) * 7 + (gain, gain, P("tp", None), P("tp"), weight, weight),
        check_vma=False,
    )
```

time: 662 us -> 526 us (0.79)
  starting transfers between devices: 141 us -> 82.6 us
  waiting for transfers between devices: 313 us -> 262 us
  matrix products: 69.2 us -> 35.1 us
  Pallas kernels: 29.5 us -> 51.7 us
  other arithmetic: 55.4 us -> 43.3 us
    ppermute x48 -> x0, waiting for transfers between devices: 252 us -> none  [around(): lax.ppermute(value, 'ctx', [(i, (i + steps) % count) for i in range(count)])]
    ppermute x48 -> x0, starting transfers between devices: 120 us -> none  [around(): lax.ppermute(value, 'ctx', [(i, (i + steps) % count) for i in range(count)])]
    ppermute x10 -> x30, waiting for transfers between devices: 54.1 us -> 156 us  [flip(): return lax.ppermute(value, 'fsdp', [(i, i ^ mask) for i in range(groups)])]
    all_to_all x0 -> x9, waiting for transfers between devices: none -> 52.8 us  [the longest x5 37.3 us: spread(): lax.all_to_all(jnp.concatenate(blocks, axis=0), 'ctx', 0, 0, tiled=True)]
    all_to_all x0 -> x9, starting transfers between devices: none -> 37.8 us  [the longest x5 22.5 us: spread(): lax.all_to_all(jnp.concatenate(blocks, axis=0), 'ctx', 0, 0, tiled=True)]
    dot_general x16 -> x8, matrix products: 69.2 us -> 35.1 us  [contract(): lax.dot_general(left, right, (((left_dim,), (right_dim,)), ((), ())), pre...]
    ppermute x10 -> x30, starting transfers between devices: 13.6 us -> 36.5 us  [flip(): return lax.ppermute(value, 'fsdp', [(i, i ^ mask) for i in range(groups)])]
    pallas_call x2 -> x5, Pallas kernels: 29.5 us -> 51.7 us  [the longest x1 19.6 us: ffn_both_ways(): pl.pallas_call(functools.partial(ffn_kernel, count=len(downs), units=unit...]
  transfers between devices with their start and end apart: 77 -> 52, of which waited for: 37 -> 26; matrix products, arithmetic and copies ran while one was open for 20% -> 17% of each run, Pallas kernels for 5% -> 6%
where the time goes in v2:
time: 526 us; the launch traced here: 521 us
  waiting for transfers between devices  262 us (50%)
  starting transfers between devices  82.6 us (16%)
  Pallas kernels  51.7 us (10%)
  other arithmetic  43.3 us (8%)
  matrix products  35.1 us (7%)
  local copies, waits for them, and re-layouts  29.4 us (6%)
  between operations  16.6 us (3%)
    ppermute x30, waiting for transfers between devices, flip(): return lax.ppermute(value, 'fsdp', [(i, i ^ mask) for i in range(groups)])  156 us
    all_to_all x5, waiting for transfers between devices, spread(): lax.all_to_all(jnp.concatenate(blocks, axis=0), 'ctx', 0, 0, tiled=True)  37.3 us
    ppermute x30, starting transfers between devices, flip(): return lax.ppermute(value, 'fsdp', [(i, i ^ mask) for i in range(groups)])  36.5 us
    dot_general x8, matrix products, contract(): lax.dot_general(left, right, (((left_dim,), (right_dim,)), ((), ())), pre...  35.1 us
    all_to_all x5, starting transfers between devices, spread(): lax.all_to_all(jnp.concatenate(blocks, axis=0), 'ctx', 0, 0, tiled=True)  22.5 us
    ppermute x2, waiting for transfers between devices, shards(): lax.ppermute(small, 'ctx', [(i, i ^ mask) for i in range(count)])  20.9 us
    pallas_call x1, Pallas kernels, ffn_both_ways(): pl.pallas_call(functools.partial(ffn_kernel, count=len(downs), units=unit...  19.6 us
    reduce_scatter x4, waiting for transfers between devices, reduce_rows(): lax.psum_scatter(terms.astype(LOW), ('ctx', 'tp'), scatter_dimension=0, t...  16.6 us
  transfers between devices with their start and end apart: 52, of which 26 were waited for; matrix products, arithmetic and copies ran while one was open for 17% of the time, Pallas kernels for 6%

profile of v2, /device:TPU:0, one launch (start us, length us, event | category | flops | bytes accessed | tf_op | source)
XLA Modules:
  0.0 520.8 jit_solution(1814239974499729551)
XLA Ops:
  10.3 6.3 %all-to-all-start = ((bf16[4,128,768]{2,1,0:T(8,128)(2,1)}), bf16[4,128,768]{2,1,0:T(8,128)(2,1)S(1)}, u32[]{:S(2)}, u32[]{:S(2)}) async-start(bf16[4,128,768]{2,1,0:T(8,128)(2,1)} %bitcast.4), calls=%async_computation | async-start | bytes 1572864 | tf_op jit(solution)/shard_map/all_to_all | solution.py:360
  23.1 13.6 %all-to-all-done = bf16[4,128,768]{2,1,0:T(8,128)(2,1)S(1)} async-done(((bf16[4,128,768]{2,1,0:T(8,128)(2,1)}), bf16[4,128,768]{2,1,0:T(8,128)(2,1)S(1)}, u32[]{:S(2)}, u32[]{:S(2)}) %all-to-all-start) | async-done | bytes 786464 | tf_op jit(solution)/shard_map/all_to_all | solution.py:360
  41.2 14.2 %collective-permute-done.1 = bf16[512,768]{1,0:T(8,128)(2,1)S(1)} collective-permute-done((bf16[512,768]{1,0:T(8,128)(2,1)S(1)}, bf16[512,768]{1,0:T(8,128)(2,1)S(1)}, u32[]{:S(2)}, u32[]{:S(2)}) %collective-permute-start.1) | collective-permute-done | bytes 786464 | tf_op jit(solution)/shard_map/ppermute | solution.py:351
  57.7 3.4 all-to-all-start.1
  61.8 14.2 %collective-permute-done = bf16[512,768]{1,0:T(8,128)(2,1)S(1)} collective-permute-done((bf16[512,768]{1,0:T(8,128)(2,1)S(1)}, bf16[512,768]{1,0:T(8,128)(2,1)S(1)}, u32[]{:S(2)}, u32[]{:S(2)}) %collective-permute-start) | collective-permute-done | bytes 786464 | tf_op jit(solution)/shard_map/ppermute | solution.py:351
  85.6 2.5 collective-permute-start.4
  92.5 3.9 collective-permute-done.5
  98.9 5.9 %all-to-all-start.2 = ((bf16[4,128,640]{2,1,0:T(8,128)(2,1)}), bf16[4,128,640]{2,1,0:T(8,128)(2,1)S(1)}, u32[]{:S(2)}, u32[]{:S(2)}) async-start(bf16[4,128,640]{2,1,0:T(8,128)(2,1)} %bitcast.8), calls=%async_computation.2 | async-start | bytes 1310720 | tf_op jit(solution)/shard_map/all_to_all | solution.py:360
  105.2 5.5 %convolution_convert_fusion.6.rows_ref = bf16[768,768]{1,0:T(8,128)(2,1)S(1)} fusion(bf16[768,2048]{1,0:T(8,128)(2,1)} %all-gather.5.cloned.1.call-done, bf16[2048,768]{1,0:T(8,128)(2,1)} %constant_dynamic-update-slice_fusion.4), kind=kOutput, calls=%fused_computation.17 | convolution fusion | flops 2416508928 | bytes 7471104 | tf_op jit(solution)/shard_map/dot_general | solution.py:35
  110.7 9.6 %attend_forward.1 = (bf16[768,256]{1,0:T(8,128)(2,1)S(1)}, f32[8,768]{1,0:T(8,128)S(1)}, f32[8,128]{1,0:T(8,128)S(1)}) custom-call(s32[2]{0:T(128)S(1)} %pad_add_fusion.meta_ref, bf16[768,768]{1,0:T(8,128)(2,1)S(1)} %convolution_convert_fusion.6.rows_ref, f32[4,1280,256]{2,1,0:T(8,128)} %copy-done.4), custom_call_target="tpu_custom_call" | custom-call | flops 11000000512 | bytes 33000000 | tf_op jit(solution)/shard_map/attend_forward/pallas_call | solution.py:205
  120.3 2.7 convolution_convert_fusion.3
  123.0 9.8 %all-gather.7.cloned.1.call-done.grad_ref = bf16[768,2048]{1,0:T(8,128)(2,1)} async-done(((bf16[96,2048]{1,0:T(8,128)(2,1)}), bf16[768,2048]{1,0:T(8,128)(2,1)}) %all-gather.7.cloned.1.call-update) | async-done | bytes 3145744 | tf_op jit(solution)/shard_map/all_gather | solution.py:410
  135.1 3.5 all-to-all-start.3
  138.6 2.9 collective-permute-start.9
  142.1 23.7 %all-to-all-done.3 = bf16[4,128,640]{2,1,0:T(8,128)(2,1)S(1)} async-done(((bf16[4,128,640]{2,1,0:T(8,128)(2,1)}), bf16[4,128,640]{2,1,0:T(8,128)(2,1)S(1)}, u32[]{:S(2)}, u32[]{:S(2)}) %all-to-all-start.3) | async-done | bytes 655392 | tf_op jit(solution)/shard_map/all_to_all | solution.py:360
  167.9 3.5 all-to-all-start.4
  171.5 3.3 collective-permute-start.12
  175.5 16.6 %reduce-scatter.5.cloned.1.call-done = bf16[96,2048]{1,0:T(8,128)(2,1)} async-done(((bf16[768,2048]{1,0:T(8,128)(2,1)}), bf16[96,2048]{1,0:T(8,128)(2,1)}) %reduce-scatter.5.cloned.1.call-update) | async-done | bytes 393232 | tf_op jit(solution)/shard_map/reduce_scatter | solution.py:413
  194.0 8.5 %collective-permute-done.11.refs_6_ = bf16[512,640]{1,0:T(8,128)(2,1)} collective-permute-done((bf16[512,640]{1,0:T(8,128)(2,1)S(1)}, bf16[512,640]{1,0:T(8,128)(2,1)}, u32[]{:S(2)}, u32[]{:S(2)}) %collective-permute-start.11) | collective-permute-done | bytes 655392 | tf_op jit(solution)/shard_map/ppermute | solution.py:351
  209.5 15.0 %collective-permute-done.15.refs_11_.refs_3_ = bf16[512,640]{1,0:T(8,128)(2,1)S(1)} collective-permute-done((bf16[512,640]{1,0:T(8,128)(2,1)S(1)}, bf16[512,640]{1,0:T(8,128)(2,1)S(1)}, u32[]{:S(2)}, u32[]{:S(2)}) %collective-permute-start.15) | collective-permute-done | bytes 655392 | tf_op jit(solution)/shard_map/ppermute | solution.py:351
  224.5 13.1 %collective-permute-done.14.refs_10_.refs_2_ = bf16[512,640]{1,0:T(8,128)(2,1)S(1)} collective-permute-done((bf16[512,640]{1,0:T(8,128)(2,1)S(1)}, bf16[512,640]{1,0:T(8,128)(2,1)S(1)}, u32[]{:S(2)}, u32[]{:S(2)}) %collective-permute-start.14) | collective-permute-done | bytes 655392 | tf_op jit(solution)/shard_map/ppermute | solution.py:351
  238.4 6.2 %all-gather.9.cloned.1.call-done.rows_ref = bf16[768,2048]{1,0:T(8,128)(2,1)} async-done(((bf16[96,2048]{1,0:T(8,128)(2,1)}), bf16[768,2048]{1,0:T(8,128)(2,1)}) %all-gather.9.cloned.1.call-update) | async-done | bytes 3145744 | tf_op jit(solution)/shard_map/all_gather | solution.py:410
  244.6 19.6 %ffn_both_ways.1 = (bf16[768,640]{1,0:T(8,128)(2,1)}, bf16[768,1280]{1,0:T(8,128)(2,1)}, bf16[768,2048]{1,0:T(8,128)(2,1)}) custom-call(s32[1]{0:T(128)} %bitcast.16.place_ref, bf16[768,2048]{1,0:T(8,128)(2,1)} %all-gather.9.cloned.1.call-done.rows_ref, bf16[768,2048]{1,0:T(8,128)(2,1)} %all-gather.7.cloned.1.call-done.grad_ref, ...), custom_call_target="tpu_custom_call" | custom-call | flops 20899999744 | bytes 62700000 | tf_op jit(solution)/shard_map/ffn_both_ways/pallas_call | solution.py:287
  265.4 4.7 convolution_convert_fusion.4
  275.9 6.0 %convolution_convert_fusion = bf16[2048,1280]{1,0:T(8,128)(2,1)} fusion(bf16[768,2048]{1,0:T(8,128)(2,1)S(1)} %copy-done.41, bf16[768,1280]{1,0:T(8,128)(2,1)S(1)} %copy-done.45), kind=kOutput, calls=%fused_computation | convolution fusion | flops 4029153280 | bytes 10354688 | tf_op jit(solution)/shard_map/dot_general | solution.py:35
  282.0 5.4 %ffn_out.1 = bf16[768,2048]{1,0:T(8,128)(2,1)} custom-call(s32[1]{0:T(128)} %bitcast.16.place_ref, bf16[768,640]{1,0:T(8,128)(2,1)S(1)} %copy-done.5, bf16[512,640]{1,0:T(8,128)(2,1)S(1)} %bitcast.73, bf16[512,640]{1,0:T(8,128)(2,1)} %collective-permute-done.13.refs_9_.refs_1_, bf16[512,640]{1,0:T(8,128)(2,1)S(1)} %copy-done.3, bf16[512,640]{1,0:T(8,128)(2,1)S(1)} %copy-done.1), custom_call_target="tpu_custom_call" | custom-call | flops 5500000256 | bytes 16500000 | tf_op jit(solution)/shard_map/ffn_out/pallas_call | solution.py:313
  287.4 2.8 collective-permute-done.16
  290.2 14.5 %collective-permute-done.18 = bf16[512,640]{1,0:T(8,128)(2,1)} collective-permute-done((bf16[512,640]{1,0:T(8,128)(2,1)}, bf16[512,640]{1,0:T(8,128)(2,1)}, u32[]{:S(2)}, u32[]{:S(2)}) %collective-permute-start.18) | collective-permute-done | bytes 655392 | tf_op jit(solution)/shard_map/ppermute | solution.py:351
  306.0 2.6 add_convert_fusion.2
  311.3 4.1 constant_dynamic-slice_fusion.8
  318.9 3.5 all-to-all-start.5
  322.7 24.7 %collective-permute-done.19 = bf16[512,1280]{1,0:T(8,128)(2,1)S(1)} collective-permute-done((bf16[512,1280]{1,0:T(8,128)(2,1)}, bf16[512,1280]{1,0:T(8,128)(2,1)S(1)}, u32[]{:S(2)}, u32[]{:S(2)}) %collective-permute-start.19) | collective-permute-done | bytes 1310752 | tf_op jit(solution)/shard_map/ppermute | solution.py:351
  347.4 26.0 %collective-permute-done.21 = bf16[512,1280]{1,0:T(8,128)(2,1)} collective-permute-done((bf16[512,1280]{1,0:T(8,128)(2,1)}, bf16[512,1280]{1,0:T(8,128)(2,1)}, u32[]{:S(2)}, u32[]{:S(2)}) %collective-permute-start.21) | collective-permute-done | bytes 1310752 | tf_op jit(solution)/shard_map/ppermute | solution.py:351
  374.7 3.8 add_convert_fusion
  380.6 3.0 convolution_convert_fusion.7.grad_ref
  389.1 14.9 %attend_backward.1 = (bf16[768,768]{1,0:T(8,128)(2,1)S(1)}, f32[8,128]{1,0:T(8,128)S(1)}) custom-call(s32[2]{0:T(128)S(1)} %pad_add_fusion.meta_ref, bf16[768,768]{1,0:T(8,128)(2,1)S(1)} %copy-done.7, bf16[768,256]{1,0:T(8,128)(2,1)S(1)} %convolution_convert_fusion.7.grad_ref, f32[8,768]{1,0:T(8,128)S(1)} %get-tuple-element.79.log_ref, f32[4,1280,256]{2,1,0:T(8,128)} %copy-done.4), custom_call_target="tpu_custom_call" | custom-call | flops 16499999744 | bytes 49500000 | tf_op jit(solution)/shard_map/attend_backward/pallas_call | solution.py:226
  404.0 3.6 all-to-all-start.6
  409.7 6.2 %convolution_convert_fusion.2 = bf16[2048,768]{1,0:T(8,128)(2,1)} fusion(bf16[768,2048]{1,0:T(8,128)(2,1)} %all-gather.5.cloned.1.call-done, bf16[768,768]{1,0:T(8,128)(2,1)S(1)} %get-tuple-element.83), kind=kOutput, calls=%fused_computation.2 | convolution fusion | flops 2417491968 | bytes 7471104 | tf_op jit(solution)/shard_map/dot_general | solution.py:35
  415.9 5.9 %convolution_convert_fusion.1 = bf16[768,2048]{1,0:T(8,128)(2,1)} fusion(bf16[768,768]{1,0:T(8,128)(2,1)S(1)} %get-tuple-element.83, bf16[2048,768]{1,0:T(8,128)(2,1)} %constant_dynamic-update-slice_fusion.4), kind=kOutput, calls=%fused_computation.1 | convolution fusion | flops 2417491968 | bytes 7471104 | tf_op jit(solution)/shard_map/dot_general | solution.py:35
  421.9 3.2 constant_dynamic-slice_fusion.2
  429.8 15.5 %all-to-all-done.6 = bf16[4,128,1280]{2,1,0:T(8,128)(2,1)S(1)} async-done(((bf16[4,128,1280]{2,1,0:T(8,128)(2,1)}), bf16[4,128,1280]{2,1,0:T(8,128)(2,1)S(1)}, u32[]{:S(2)}, u32[]{:S(2)}) %all-to-all-start.6) | async-done | bytes 1310752 | tf_op jit(solution)/shard_map/all_to_all | solution.py:363
  445.3 3.4 all-to-all-start.7
  448.7 9.5 %collective-permute-done.29 = bf16[512,768]{1,0:T(8,128)(2,1)} collective-permute-done((bf16[512,768]{1,0:T(8,128)(2,1)}, bf16[512,768]{1,0:T(8,128)(2,1)}, u32[]{:S(2)}, u32[]{:S(2)}) %collective-permute-start.29) | collective-permute-done | bytes 786464 | tf_op jit(solution)/shard_map/ppermute | solution.py:351
  459.6 3.1 add_convert_fusion.1
  465.2 2.5 fusion.1
  469.9 4.8 all-to-all-start.8
  476.8 18.4 %collective-permute-done.33 = f32[16,33]{1,0:T(8,128)S(1)} collective-permute-done((f32[16,33]{1,0:T(8,128)S(1)}, f32[16,33]{1,0:T(8,128)S(1)}, u32[]{:S(2)}, u32[]{:S(2)}) %collective-permute-start.33) | collective-permute-done | bytes 2144 | tf_op jit(solution)/shard_map/ppermute | solution.py:556
  495.2 4.3 collective-permute-start.34
  (259 shorter events, 100.4 us)
Async XLA Ops:
  10.3 26.4 %all-to-all-start = ((bf16[4,128,768]{2,1,0:T(8,128)(2,1)}), bf16[4,128,768]{2,1,0:T(8,128)(2,1)S(1)}, u32[]{:S(2)}, u32[]{:S(2)}) async-start(bf16[4,128,768]{2,1,0:T(8,128)(2,1)} %bitcast.4), calls=%async_computation | async-start | bytes 1572864 | tf_op jit(solution)/shard_map/all_to_all | solution.py:360
  16.6 81.1 %all-gather.5.cloned.1.call-start = ((), (), s32[]{:S(2)}) async-start(), calls=%async_computation.13 | async-start | bytes 3538944 | tf_op jit(solution)/shard_map/all_gather | solution.py:410
  36.8 96.1 %all-gather.7.cloned.1.call-start = ((), (), s32[]{:S(2)}) async-start(), calls=%async_computation.14 | async-start | bytes 3538944 | tf_op jit(solution)/shard_map/all_gather | solution.py:410
  36.8 18.6 %collective-permute-start.1 = (bf16[512,768]{1,0:T(8,128)(2,1)S(1)}, bf16[512,768]{1,0:T(8,128)(2,1)S(1)}, u32[]{:S(2)}, u32[]{:S(2)}) collective-permute-start(bf16[512,768]{1,0:T(8,128)(2,1)S(1)} %bitcast.80), channel_id=1, source_target_pairs={{0,16},{8,24},{16,0},{24,8},{1,17},{9,25},{17,1},{25,9},{2,18},{10... | collective-permute-start | bytes 2359304 | tf_op jit(solution)/shard_map/ppermute | solution.py:351
  55.4 20.5 %collective-permute-start = (bf16[512,768]{1,0:T(8,128)(2,1)S(1)}, bf16[512,768]{1,0:T(8,128)(2,1)S(1)}, u32[]{:S(2)}, u32[]{:S(2)}) collective-permute-start(bf16[512,768]{1,0:T(8,128)(2,1)S(1)} %bitcast.81), channel_id=1, source_target_pairs={{0,8},{8,0},{16,24},{24,16},{1,9},{9,1},{17,25},{25,17},{2,10},{10... | collective-permute-start | bytes 2359304 | tf_op jit(solution)/shard_map/ppermute | solution.py:351
  57.7 27.9 %all-to-all-start.1 = ((bf16[4,128,256]{2,1,0:T(8,128)(2,1)}), bf16[4,128,256]{2,1,0:T(8,128)(2,1)S(1)}, u32[]{:S(2)}, u32[]{:S(2)}) async-start(bf16[4,128,256]{2,1,0:T(8,128)(2,1)} %bitcast.6), calls=%async_computation.1 | async-start | bytes 524288 | tf_op jit(solution)/shard_map/all_to_all | solution.py:360
  61.2 23.7 %collective-permute-start.3 = (bf16[256,768]{1,0:T(8,128)(2,1)S(1)}, bf16[256,768]{1,0:T(8,128)(2,1)S(1)}, u32[]{:S(2)}, u32[]{:S(2)}) collective-permute-start(bf16[256,768]{1,0:T(8,128)(2,1)S(1)} %slice.306), channel_id=1, source_target_pairs={{0,8},{8,0},{16,24},{24,16},{1,9},{9,1},{17,25},{25,17},{2,10},{10... | collective-permute-start | bytes 1179656 | tf_op jit(solution)/shard_map/ppermute | solution.py:351
  76.0 8.1 %collective-permute-start.2 = (bf16[256,768]{1,0:T(8,128)(2,1)S(1)}, bf16[256,768]{1,0:T(8,128)(2,1)S(1)}, u32[]{:S(2)}, u32[]{:S(2)}) collective-permute-start(bf16[256,768]{1,0:T(8,128)(2,1)S(1)} %slice.305), channel_id=1, source_target_pairs={{0,16},{8,24},{16,0},{24,8},{1,17},{9,25},{17,1},{25,9},{2,18},{10... | collective-permute-start | bytes 1179656 | tf_op jit(solution)/shard_map/ppermute | solution.py:351
  85.6 6.8 %collective-permute-start.4 = (bf16[512,256]{1,0:T(8,128)(2,1)S(1)}, bf16[512,256]{1,0:T(8,128)(2,1)S(1)}, u32[]{:S(2)}, u32[]{:S(2)}) collective-permute-start(bf16[512,256]{1,0:T(8,128)(2,1)S(1)} %bitcast.88), channel_id=1, source_target_pairs={{0,8},{8,0},{16,24},{24,16},{1,9},{9,1},{17,25},{25,17},{2,10},{10... | collective-permute-start | bytes 786440 | tf_op jit(solution)/shard_map/ppermute | solution.py:351
  88.1 8.3 %collective-permute-start.5 = (bf16[512,256]{1,0:T(8,128)(2,1)S(1)}, bf16[512,256]{1,0:T(8,128)(2,1)S(1)}, u32[]{:S(2)}, u32[]{:S(2)}) collective-permute-start(bf16[512,256]{1,0:T(8,128)(2,1)S(1)} %bitcast.89), channel_id=1, source_target_pairs={{0,16},{8,24},{16,0},{24,8},{1,17},{9,25},{17,1},{25,9},{2,18},{10... | collective-permute-start | bytes 786440 | tf_op jit(solution)/shard_map/ppermute | solution.py:351
  90.4 7.3 %collective-permute-start.6 = (bf16[512,256]{1,0:T(8,128)(2,1)S(1)}, bf16[512,256]{1,0:T(8,128)(2,1)S(1)}, u32[]{:S(2)}, u32[]{:S(2)}) collective-permute-start(bf16[512,256]{1,0:T(8,128)(2,1)S(1)} %bitcast.90), channel_id=1, source_target_pairs={{0,24},{8,16},{16,8},{24,0},{1,25},{9,17},{17,9},{25,1},{2,26},{10... | collective-permute-start | bytes 786440 | tf_op jit(solution)/shard_map/ppermute | solution.py:351
  98.9 33.9 %all-to-all-start.2 = ((bf16[4,128,640]{2,1,0:T(8,128)(2,1)}), bf16[4,128,640]{2,1,0:T(8,128)(2,1)S(1)}, u32[]{:S(2)}, u32[]{:S(2)}) async-start(bf16[4,128,640]{2,1,0:T(8,128)(2,1)} %bitcast.8), calls=%async_computation.2 | async-start | bytes 1310720 | tf_op jit(solution)/shard_map/all_to_all | solution.py:360
  104.8 87.3 %reduce-scatter.5.cloned.1.call-start = ((), (), s32[]{:S(2)}) async-start(), calls=%async_computation.15 | async-start | bytes 3538944 | tf_op jit(solution)/shard_map/reduce_scatter | solution.py:413
  135.1 30.7 %all-to-all-start.3 = ((bf16[4,128,640]{2,1,0:T(8,128)(2,1)}), bf16[4,128,640]{2,1,0:T(8,128)(2,1)S(1)}, u32[]{:S(2)}, u32[]{:S(2)}) async-start(bf16[4,128,640]{2,1,0:T(8,128)(2,1)} %bitcast.12), calls=%async_computation.4 | async-start | bytes 1310720 | tf_op jit(solution)/shard_map/all_to_all | solution.py:360
  138.6 32.9 %collective-permute-start.9 = (bf16[512,640]{1,0:T(8,128)(2,1)S(1)}, bf16[512,640]{1,0:T(8,128)(2,1)S(1)}, u32[]{:S(2)}, u32[]{:S(2)}) collective-permute-start(bf16[512,640]{1,0:T(8,128)(2,1)S(1)} %bitcast.65), channel_id=1, source_target_pairs={{0,24},{8,16},{16,8},{24,0},{1,25},{9,17},{17,9},{25,1},{2,26},{10... | collective-permute-start | bytes 1966088 | tf_op jit(solution)/shard_map/ppermute | solution.py:351
  141.5 30.0 %collective-permute-start.8 = (bf16[512,640]{1,0:T(8,128)(2,1)S(1)}, bf16[512,640]{1,0:T(8,128)(2,1)}, u32[]{:S(2)}, u32[]{:S(2)}) collective-permute-start(bf16[512,640]{1,0:T(8,128)(2,1)S(1)} %bitcast.66), channel_id=1, source_target_pairs={{0,16},{8,24},{16,0},{24,8},{1,17},{9,25},{17,1},{25,9},{2,18},{10... | collective-permute-start | bytes 1966088 | tf_op jit(solution)/shard_map/ppermute | solution.py:351
  141.8 29.7 %collective-permute-start.7 = (bf16[512,640]{1,0:T(8,128)(2,1)S(1)}, bf16[512,640]{1,0:T(8,128)(2,1)}, u32[]{:S(2)}, u32[]{:S(2)}) collective-permute-start(bf16[512,640]{1,0:T(8,128)(2,1)S(1)} %bitcast.67), channel_id=1, source_target_pairs={{0,8},{8,0},{16,24},{24,16},{1,9},{9,1},{17,25},{25,17},{2,10},{10... | collective-permute-start | bytes 1966088 | tf_op jit(solution)/shard_map/ppermute | solution.py:351
  167.9 34.6 %all-to-all-start.4 = ((bf16[4,128,640]{2,1,0:T(8,128)(2,1)}), bf16[4,128,640]{2,1,0:T(8,128)(2,1)S(1)}, u32[]{:S(2)}, u32[]{:S(2)}) async-start(bf16[4,128,640]{2,1,0:T(8,128)(2,1)} %bitcast.85), calls=%async_computation.5 | async-start | bytes 1310720 | tf_op jit(solution)/shard_map/all_to_all | solution.py:360
  171.4 73.2 %all-gather.9.cloned.1.call-start = ((), (), s32[]{:S(2)}) async-start(), calls=%async_computation.16 | async-start | bytes 3538944 | tf_op jit(solution)/shard_map/all_gather | solution.py:410
  171.5 22.5 %collective-permute-start.12 = (bf16[512,640]{1,0:T(8,128)(2,1)S(1)}, bf16[512,640]{1,0:T(8,128)(2,1)}, u32[]{:S(2)}, u32[]{:S(2)}) collective-permute-start(bf16[512,640]{1,0:T(8,128)(2,1)S(1)} %bitcast.74), channel_id=1, source_target_pairs={{0,24},{8,16},{16,8},{24,0},{1,25},{9,17},{17,9},{25,1},{2,26},{10... | collective-permute-start | bytes 1966088 | tf_op jit(solution)/shard_map/ppermute | solution.py:351
  174.8 27.6 %collective-permute-start.11 = (bf16[512,640]{1,0:T(8,128)(2,1)S(1)}, bf16[512,640]{1,0:T(8,128)(2,1)}, u32[]{:S(2)}, u32[]{:S(2)}) collective-permute-start(bf16[512,640]{1,0:T(8,128)(2,1)S(1)} %bitcast.75), channel_id=1, source_target_pairs={{0,16},{8,24},{16,0},{24,8},{1,17},{9,25},{17,1},{25,9},{2,18},{10... | collective-permute-start | bytes 1966088 | tf_op jit(solution)/shard_map/ppermute | solution.py:351
  174.8 27.6 %collective-permute-start.10 = (bf16[512,640]{1,0:T(8,128)(2,1)S(1)}, bf16[512,640]{1,0:T(8,128)(2,1)}, u32[]{:S(2)}, u32[]{:S(2)}) collective-permute-start(bf16[512,640]{1,0:T(8,128)(2,1)S(1)} %bitcast.76), channel_id=1, source_target_pairs={{0,8},{8,0},{16,24},{24,16},{1,9},{9,1},{17,25},{25,17},{2,10},{10... | collective-permute-start | bytes 1966088 | tf_op jit(solution)/shard_map/ppermute | solution.py:351
  205.7 103.0 %reduce-scatter.7.cloned.1.call-start = ((), (), s32[]{:S(2)}) async-start(), calls=%async_computation.17 | async-start | bytes 3538944 | tf_op jit(solution)/shard_map/reduce_scatter | solution.py:413
  205.9 18.6 %collective-permute-start.15 = (bf16[512,640]{1,0:T(8,128)(2,1)S(1)}, bf16[512,640]{1,0:T(8,128)(2,1)S(1)}, u32[]{:S(2)}, u32[]{:S(2)}) collective-permute-start(bf16[512,640]{1,0:T(8,128)(2,1)S(1)} %bitcast.69), channel_id=1, source_target_pairs={{0,24},{8,16},{16,8},{24,0},{1,25},{9,17},{17,9},{25,1},{2,26},{10... | collective-permute-start | bytes 1966088 | tf_op jit(solution)/shard_map/ppermute | solution.py:351
  207.7 29.8 %collective-permute-start.14 = (bf16[512,640]{1,0:T(8,128)(2,1)S(1)}, bf16[512,640]{1,0:T(8,128)(2,1)S(1)}, u32[]{:S(2)}, u32[]{:S(2)}) collective-permute-start(bf16[512,640]{1,0:T(8,128)(2,1)S(1)} %bitcast.70), channel_id=1, source_target_pairs={{0,16},{8,24},{16,0},{24,8},{1,17},{9,25},{17,1},{25,9},{2,18},{10... | collective-permute-start | bytes 1966088 | tf_op jit(solution)/shard_map/ppermute | solution.py:351
  209.2 29.3 %collective-permute-start.13 = (bf16[512,640]{1,0:T(8,128)(2,1)S(1)}, bf16[512,640]{1,0:T(8,128)(2,1)}, u32[]{:S(2)}, u32[]{:S(2)}) collective-permute-start(bf16[512,640]{1,0:T(8,128)(2,1)S(1)} %bitcast.71), channel_id=1, source_target_pairs={{0,8},{8,0},{16,24},{24,16},{1,9},{9,1},{17,25},{25,17},{2,10},{10... | collective-permute-start | bytes 1966088 | tf_op jit(solution)/shard_map/ppermute | solution.py:351
  264.2 114.3 %all-gather.11.cloned.1.call-start = ((), (), s32[]{:S(2)}) async-start(), calls=%async_computation.18 | async-start | bytes 3538944 | tf_op jit(solution)/shard_map/all_gather | solution.py:410
  272.4 17.8 %collective-permute-start.16 = (bf16[512,640]{1,0:T(8,128)(2,1)}, bf16[512,640]{1,0:T(8,128)(2,1)S(1)}, u32[]{:S(2)}, u32[]{:S(2)}) collective-permute-start(bf16[512,640]{1,0:T(8,128)(2,1)} %get-tuple-element.105), channel_id=1, source_target_pairs={{0,8},{8,0},{16,24},{24,16},{1,9},{9,1},{17,25},{25,17},{2,10},{10... | collective-permute-start | bytes 1966088 | tf_op jit(solution)/shard_map/ppermute | solution.py:351
  273.9 30.8 %collective-permute-start.18 = (bf16[512,640]{1,0:T(8,128)(2,1)}, bf16[512,640]{1,0:T(8,128)(2,1)}, u32[]{:S(2)}, u32[]{:S(2)}) collective-permute-start(bf16[512,640]{1,0:T(8,128)(2,1)} %get-tuple-element.106), channel_id=1, source_target_pairs={{0,24},{8,16},{16,8},{24,0},{1,25},{9,17},{17,9},{25,1},{2,26},{10... | collective-permute-start | bytes 1966088 | tf_op jit(solution)/shard_map/ppermute | solution.py:351
  275.4 30.7 %collective-permute-start.17 = (bf16[512,640]{1,0:T(8,128)(2,1)}, bf16[512,640]{1,0:T(8,128)(2,1)}, u32[]{:S(2)}, u32[]{:S(2)}) collective-permute-start(bf16[512,640]{1,0:T(8,128)(2,1)} %get-tuple-element.107), channel_id=1, source_target_pairs={{0,16},{8,24},{16,0},{24,8},{1,17},{9,25},{17,1},{25,9},{2,18},{10... | collective-permute-start | bytes 1966088 | tf_op jit(solution)/shard_map/ppermute | solution.py:351
  315.4 31.9 %collective-permute-start.19 = (bf16[512,1280]{1,0:T(8,128)(2,1)}, bf16[512,1280]{1,0:T(8,128)(2,1)S(1)}, u32[]{:S(2)}, u32[]{:S(2)}) collective-permute-start(bf16[512,1280]{1,0:T(8,128)(2,1)} %get-tuple-element.99), channel_id=1, source_target_pairs={{0,8},{8,0},{16,24},{24,16},{1,9},{9,1},{17,25},{25,17},{2,10},{10... | collective-permute-start | bytes 3932168 | tf_op jit(solution)/shard_map/ppermute | solution.py:351
  316.9 56.5 %collective-permute-start.21 = (bf16[512,1280]{1,0:T(8,128)(2,1)}, bf16[512,1280]{1,0:T(8,128)(2,1)}, u32[]{:S(2)}, u32[]{:S(2)}) collective-permute-start(bf16[512,1280]{1,0:T(8,128)(2,1)} %get-tuple-element.100), channel_id=1, source_target_pairs={{0,24},{8,16},{16,8},{24,0},{1,25},{9,17},{17,9},{25,1},{2,26},{10... | collective-permute-start | bytes 3932168 | tf_op jit(solution)/shard_map/ppermute | solution.py:351
  317.4 57.3 %collective-permute-start.20 = (bf16[512,1280]{1,0:T(8,128)(2,1)}, bf16[512,1280]{1,0:T(8,128)(2,1)}, u32[]{:S(2)}, u32[]{:S(2)}) collective-permute-start(bf16[512,1280]{1,0:T(8,128)(2,1)} %get-tuple-element.101), channel_id=1, source_target_pairs={{0,16},{8,24},{16,0},{24,8},{1,17},{9,25},{17,1},{25,9},{2,18},{10... | collective-permute-start | bytes 3932168 | tf_op jit(solution)/shard_map/ppermute | solution.py:351
  318.9 59.6 %all-to-all-start.5 = ((bf16[4,128,640]{2,1,0:T(8,128)(2,1)}), bf16[4,128,640]{2,1,0:T(8,128)(2,1)S(1)}, u32[]{:S(2)}, u32[]{:S(2)}) async-start(bf16[4,128,640]{2,1,0:T(8,128)(2,1)} %bitcast.17), calls=%async_computation.7 | async-start | bytes 1310720 | tf_op jit(solution)/shard_map/all_to_all | solution.py:363
  322.4 184.3 %reduce-scatter.9.cloned.1.call-start = ((), (), s32[]{:S(2)}) async-start(), calls=%async_computation.19 | async-start | bytes 3538944 | tf_op jit(solution)/shard_map/reduce_scatter | solution.py:413
  385.6 22.0 %collective-permute-start.23 = (bf16[512,256]{1,0:T(8,128)(2,1)}, bf16[512,256]{1,0:T(8,128)(2,1)}, u32[]{:S(2)}, u32[]{:S(2)}) collective-permute-start(bf16[512,256]{1,0:T(8,128)(2,1)} %get-tuple-element.116), channel_id=1, source_target_pairs={{0,8},{8,0},{16,24},{24,16},{1,9},{9,1},{17,25},{25,17},{2,10},{10... | collective-permute-start | bytes 786440 | tf_op jit(solution)/shard_map/ppermute | solution.py:351
  387.2 20.5 %collective-permute-start.25 = (bf16[512,256]{1,0:T(8,128)(2,1)}, bf16[512,256]{1,0:T(8,128)(2,1)}, u32[]{:S(2)}, u32[]{:S(2)}) collective-permute-start(bf16[512,256]{1,0:T(8,128)(2,1)} %get-tuple-element.117), channel_id=1, source_target_pairs={{0,24},{8,16},{16,8},{24,0},{1,25},{9,17},{17,9},{25,1},{2,26},{10... | collective-permute-start | bytes 786440 | tf_op jit(solution)/shard_map/ppermute | solution.py:351
  388.6 19.0 %collective-permute-start.24 = (bf16[512,256]{1,0:T(8,128)(2,1)}, bf16[512,256]{1,0:T(8,128)(2,1)}, u32[]{:S(2)}, u32[]{:S(2)}) collective-permute-start(bf16[512,256]{1,0:T(8,128)(2,1)} %get-tuple-element.118), channel_id=1, source_target_pairs={{0,16},{8,24},{16,0},{24,8},{1,17},{9,25},{17,1},{25,9},{2,18},{10... | collective-permute-start | bytes 786440 | tf_op jit(solution)/shard_map/ppermute | solution.py:351
  404.0 41.3 %all-to-all-start.6 = ((bf16[4,128,1280]{2,1,0:T(8,128)(2,1)}), bf16[4,128,1280]{2,1,0:T(8,128)(2,1)S(1)}, u32[]{:S(2)}, u32[]{:S(2)}) async-start(bf16[4,128,1280]{2,1,0:T(8,128)(2,1)} %bitcast.79), calls=%async_computation.10 | async-start | bytes 2621440 | tf_op jit(solution)/shard_map/all_to_all | solution.py:363
  407.5 100.5 %reduce-scatter.11.cloned.1.call-start = ((), (), s32[]{:S(2)}) async-start(), calls=%async_computation.20 | async-start | bytes 3538944 | tf_op jit(solution)/shard_map/reduce_scatter | solution.py:413
  425.0 23.7 %collective-permute-start.27 = (bf16[512,768]{1,0:T(8,128)(2,1)}, bf16[512,768]{1,0:T(8,128)(2,1)}, u32[]{:S(2)}, u32[]{:S(2)}) collective-permute-start(bf16[512,768]{1,0:T(8,128)(2,1)} %get-tuple-element.102), channel_id=1, source_target_pairs={{0,8},{8,0},{16,24},{24,16},{1,9},{9,1},{17,25},{25,17},{2,10},{10... | collective-permute-start | bytes 2359304 | tf_op jit(solution)/shard_map/ppermute | solution.py:351
  426.6 31.7 %collective-permute-start.29 = (bf16[512,768]{1,0:T(8,128)(2,1)}, bf16[512,768]{1,0:T(8,128)(2,1)}, u32[]{:S(2)}, u32[]{:S(2)}) collective-permute-start(bf16[512,768]{1,0:T(8,128)(2,1)} %get-tuple-element.103), channel_id=1, source_target_pairs={{0,24},{8,16},{16,8},{24,0},{1,25},{9,17},{17,9},{25,1},{2,26},{10... | collective-permute-start | bytes 2359304 | tf_op jit(solution)/shard_map/ppermute | solution.py:351
  428.0 31.6 %collective-permute-start.28 = (bf16[512,768]{1,0:T(8,128)(2,1)}, bf16[512,768]{1,0:T(8,128)(2,1)}, u32[]{:S(2)}, u32[]{:S(2)}) collective-permute-start(bf16[512,768]{1,0:T(8,128)(2,1)} %get-tuple-element.104), channel_id=1, source_target_pairs={{0,16},{8,24},{16,0},{24,8},{1,17},{9,25},{17,1},{25,9},{2,18},{10... | collective-permute-start | bytes 2359304 | tf_op jit(solution)/shard_map/ppermute | solution.py:351
  445.3 18.3 %all-to-all-start.7 = ((bf16[4,128,256]{2,1,0:T(8,128)(2,1)}), bf16[4,128,256]{2,1,0:T(8,128)(2,1)S(1)}, u32[]{:S(2)}, u32[]{:S(2)}) async-start(bf16[4,128,256]{2,1,0:T(8,128)(2,1)} %bitcast.25), calls=%async_computation.11 | async-start | bytes 524288 | tf_op jit(solution)/shard_map/all_to_all | solution.py:363
  467.8 6.9 %collective-permute-start.32 = (f32[16,33]{1,0:T(8,128)S(1)}, f32[16,33]{1,0:T(8,128)S(1)}, u32[]{:S(2)}, u32[]{:S(2)}) collective-permute-start(f32[16,33]{1,0:T(8,128)S(1)} %maximum_select_fusion.5), channel_id=1, source_target_pairs={{0,16},{8,24},{16,0},{24,8},{1,17},{9,25},{17,1},{25,9},{2,18},{10... | collective-permute-start | bytes 6344 | tf_op jit(solution)/shard_map/ppermute | solution.py:351
  469.9 32.5 %all-to-all-start.8 = ((bf16[4,128,768]{2,1,0:T(8,128)(2,1)}), bf16[4,128,768]{2,1,0:T(8,128)(2,1)S(1)}, u32[]{:S(2)}, u32[]{:S(2)}) async-start(bf16[4,128,768]{2,1,0:T(8,128)(2,1)} %bitcast.27), calls=%async_computation.12 | async-start | bytes 1572864 | tf_op jit(solution)/shard_map/all_to_all | solution.py:363
  474.7 20.5 %collective-permute-start.33 = (f32[16,33]{1,0:T(8,128)S(1)}, f32[16,33]{1,0:T(8,128)S(1)}, u32[]{:S(2)}, u32[]{:S(2)}) collective-permute-start(f32[16,33]{1,0:T(8,128)S(1)} %maximum_select_fusion.4), channel_id=1, source_target_pairs={{0,2},{2,0},{4,6},{6,4},{1,3},{3,1},{5,7},{7,5},{8,10},{10,8},{12,... | collective-permute-start | bytes 6344 | tf_op jit(solution)/shard_map/ppermute | solution.py:556
  495.2 6.8 %collective-permute-start.34 = (f32[16,33]{1,0:T(8,128)S(1)}, f32[16,33]{1,0:T(8,128)S(1)}, u32[]{:S(2)}, u32[]{:S(2)}) collective-permute-start(f32[16,33]{1,0:T(8,128)S(1)} %maximum_select_fusion.3), channel_id=1, source_target_pairs={{0,4},{2,6},{4,0},{6,2},{1,5},{3,7},{5,1},{7,3},{8,12},{10,14},{12... | collective-permute-start | bytes 6344 | tf_op jit(solution)/shard_map/ppermute | solution.py:556
  (50 other events, 444.4 us)
Sparse Core Ops, SparseCore 0:
  36.9 43.0 all-gather.4
  82.1 50.6 all-gather.6
  135.1 56.8 reduce-scatter.4
  205.8 38.7 all-gather.8
  264.3 39.1 reduce-scatter.6
  311.4 50.2 all-gather.10
  379.5 47.2 reduce-scatter.8
  429.2 68.2 reduce-scatter.10

commit v3 on v2

--- a/solution.py
+++ b/solution.py
@@ -321,6 +321,30 @@
     )(place, product, *pieces)
 
 
+def pack_kernel(gain_ref, *refs, count, scaled):
+    parts, out_ref = refs[:-1], refs[-1]
+    rows, width = parts[0].shape[0], parts[0].shape[1] // count
+    for n, (part, scale) in enumerate(zip(parts, scaled, strict=True)):
+        for block in range(count):
+            piece = part[:, block * width : (block + 1) * width]
+            if scale:
+                piece = (piece.astype(WIDE) * gain_ref[...]).astype(LOW)
+            out_ref[block * rows : (block + 1) * rows, n * width : (n + 1) * width] = piece
+
+
+def pack(gain, parts, scaled, count):
+    rows, columns = parts[0].shape
+    return pl.pallas_call(
+        functools.partial(pack_kernel, count=count, scaled=scaled),
+        out_shape=jax.ShapeDtypeStruct((count * rows, len(parts) * columns // count), LOW),
+        in_specs=[whole()] * (1 + len(parts)),
+        out_specs=whole(),
+        compiler_params=pltpu.CompilerParams(vmem_limit_bytes=VMEM_LIMIT),
+        cost_estimate=lasting(2),
+        name="pack",
+    )(gain, *parts)
+
+
 def shards(
     tokens,
     out_grad,
@@ -353,11 +377,20 @@
     def swap(value):
         return lax.ppermute(value, "tp", [(0, 1), (1, 0)])
 
-    def spread(parts, width):
-        blocks = [
-            jnp.concatenate([p[:, n * width : (n + 1) * width] for p in parts], axis=1) for n in range(count)
-        ]
-        return lax.all_to_all(jnp.concatenate(blocks, axis=0), "ctx", 0, 0, tiled=True)
+    def spread(parts, gain, scaled):
+        if parts[0].shape[1] // count % 128 == 0:
+            packed = pack(gain, parts, scaled, count)
+        else:
+            parts = [(p.astype(WIDE) * gain).astype(LOW) if s else p for p, s in zip(parts, scaled, strict=True)]
+            width = parts[0].shape[1] // count
+            packed = jnp.concatenate(
+                [
+                    jnp.concatenate([p[:, n * width : (n + 1) * width] for p in parts], axis=1)
+                    for n in range(count)
+                ],
+                axis=0,
+            )
+        return lax.all_to_all(packed, "ctx", 0, 0, tiled=True)
 
     def return_rows(block):
         return lax.all_to_all(block, "ctx", 0, 0, tiled=True)
@@ -387,18 +420,20 @@
         middle = block.shape[0] // 2
         first, second = flip(block, 1), flip(block, 2)
         low, high = flip(first[:middle], 2), flip(second[middle:], 1)
-        return assemble([block, first, second, (3, 0, low), (3, middle, high)]), second
+        return assemble([block, first, second, (3, 0, low), (3, middle, high)]), first, second
+
+    def blocks_of(terms):
+        rows = terms.shape[0] // groups
+        return [lax.dynamic_slice_in_dim(terms, (group ^ n) * rows, rows, 0) for n in range(groups)]
+
+    def flip_blocks(blocks):
+        return [block if n == 0 else flip(block, n) for n, block in enumerate(blocks)]
+
+    def sum_of(blocks):
+        return sum(block.astype(WIDE) for block in blocks).astype(LOW)
 
     def reduce_weights(terms):
-        rows = terms.shape[0] // groups
-
-        def block(mask):
-            return lax.dynamic_slice_in_dim(terms, (group ^ mask) * rows, rows, 0)
-
-        total = block(0).astype(WIDE)
-        for mask in range(1, groups):
-            total = total + flip(block(mask), mask).astype(WIDE)
-        return total.astype(LOW)
+        return sum_of(flip_blocks(blocks_of(terms)))
 
     def after(value, *earlier):
         return lax.optimization_barrier((value, *earlier))[0]
@@ -450,10 +485,6 @@
     attn_gain = gain_attn.astype(WIDE)[:, None]
     ffn_gain = gain_ffn.astype(WIDE)[:, None]
 
-    def scaled(weight, gain):
-        return (weight.astype(WIDE) * gain).astype(LOW)
-
-    query_key_value = [scaled(w, attn_gain) for w in (w_query, w_key, w_value)]
     inputs = own_rows(tokens).astype(WIDE)
     inverse_one = inverse_norm(inputs)
     row_place = (here * cores + core) * half + jnp.arange(half, dtype=jnp.int32)
@@ -462,22 +493,23 @@
     my_table = lax.dynamic_slice_in_dim(bias_table, here * heads, heads, 0).astype(WIDE)
 
     bias = bias_master(my_table, slots)
-    attn_mine = after(spread(query_key_value, head_width), bias)
+    attn_mine = after(
+        spread([w_query, w_key, w_value, w_out], attn_gain, (True, True, True, False)), bias
+    )
     normed_rows = gather_rows(after((inputs * inverse_one).astype(LOW), attn_mine))
-    attn_columns, arrived = gather_quickly(attn_mine)
-    out_mine = spread([after(w_out, attn_mine)], head_width)
-    normed = after(normed_rows, attn_columns, out_mine)
-    out_pieces = pieces_of(after(out_mine, attn_columns))
-    grad_rows = gather_rows(after(grad_out.astype(LOW), arrived))
+    all_columns, *arrived = gather_quickly(attn_mine)
+    attn_columns, out_columns = all_columns[:, : 3 * head_width], all_columns[:, 3 * head_width :]
+    gate_mine = spread([after(w_gate, attn_mine)], ffn_gain, (True,))
+    normed = after(normed_rows, all_columns, gate_mine)
+    grad_rows = gather_rows(after(grad_out.astype(LOW), *arrived))
 
     projected = contract(normed, attn_columns, 1, 0).astype(LOW)
-    gate_mine = spread([scaled(after(w_gate, normed), ffn_gain)], unit_width)
+    gate_pieces = pieces_of(after(gate_mine, all_columns))
     mixed, log_total, peaks = attend_forward(meta, projected, bias, slots, heads)
-    branch_terms = contract(mixed, assemble(out_pieces), 1, 1).astype(LOW)
-    branch_terms = after(branch_terms, gate_mine, grad_rows)
-    up_mine = spread([scaled(after(w_up, gate_mine), ffn_gain)], unit_width)
-    down_mine = spread([after(w_down, up_mine)], unit_width)
-    gate_pieces = pieces_of(gate_mine)
+    branch_terms = contract(mixed, out_columns, 1, 1).astype(LOW)
+    up_mine = spread([after(w_up, normed)], ffn_gain, (True,))
+    branch_terms = after(branch_terms, grad_rows, up_mine, *gate_pieces)
+    down_mine = spread([after(w_down, up_mine)], ffn_gain, (False,))
     up_pieces = pieces_of(after(up_mine, *gate_pieces))
     branch = after(reduce_rows(branch_terms), down_mine, *up_pieces)
     down_pieces = pieces_of(after(down_mine, *up_pieces))
@@ -485,41 +517,50 @@
     inverse_two = inverse_norm(hidden)
     normed_ffn = gather_rows((hidden * inverse_two).astype(LOW))
 
-    def sum_groups(left, right):
-        return reduce_weights(contract(left, right, 0, 0).astype(LOW))
-
     place = group.astype(jnp.int32)[None]
     product, grad_both, ffn_terms = feed_forward(place, normed_ffn, grad_rows, gate_pieces, up_pieces, down_pieces)
     grad_normed_ffn = reduce_rows(ffn_terms)
-    down_sum = sum_groups(after(grad_rows, ffn_terms), product)
-    gate_up_terms = contract(after(normed_ffn, ffn_terms), grad_both, 0, 0).astype(LOW)
     out_terms = feed_forward_out(place, after(product, ffn_terms), down_pieces)
-    gate_up_sum = reduce_weights(gate_up_terms)
-    grad_normed_ffn = after(grad_normed_ffn, down_sum, gate_up_terms, out_terms)
+    gate_terms = contract(after(normed_ffn, ffn_terms), grad_both[:, :unit_width], 0, 0).astype(LOW)
+    up_terms = contract(after(normed_ffn, ffn_terms), grad_both[:, unit_width:], 0, 0).astype(LOW)
+    down_terms = contract(after(grad_rows, ffn_terms), product, 0, 0).astype(LOW)
+    first_sum = reduce_weights(gate_terms)
+    grad_normed_ffn = after(grad_normed_ffn, first_sum, up_terms, down_terms, out_terms)
     grad_hidden = grad_out + norm_back(hidden, inverse_two, grad_normed_ffn)
     branch_low = grad_hidden.astype(LOW)
-    branch_rows, down_back, gate_up_sum = together(
-        gather_rows(branch_low), return_rows(after(down_sum, branch_low)), gate_up_sum
-    )
-
-    grad_mixed = contract(branch_rows, assemble(out_pieces), 1, 0).astype(LOW)
-    ffn_out_sum = reduce_rows(after(out_terms, branch_rows))
+    cut = unit_width * 3 // 5
+    second_blocks = [
+        jnp.concatenate(pair, axis=1)
+        for pair in zip(blocks_of(up_terms), blocks_of(down_terms[:, :cut]), strict=True)
+    ]
+    second_sum = sum_of(flip_blocks(second_blocks))
+    gathered = gather_rows(branch_low)
+    branch_rows, second_sum = together(gathered, second_sum)
+    ffn_out_sum = reduce_rows(after(out_terms, gathered))
+
+    grad_mixed = contract(branch_rows, out_columns, 1, 0).astype(LOW)
+    units = jnp.concatenate([first_sum, second_sum], axis=1)
+    units = after(units, grad_mixed)
     grad_projected, table_terms = attend_backward(
         meta, projected, grad_mixed, log_total, bias, slots, heads
     )
-    out_sum = sum_groups(branch_rows, after(mixed, grad_mixed))
-    grad_projected, out_sum = together(grad_projected, out_sum)
+    units_back = return_rows(units)
+    third_blocks = blocks_of(after(down_terms[:, cut:], second_sum))
+    out_blocks = blocks_of(contract(branch_rows, after(mixed, grad_mixed), 0, 0).astype(LOW))
+    third_sum = sum_of(
+        flip_blocks([jnp.concatenate(pair, axis=1) for pair in zip(out_blocks, third_blocks, strict=True)])
+    )
+    grad_projected, third_sum = together(grad_projected, third_sum)
     attn_terms = contract(normed, grad_projected, 0, 0).astype(LOW)
     attn_sum = reduce_weights(attn_terms)
     grad_normed = reduce_rows(contract(after(grad_projected, attn_terms), attn_columns, 1, 1))
-    gate_up_back = return_rows(after(gate_up_sum, grad_mixed))
-    gate_up_back, out_sum = together(gate_up_back, out_sum)
-    attn_sum, out_back = together(attn_sum, return_rows(out_sum))
-    attn_back = return_rows(attn_sum)
-    grad_query_w, grad_key_w, grad_value_w = collect(attn_back, head_width)
-    (grad_out_w,) = collect(out_back, head_width)
-    (grad_down,) = collect(down_back, unit_width)
-    grad_gate_w, grad_up_w = collect(gate_up_back, unit_width)
+    attn_sum, units_back = together(attn_sum, units_back)
+    attn_back = return_rows(jnp.concatenate([attn_sum, third_sum], axis=1))
+    grad_query_w, grad_key_w, grad_value_w, grad_out_w = collect(attn_back[:, : 4 * head_width], head_width)
+    grad_gate_w, grad_up_w = collect(units_back[:, : 2 * unit_width], unit_width)
+    (grad_down,) = collect(
+        jnp.concatenate([units_back[:, 2 * unit_width :], attn_back[:, 4 * head_width :]], axis=1), unit_width
+    )
     mixed_out = both_cores((hidden + ffn_out_sum).astype(LOW))[None]
     grad_tokens = both_cores((grad_hidden + norm_back(inputs, inverse_one, grad_normed)).astype(LOW))[None]
 

time: 526 us -> 500 us (0.951)
  waiting for transfers between devices: 262 us -> 235 us
  starting transfers between devices: 82.6 us -> 65.5 us
  local copies, waits for them, and re-layouts: 29.4 us -> 38.9 us
    ppermute x30 -> x27, waiting for transfers between devices: 156 us -> 110 us  [flip(): return lax.ppermute(value, 'fsdp', [(i, i ^ mask) for i in range(groups)])]
    reduce_scatter x4, waiting for transfers between devices: 16.6 us -> 42.1 us  [reduce_rows(): lax.psum_scatter(terms.astype(LOW), ('ctx', 'tp'), scatter_dimension=0, t...]
    all_gather x4, waiting for transfers between devices: 16.1 us -> 36.6 us  [gather_rows(): return lax.all_gather(piece, ('ctx', 'tp'), axis=0, tiled=True)]
    all_to_all x4 -> x2, waiting for transfers between devices: 15.5 us -> 0.01 us  [return_rows(): return lax.all_to_all(block, 'ctx', 0, 0, tiled=True)]
    ppermute x2, waiting for transfers between devices: 20.9 us -> 13.8 us  [shards(): lax.ppermute(small, 'ctx', [(i, i ^ mask) for i in range(count)])]
    all_to_all x4 -> x2, starting transfers between devices: 15.3 us -> 9.19 us  [return_rows(): return lax.all_to_all(block, 'ctx', 0, 0, tiled=True)]
    all_to_all x5 -> x4, starting transfers between devices: 22.5 us -> 16.9 us  [spread(): return lax.all_to_all(packed, 'ctx', 0, 0, tiled=True)]
    ppermute x30 -> x27, starting transfers between devices: 36.5 us -> 31.9 us  [flip(): return lax.ppermute(value, 'fsdp', [(i, i ^ mask) for i in range(groups)])]
  transfers between devices with their start and end apart: 52 -> 46, of which waited for: 26 -> 25; matrix products, arithmetic and copies ran while one was open for 17% -> 20% of each run, Pallas kernels for 6% -> 7%
where the time goes in v3:
time: 500 us; the launch traced here: 494 us
  waiting for transfers between devices  235 us (47%)
  starting transfers between devices  65.5 us (13%)
  Pallas kernels  56 us (11%)
  other arithmetic  46.4 us (9%)
  local copies, waits for them, and re-layouts  38.9 us (8%)
  matrix products  35.7 us (7%)
  between operations  16.4 us (3%)
    ppermute x27, waiting for transfers between devices, flip(): return lax.ppermute(value, 'fsdp', [(i, i ^ mask) for i in range(groups)])  110 us
    reduce_scatter x4, waiting for transfers between devices, reduce_rows(): lax.psum_scatter(terms.astype(LOW), ('ctx', 'tp'), scatter_dimension=0, t...  42.1 us
    all_gather x4, waiting for transfers between devices, gather_rows(): return lax.all_gather(piece, ('ctx', 'tp'), axis=0, tiled=True)  36.6 us
    dot_general x9, matrix products, contract(): lax.dot_general(left, right, (((left_dim,), (right_dim,)), ((), ())), pre...  35.7 us
    all_to_all x4, waiting for transfers between devices, spread(): return lax.all_to_all(packed, 'ctx', 0, 0, tiled=True)  32.8 us
    ppermute x27, starting transfers between devices, flip(): return lax.ppermute(value, 'fsdp', [(i, i ^ mask) for i in range(groups)])  31.9 us
    pallas_call x1, Pallas kernels, ffn_both_ways(): pl.pallas_call(functools.partial(ffn_kernel, count=len(downs), units=unit...  19.8 us
    all_to_all x4, starting transfers between devices, spread(): return lax.all_to_all(packed, 'ctx', 0, 0, tiled=True)  16.9 us
  transfers between devices with their start and end apart: 46, of which 25 were waited for; matrix products, arithmetic and copies ran while one was open for 20% of the time, Pallas kernels for 7%

profile of v3, /device:TPU:0, one launch (start us, length us, event | category | flops | bytes accessed | tf_op | source)
XLA Modules:
  0.0 494.2 jit_solution(9034336728359851050)
XLA Ops:
  13.5 6.4 %all-to-all-start = ((bf16[4,128,1024]{2,1,0:T(8,128)(2,1)}), bf16[4,128,1024]{2,1,0:T(8,128)(2,1)S(1)}, u32[]{:S(2)}, u32[]{:S(2)}) async-start(bf16[4,128,1024]{2,1,0:T(8,128)(2,1)} %bitcast.5), calls=%async_computation | async-start | bytes 2097152 | tf_op jit(solution)/shard_map/all_to_all | solution.py:393
  20.8 2.3 bias_master.1.bias_ref
  23.2 2.3 copy-done.16
  26.4 19.3 %all-to-all-done = bf16[4,128,1024]{2,1,0:T(8,128)(2,1)S(1)} async-done(((bf16[4,128,1024]{2,1,0:T(8,128)(2,1)}), bf16[4,128,1024]{2,1,0:T(8,128)(2,1)S(1)}, u32[]{:S(2)}, u32[]{:S(2)}) %all-to-all-start) | async-done | bytes 1048608 | tf_op jit(solution)/shard_map/all_to_all | solution.py:393
  52.7 17.3 %collective-permute-done.1 = bf16[512,1024]{1,0:T(8,128)(2,1)S(1)} collective-permute-done((bf16[512,1024]{1,0:T(8,128)(2,1)S(1)}, bf16[512,1024]{1,0:T(8,128)(2,1)S(1)}, u32[]{:S(2)}, u32[]{:S(2)}) %collective-permute-start.1) | collective-permute-done | bytes 1048608 | tf_op jit(solution)/shard_map/ppermute | solution.py:375
  73.0 3.5 all-to-all-start.1
  81.6 2.6 broadcast_in_dim.76
  85.3 2.4 constant_dynamic-update-slice_fusion.3
  92.8 3.0 all-to-all-done.1
  95.7 2.4 collective-permute-start.6
  100.3 3.5 all-to-all-start.2
  104.0 5.5 %fusion.3.rows_ref = bf16[768,768]{1,0:T(8,128)(2,1)S(1)} fusion(bf16[768,2048]{1,0:T(8,128)(2,1)} %all-gather.5.cloned.1.call-done, bf16[2048,1024]{1,0:T(8,128)(2,1)} %constant_dynamic-update-slice_fusion), kind=kOutput, calls=%fused_computation.23 | convolution fusion | flops 2416508928 | bytes 7471104 | tf_op jit(solution)/shard_map/dot_general | solution.py:35
  109.5 9.6 %attend_forward.1 = (bf16[768,256]{1,0:T(8,128)(2,1)S(1)}, f32[8,768]{1,0:T(8,128)S(1)}, f32[8,128]{1,0:T(8,128)S(1)}) custom-call(s32[2]{0:T(128)S(1)} %pad_add_fusion.meta_ref, bf16[768,768]{1,0:T(8,128)(2,1)S(1)} %fusion.3.rows_ref, f32[4,1280,256]{2,1,0:T(8,128)} %copy-done.16), custom_call_target="tpu_custom_call" | custom-call | flops 11000000512 | bytes 33000000 | tf_op jit(solution)/shard_map/attend_forward/pallas_call | solution.py:205
  119.8 3.9 convolution_convert_fusion.2
  123.7 3.4 collective-permute-done.5.refs_2_
  127.2 10.5 %all-to-all-done.2 = bf16[4,128,640]{2,1,0:T(8,128)(2,1)S(1)} async-done(((bf16[4,128,640]{2,1,0:T(8,128)(2,1)}), bf16[4,128,640]{2,1,0:T(8,128)(2,1)S(1)}, u32[]{:S(2)}, u32[]{:S(2)}) %all-to-all-start.2) | async-done | bytes 655392 | tf_op jit(solution)/shard_map/all_to_all | solution.py:393
  137.8 3.6 all-gather.7.cloned.1.call-done.grad_ref
  143.4 3.5 all-to-all-start.3
  147.0 2.5 collective-permute-start.9
  150.5 42.1 %reduce-scatter.5.cloned.1.call-done = bf16[96,2048]{1,0:T(8,128)(2,1)} async-done(((bf16[768,2048]{1,0:T(8,128)(2,1)}), bf16[96,2048]{1,0:T(8,128)(2,1)}) %reduce-scatter.5.cloned.1.call-update) | async-done | bytes 393232 | tf_op jit(solution)/shard_map/reduce_scatter | solution.py:448
  198.2 2.6 collective-permute-start.12
  201.8 15.1 %collective-permute-done.12.refs_11_.refs_3_ = bf16[512,640]{1,0:T(8,128)(2,1)S(1)} collective-permute-done((bf16[512,640]{1,0:T(8,128)(2,1)S(1)}, bf16[512,640]{1,0:T(8,128)(2,1)S(1)}, u32[]{:S(2)}, u32[]{:S(2)}) %collective-permute-start.12) | collective-permute-done | bytes 655392 | tf_op jit(solution)/shard_map/ppermute | solution.py:375
  216.8 13.8 %collective-permute-done.11.refs_10_.refs_2_ = bf16[512,640]{1,0:T(8,128)(2,1)S(1)} collective-permute-done((bf16[512,640]{1,0:T(8,128)(2,1)S(1)}, bf16[512,640]{1,0:T(8,128)(2,1)S(1)}, u32[]{:S(2)}, u32[]{:S(2)}) %collective-permute-start.11) | collective-permute-done | bytes 655392 | tf_op jit(solution)/shard_map/ppermute | solution.py:375
  231.5 6.8 %all-gather.9.cloned.1.call-done.rows_ref = bf16[768,2048]{1,0:T(8,128)(2,1)} async-done(((bf16[96,2048]{1,0:T(8,128)(2,1)}), bf16[768,2048]{1,0:T(8,128)(2,1)}) %all-gather.9.cloned.1.call-update) | async-done | bytes 3145744 | tf_op jit(solution)/shard_map/all_gather | solution.py:445
  238.3 19.8 %ffn_both_ways.1 = (bf16[768,640]{1,0:T(8,128)(2,1)}, bf16[768,1280]{1,0:T(8,128)(2,1)}, bf16[768,2048]{1,0:T(8,128)(2,1)}) custom-call(s32[1]{0:T(128)} %bitcast.16.place_ref, bf16[768,2048]{1,0:T(8,128)(2,1)} %all-gather.9.cloned.1.call-done.rows_ref, bf16[768,2048]{1,0:T(8,128)(2,1)} %all-gather.7.cloned.1.call-done.grad_ref, ...), custom_call_target="tpu_custom_call" | custom-call | flops 20899999744 | bytes 62700000 | tf_op jit(solution)/shard_map/ffn_both_ways/pallas_call | solution.py:287
  258.1 4.5 convolution_convert_fusion.5
  267.6 3.8 convolution_convert_fusion.4
  271.4 5.4 %ffn_out.1 = bf16[768,2048]{1,0:T(8,128)(2,1)} custom-call(s32[1]{0:T(128)} %bitcast.16.place_ref, bf16[768,640]{1,0:T(8,128)(2,1)S(1)} %copy-done.17, bf16[512,640]{1,0:T(8,128)(2,1)S(1)} %bitcast.75, bf16[512,640]{1,0:T(8,128)(2,1)} %collective-permute-done.10.refs_9_.refs_1_, bf16[512,640]{1,0:T(8,128)(2,1)S(1)} %copy-done.14, bf16[512,640]{1,0:T(8,128)(2,1)S(1)} %copy-done.12), custom_call_target="tpu_custom_call" | custom-call | flops 5500000256 | bytes 16500000 | tf_op jit(solution)/shard_map/ffn_out/pallas_call | solution.py:313
  276.8 5.7 %convolution_convert_fusion.3 = bf16[2048,640]{0,1:T(8,128)(2,1)} fusion(bf16[768,2048]{1,0:T(8,128)(2,1)} %all-gather.7.cloned.1.call-done.grad_ref, bf16[768,640]{1,0:T(8,128)(2,1)S(1)} %copy-done.17), kind=kOutput, calls=%fused_computation.3 | convolution fusion | flops 2014576640 | bytes 6750208 | tf_op jit(solution)/shard_map/dot_general | solution.py:35
  282.5 13.8 %collective-permute-done.15 = bf16[512,640]{0,1:T(8,128)(2,1)} collective-permute-done((bf16[512,640]{0,1:T(8,128)(2,1)}, bf16[512,640]{0,1:T(8,128)(2,1)}, u32[]{:S(2)}, u32[]{:S(2)}) %collective-permute-start.15) | collective-permute-done | bytes 655392 | tf_op jit(solution)/shard_map/ppermute | solution.py:375
  297.7 2.9 add_convert_fusion.2
  313.5 26.2 %all-gather.11.cloned.1.call-done = bf16[768,2048]{1,0:T(8,128)(2,1)} async-done(((bf16[96,2048]{1,0:T(8,128)(2,1)}), bf16[768,2048]{1,0:T(8,128)(2,1)}) %all-gather.11.cloned.1.call-update) | async-done | bytes 3145744 | tf_op jit(solution)/shard_map/all_gather | solution.py:445
  339.7 17.0 %collective-permute-done.18 = bf16[512,1024]{0,1:T(8,128)(2,1)} collective-permute-done((bf16[512,1024]{0,1:T(8,128)(2,1)}, bf16[512,1024]{0,1:T(8,128)(2,1)}, u32[]{:S(2)}, u32[]{:S(2)}) %collective-permute-start.18) | collective-permute-done | bytes 1048608 | tf_op jit(solution)/shard_map/ppermute | solution.py:375
  366.7 2.3 collective-permute-start.22
  370.7 4.4 all-to-all-start.4
  376.4 14.7 %attend_backward.1 = (bf16[768,768]{1,0:T(8,128)(2,1)S(1)}, f32[8,128]{1,0:T(8,128)S(1)}) custom-call(s32[2]{0:T(128)S(1)} %pad_add_fusion.meta_ref, bf16[768,768]{1,0:T(8,128)(2,1)S(1)} %copy-done.19, bf16[768,256]{1,0:T(8,128)(2,1)S(1)} %convolution_convert_fusion.7.grad_ref, f32[8,768]{1,0:T(8,128)S(1)} %get-tuple-element.73.log_ref, ...), custom_call_target="tpu_custom_call" | custom-call | flops 16499999744 | bytes 49500000 | tf_op jit(solution)/shard_map/attend_backward/pallas_call | solution.py:226
  392.5 3.1 convolution_convert_fusion.1
  401.5 5.9 %convolution_convert_fusion = bf16[768,2048]{1,0:T(8,128)(2,1)} fusion(bf16[768,768]{1,0:T(8,128)(2,1)S(1)} %get-tuple-element.79, bf16[2048,1024]{1,0:T(8,128)(2,1)} %constant_dynamic-update-slice_fusion), kind=kOutput, calls=%fused_computation | convolution fusion | flops 2417491968 | bytes 7471104 | tf_op jit(solution)/shard_map/dot_general | solution.py:35
  408.5 10.2 %collective-permute-done.24 = bf16[512,768]{1,0:T(8,128)(2,1)S(1)} collective-permute-done((bf16[512,768]{1,0:T(8,128)(2,1)}, bf16[512,768]{1,0:T(8,128)(2,1)S(1)}, u32[]{:S(2)}, u32[]{:S(2)}) %collective-permute-start.24) | collective-permute-done | bytes 786464 | tf_op jit(solution)/shard_map/ppermute | solution.py:375
  418.7 11.8 %collective-permute-done.26 = bf16[512,768]{1,0:T(8,128)(2,1)S(1)} collective-permute-done((bf16[512,768]{1,0:T(8,128)(2,1)}, bf16[512,768]{1,0:T(8,128)(2,1)S(1)}, u32[]{:S(2)}, u32[]{:S(2)}) %collective-permute-start.26) | collective-permute-done | bytes 786464 | tf_op jit(solution)/shard_map/ppermute | solution.py:375
  432.0 2.7 add_convert_fusion.1
  434.7 2.8 copy.52
  439.9 2.5 pad_maximum_fusion.1
  443.3 4.8 all-to-all-start.5
  449.4 2.4 fusion.7
  455.9 8.9 %collective-permute-done.30 = f32[16,33]{1,0:T(8,128)S(1)} collective-permute-done((f32[16,33]{1,0:T(8,128)S(1)}, f32[16,33]{1,0:T(8,128)S(1)}, u32[]{:S(2)}, u32[]{:S(2)}) %collective-permute-start.30) | collective-permute-done | bytes 2144 | tf_op jit(solution)/shard_map/ppermute | solution.py:597
  464.8 3.7 collective-permute-start.31
  469.6 4.8 collective-permute-done.31
  (268 shorter events, 105.9 us)
Async XLA Ops:
  13.5 32.2 %all-to-all-start = ((bf16[4,128,1024]{2,1,0:T(8,128)(2,1)}), bf16[4,128,1024]{2,1,0:T(8,128)(2,1)S(1)}, u32[]{:S(2)}, u32[]{:S(2)}) async-start(bf16[4,128,1024]{2,1,0:T(8,128)(2,1)} %bitcast.5), calls=%async_computation | async-start | bytes 2097152 | tf_op jit(solution)/shard_map/all_to_all | solution.py:393
  20.0 79.3 %all-gather.5.cloned.1.call-start = ((), (), s32[]{:S(2)}) async-start(), calls=%async_computation.10 | async-start | bytes 3538944 | tf_op jit(solution)/shard_map/all_gather | solution.py:445
  25.5 45.8 %copy-start.51 = (bf16[128]{0:T(256)(128)(2,1)S(1)}, bf16[128]{0:T(256)(128)(2,1)}, u32[]{:S(2)}) copy-start(bf16[128]{0:T(256)(128)(2,1)} %param.25) | copy-start | bytes 772
  25.5 46.4 %copy-start.1 = (bf16[128,2560]{1,0:T(8,128)(2,1)S(1)}, bf16[128,2560]{1,0:T(8,128)(2,1)}, u32[]{:S(2)}) copy-start(bf16[128,2560]{1,0:T(8,128)(2,1)} %refs_0_.2) | copy-start | bytes 1966084
  45.7 95.7 %all-gather.7.cloned.1.call-start = ((), (), s32[]{:S(2)}) async-start(), calls=%async_computation.11 | async-start | bytes 3538944 | tf_op jit(solution)/shard_map/all_gather | solution.py:445
  45.8 24.2 %collective-permute-start.1 = (bf16[512,1024]{1,0:T(8,128)(2,1)S(1)}, bf16[512,1024]{1,0:T(8,128)(2,1)S(1)}, u32[]{:S(2)}, u32[]{:S(2)}) collective-permute-start(bf16[512,1024]{1,0:T(8,128)(2,1)S(1)} %bitcast.81), channel_id=1, source_target_pairs={{0,16},{8,24},{16,0},{24,8},{1,17},{9,25},{17,1},{25,9},{2,18},{10... | collective-permute-start | bytes 3145736 | tf_op jit(solution)/shard_map/ppermute | solution.py:375
  47.4 24.0 %collective-permute-start = (bf16[512,1024]{1,0:T(8,128)(2,1)S(1)}, bf16[512,1024]{1,0:T(8,128)(2,1)}, u32[]{:S(2)}, u32[]{:S(2)}) collective-permute-start(bf16[512,1024]{1,0:T(8,128)(2,1)S(1)} %bitcast.82), channel_id=1, source_target_pairs={{0,8},{8,0},{16,24},{24,16},{1,9},{9,1},{17,25},{25,17},{2,10},{10... | collective-permute-start | bytes 3145736 | tf_op jit(solution)/shard_map/ppermute | solution.py:375
  73.0 22.7 %all-to-all-start.1 = ((bf16[4,128,640]{2,1,0:T(8,128)(2,1)}), bf16[4,128,640]{2,1,0:T(8,128)(2,1)S(1)}, u32[]{:S(2)}, u32[]{:S(2)}) async-start(bf16[4,128,640]{2,1,0:T(8,128)(2,1)} %bitcast.8), calls=%async_computation.1 | async-start | bytes 1310720 | tf_op jit(solution)/shard_map/all_to_all | solution.py:393
  77.6 11.7 %collective-permute-start.2 = (bf16[256,1024]{1,0:T(8,128)(2,1)S(1)}, bf16[256,1024]{1,0:T(8,128)(2,1)S(1)}, u32[]{:S(2)}, u32[]{:S(2)}) collective-permute-start(bf16[256,1024]{1,0:T(8,128)(2,1)S(1)} %slice.227), channel_id=1, source_target_pairs={{0,16},{8,24},{16,0},{24,8},{1,17},{9,25},{17,1},{25,9},{2,18},{10... | collective-permute-start | bytes 1572872 | tf_op jit(solution)/shard_map/ppermute | solution.py:375
  80.1 11.8 %collective-permute-start.3 = (bf16[256,1024]{1,0:T(8,128)(2,1)S(1)}, bf16[256,1024]{1,0:T(8,128)(2,1)S(1)}, u32[]{:S(2)}, u32[]{:S(2)}) collective-permute-start(bf16[256,1024]{1,0:T(8,128)(2,1)S(1)} %slice.228), channel_id=1, source_target_pairs={{0,8},{8,0},{16,24},{24,16},{1,9},{9,1},{17,25},{25,17},{2,10},{10... | collective-permute-start | bytes 1572872 | tf_op jit(solution)/shard_map/ppermute | solution.py:375
  95.7 28.0 %collective-permute-start.6 = (bf16[512,640]{1,0:T(8,128)(2,1)S(1)}, bf16[512,640]{1,0:T(8,128)(2,1)}, u32[]{:S(2)}, u32[]{:S(2)}) collective-permute-start(bf16[512,640]{1,0:T(8,128)(2,1)S(1)} %bitcast.63), channel_id=1, source_target_pairs={{0,24},{8,16},{16,8},{24,0},{1,25},{9,17},{17,9},{25,1},{2,26},{10... | collective-permute-start | bytes 1966088 | tf_op jit(solution)/shard_map/ppermute | solution.py:375
  98.1 29.0 %collective-permute-start.5 = (bf16[512,640]{1,0:T(8,128)(2,1)S(1)}, bf16[512,640]{1,0:T(8,128)(2,1)}, u32[]{:S(2)}, u32[]{:S(2)}) collective-permute-start(bf16[512,640]{1,0:T(8,128)(2,1)S(1)} %bitcast.64), channel_id=1, source_target_pairs={{0,16},{8,24},{16,0},{24,8},{1,17},{9,25},{17,1},{25,9},{2,18},{10... | collective-permute-start | bytes 1966088 | tf_op jit(solution)/shard_map/ppermute | solution.py:375
  98.7 28.6 %collective-permute-start.4 = (bf16[512,640]{1,0:T(8,128)(2,1)S(1)}, bf16[512,640]{1,0:T(8,128)(2,1)}, u32[]{:S(2)}, u32[]{:S(2)}) collective-permute-start(bf16[512,640]{1,0:T(8,128)(2,1)S(1)} %bitcast.65), channel_id=1, source_target_pairs={{0,8},{8,0},{16,24},{24,16},{1,9},{9,1},{17,25},{25,17},{2,10},{10... | collective-permute-start | bytes 1966088 | tf_op jit(solution)/shard_map/ppermute | solution.py:375
  100.3 37.5 %all-to-all-start.2 = ((bf16[4,128,640]{2,1,0:T(8,128)(2,1)}), bf16[4,128,640]{2,1,0:T(8,128)(2,1)S(1)}, u32[]{:S(2)}, u32[]{:S(2)}) async-start(bf16[4,128,640]{2,1,0:T(8,128)(2,1)} %bitcast.12), calls=%async_computation.2 | async-start | bytes 1310720 | tf_op jit(solution)/shard_map/all_to_all | solution.py:393
  103.8 88.8 %reduce-scatter.5.cloned.1.call-start = ((), (), s32[]{:S(2)}) async-start(), calls=%async_computation.12 | async-start | bytes 3538944 | tf_op jit(solution)/shard_map/reduce_scatter | solution.py:448
  143.4 51.1 %all-to-all-start.3 = ((bf16[4,128,640]{2,1,0:T(8,128)(2,1)}), bf16[4,128,640]{2,1,0:T(8,128)(2,1)S(1)}, u32[]{:S(2)}, u32[]{:S(2)}) async-start(bf16[4,128,640]{2,1,0:T(8,128)(2,1)} %bitcast.14), calls=%async_computation.4 | async-start | bytes 1310720 | tf_op jit(solution)/shard_map/all_to_all | solution.py:393
  146.9 91.4 %all-gather.9.cloned.1.call-start = ((), (), s32[]{:S(2)}) async-start(), calls=%async_computation.13 | async-start | bytes 3538944 | tf_op jit(solution)/shard_map/all_gather | solution.py:445
  147.0 47.6 %collective-permute-start.9 = (bf16[512,640]{1,0:T(8,128)(2,1)S(1)}, bf16[512,640]{1,0:T(8,128)(2,1)}, u32[]{:S(2)}, u32[]{:S(2)}) collective-permute-start(bf16[512,640]{1,0:T(8,128)(2,1)S(1)} %bitcast.67), channel_id=1, source_target_pairs={{0,24},{8,16},{16,8},{24,0},{1,25},{9,17},{17,9},{25,1},{2,26},{10... | collective-permute-start | bytes 1966088 | tf_op jit(solution)/shard_map/ppermute | solution.py:375
  149.4 45.1 %collective-permute-start.8 = (bf16[512,640]{1,0:T(8,128)(2,1)S(1)}, bf16[512,640]{1,0:T(8,128)(2,1)}, u32[]{:S(2)}, u32[]{:S(2)}) collective-permute-start(bf16[512,640]{1,0:T(8,128)(2,1)S(1)} %bitcast.68), channel_id=1, source_target_pairs={{0,16},{8,24},{16,0},{24,8},{1,17},{9,25},{17,1},{25,9},{2,18},{10... | collective-permute-start | bytes 1966088 | tf_op jit(solution)/shard_map/ppermute | solution.py:375
  150.0 44.5 %collective-permute-start.7 = (bf16[512,640]{1,0:T(8,128)(2,1)S(1)}, bf16[512,640]{1,0:T(8,128)(2,1)}, u32[]{:S(2)}, u32[]{:S(2)}) collective-permute-start(bf16[512,640]{1,0:T(8,128)(2,1)S(1)} %bitcast.69), channel_id=1, source_target_pairs={{0,8},{8,0},{16,24},{24,16},{1,9},{9,1},{17,25},{25,17},{2,10},{10... | collective-permute-start | bytes 1966088 | tf_op jit(solution)/shard_map/ppermute | solution.py:375
  197.8 102.8 %reduce-scatter.7.cloned.1.call-start = ((), (), s32[]{:S(2)}) async-start(), calls=%async_computation.14 | async-start | bytes 3538944 | tf_op jit(solution)/shard_map/reduce_scatter | solution.py:448
  198.2 18.6 %collective-permute-start.12 = (bf16[512,640]{1,0:T(8,128)(2,1)S(1)}, bf16[512,640]{1,0:T(8,128)(2,1)S(1)}, u32[]{:S(2)}, u32[]{:S(2)}) collective-permute-start(bf16[512,640]{1,0:T(8,128)(2,1)S(1)} %bitcast.71), channel_id=1, source_target_pairs={{0,24},{8,16},{16,8},{24,0},{1,25},{9,17},{17,9},{25,1},{2,26},{10... | collective-permute-start | bytes 1966088 | tf_op jit(solution)/shard_map/ppermute | solution.py:375
  200.8 29.8 %collective-permute-start.11 = (bf16[512,640]{1,0:T(8,128)(2,1)S(1)}, bf16[512,640]{1,0:T(8,128)(2,1)S(1)}, u32[]{:S(2)}, u32[]{:S(2)}) collective-permute-start(bf16[512,640]{1,0:T(8,128)(2,1)S(1)} %bitcast.72), channel_id=1, source_target_pairs={{0,16},{8,24},{16,0},{24,8},{1,17},{9,25},{17,1},{25,9},{2,18},{10... | collective-permute-start | bytes 1966088 | tf_op jit(solution)/shard_map/ppermute | solution.py:375
  201.4 30.1 %collective-permute-start.10 = (bf16[512,640]{1,0:T(8,128)(2,1)S(1)}, bf16[512,640]{1,0:T(8,128)(2,1)}, u32[]{:S(2)}, u32[]{:S(2)}) collective-permute-start(bf16[512,640]{1,0:T(8,128)(2,1)S(1)} %bitcast.73), channel_id=1, source_target_pairs={{0,8},{8,0},{16,24},{24,16},{1,9},{9,1},{17,25},{25,17},{2,10},{10... | collective-permute-start | bytes 1966088 | tf_op jit(solution)/shard_map/ppermute | solution.py:375
  258.1 81.6 %all-gather.11.cloned.1.call-start = ((), (), s32[]{:S(2)}) async-start(), calls=%async_computation.15 | async-start | bytes 3538944 | tf_op jit(solution)/shard_map/all_gather | solution.py:445
  264.1 18.5 %collective-permute-start.13 = (bf16[512,640]{0,1:T(8,128)(2,1)}, bf16[512,640]{0,1:T(8,128)(2,1)}, u32[]{:S(2)}, u32[]{:S(2)}) collective-permute-start(bf16[512,640]{0,1:T(8,128)(2,1)} %get-tuple-element.98), channel_id=1, source_target_pairs={{0,8},{8,0},{16,24},{24,16},{1,9},{9,1},{17,25},{25,17},{2,10},{10... | collective-permute-start | bytes 1966088 | tf_op jit(solution)/shard_map/ppermute | solution.py:375
  265.5 30.8 %collective-permute-start.15 = (bf16[512,640]{0,1:T(8,128)(2,1)}, bf16[512,640]{0,1:T(8,128)(2,1)}, u32[]{:S(2)}, u32[]{:S(2)}) collective-permute-start(bf16[512,640]{0,1:T(8,128)(2,1)} %get-tuple-element.99), channel_id=1, source_target_pairs={{0,24},{8,16},{16,8},{24,0},{1,25},{9,17},{17,9},{25,1},{2,26},{10... | collective-permute-start | bytes 1966088 | tf_op jit(solution)/shard_map/ppermute | solution.py:375
  267.0 30.7 %collective-permute-start.14 = (bf16[512,640]{0,1:T(8,128)(2,1)}, bf16[512,640]{0,1:T(8,128)(2,1)}, u32[]{:S(2)}, u32[]{:S(2)}) collective-permute-start(bf16[512,640]{0,1:T(8,128)(2,1)} %get-tuple-element.100), channel_id=1, source_target_pairs={{0,16},{8,24},{16,0},{24,8},{1,17},{9,25},{17,1},{25,9},{2,18},{10... | collective-permute-start | bytes 1966088 | tf_op jit(solution)/shard_map/ppermute | solution.py:375
  303.3 176.8 %reduce-scatter.9.cloned.1.call-start = ((), (), s32[]{:S(2)}) async-start(), calls=%async_computation.16 | async-start | bytes 3538944 | tf_op jit(solution)/shard_map/reduce_scatter | solution.py:448
  307.9 31.8 %collective-permute-start.17 = (bf16[512,1024]{0,1:T(8,128)(2,1)}, bf16[512,1024]{0,1:T(8,128)(2,1)S(1)}, u32[]{:S(2)}, u32[]{:S(2)}) collective-permute-start(bf16[512,1024]{0,1:T(8,128)(2,1)} %pad_maximum_fusion.2), channel_id=1, source_target_pairs={{0,8},{8,0},{16,24},{24,16},{1,9},{9,1},{17,25},{25,17},{2,10},{10... | collective-permute-start | bytes 3145736 | tf_op jit(solution)/shard_map/ppermute | solution.py:375
  310.4 46.3 %collective-permute-start.18 = (bf16[512,1024]{0,1:T(8,128)(2,1)}, bf16[512,1024]{0,1:T(8,128)(2,1)}, u32[]{:S(2)}, u32[]{:S(2)}) collective-permute-start(bf16[512,1024]{0,1:T(8,128)(2,1)} %pad_maximum_fusion.3), channel_id=1, source_target_pairs={{0,16},{8,24},{16,0},{24,8},{1,17},{9,25},{17,1},{25,9},{2,18},{10... | collective-permute-start | bytes 3145736 | tf_op jit(solution)/shard_map/ppermute | solution.py:375
  312.0 44.7 %collective-permute-start.19 = (bf16[512,1024]{0,1:T(8,128)(2,1)}, bf16[512,1024]{0,1:T(8,128)(2,1)}, u32[]{:S(2)}, u32[]{:S(2)}) collective-permute-start(bf16[512,1024]{0,1:T(8,128)(2,1)} %pad_maximum_fusion.4), channel_id=1, source_target_pairs={{0,24},{8,16},{16,8},{24,0},{1,25},{9,17},{17,9},{25,1},{2,26},{10... | collective-permute-start | bytes 3145736 | tf_op jit(solution)/shard_map/ppermute | solution.py:375
  363.9 27.2 %collective-permute-start.20 = (bf16[512,512]{0,1:T(8,128)(2,1)}, bf16[512,512]{0,1:T(8,128)(2,1)S(1)}, u32[]{:S(2)}, u32[]{:S(2)}) collective-permute-start(bf16[512,512]{0,1:T(8,128)(2,1)} %pad_maximum_fusion.8), channel_id=1, source_target_pairs={{0,8},{8,0},{16,24},{24,16},{1,9},{9,1},{17,25},{25,17},{2,10},{10... | collective-permute-start | bytes 1572872 | tf_op jit(solution)/shard_map/ppermute | solution.py:375
  365.4 25.8 %collective-permute-start.21 = (bf16[512,512]{0,1:T(8,128)(2,1)}, bf16[512,512]{0,1:T(8,128)(2,1)S(1)}, u32[]{:S(2)}, u32[]{:S(2)}) collective-permute-start(bf16[512,512]{0,1:T(8,128)(2,1)} %pad_maximum_fusion.9), channel_id=1, source_target_pairs={{0,16},{8,24},{16,0},{24,8},{1,17},{9,25},{17,1},{25,9},{2,18},{10... | collective-permute-start | bytes 1572872 | tf_op jit(solution)/shard_map/ppermute | solution.py:375
  366.7 24.4 %collective-permute-start.22 = (bf16[512,512]{0,1:T(8,128)(2,1)}, bf16[512,512]{0,1:T(8,128)(2,1)}, u32[]{:S(2)}, u32[]{:S(2)}) collective-permute-start(bf16[512,512]{0,1:T(8,128)(2,1)} %pad_maximum_fusion.10), channel_id=1, source_target_pairs={{0,24},{8,16},{16,8},{24,0},{1,25},{9,17},{17,9},{25,1},{2,26},{10... | collective-permute-start | bytes 1572872 | tf_op jit(solution)/shard_map/ppermute | solution.py:375
  370.7 64.0 %all-to-all-start.4 = ((bf16[4,128,1664]{1,2,0:T(8,128)(2,1)}), bf16[4,128,1664]{1,2,0:T(8,128)(2,1)}, u32[]{:S(2)}, u32[]{:S(2)}) async-start(bf16[4,128,1664]{1,2,0:T(8,128)(2,1)} %copy_bitcast_fusion), calls=%async_computation.8 | async-start | bytes 3407872 | tf_op jit(solution)/shard_map/all_to_all | solution.py:396
  375.1 106.7 %reduce-scatter.11.cloned.1.call-start = ((), (), s32[]{:S(2)}) async-start(), calls=%async_computation.17 | async-start | bytes 3538944 | tf_op jit(solution)/shard_map/reduce_scatter | solution.py:448
  398.0 20.7 %collective-permute-start.24 = (bf16[512,768]{1,0:T(8,128)(2,1)}, bf16[512,768]{1,0:T(8,128)(2,1)S(1)}, u32[]{:S(2)}, u32[]{:S(2)}) collective-permute-start(bf16[512,768]{1,0:T(8,128)(2,1)} %get-tuple-element.91), channel_id=1, source_target_pairs={{0,8},{8,0},{16,24},{24,16},{1,9},{9,1},{17,25},{25,17},{2,10},{10... | collective-permute-start | bytes 2359304 | tf_op jit(solution)/shard_map/ppermute | solution.py:375
  398.7 31.8 %collective-permute-start.26 = (bf16[512,768]{1,0:T(8,128)(2,1)}, bf16[512,768]{1,0:T(8,128)(2,1)S(1)}, u32[]{:S(2)}, u32[]{:S(2)}) collective-permute-start(bf16[512,768]{1,0:T(8,128)(2,1)} %get-tuple-element.92), channel_id=1, source_target_pairs={{0,24},{8,16},{16,8},{24,0},{1,25},{9,17},{17,9},{25,1},{2,26},{10... | collective-permute-start | bytes 2359304 | tf_op jit(solution)/shard_map/ppermute | solution.py:375
  400.1 31.9 %collective-permute-start.25 = (bf16[512,768]{1,0:T(8,128)(2,1)}, bf16[512,768]{1,0:T(8,128)(2,1)}, u32[]{:S(2)}, u32[]{:S(2)}) collective-permute-start(bf16[512,768]{1,0:T(8,128)(2,1)} %get-tuple-element.93), channel_id=1, source_target_pairs={{0,16},{8,24},{16,0},{24,8},{1,17},{9,25},{17,1},{25,9},{2,18},{10... | collective-permute-start | bytes 2359304 | tf_op jit(solution)/shard_map/ppermute | solution.py:375
  438.5 9.6 %collective-permute-start.28 = (f32[16,33]{1,0:T(8,128)}, f32[16,33]{1,0:T(8,128)}, u32[]{:S(2)}, u32[]{:S(2)}) collective-permute-start(f32[16,33]{1,0:T(8,128)} %broadcast_select_fusion), channel_id=1, source_target_pairs={{0,8},{8,0},{16,24},{24,16},{1,9},{9,1},{17,25},{25,17},{2,10},{10... | collective-permute-start | bytes 6344 | tf_op jit(solution)/shard_map/ppermute | solution.py:375
  443.3 31.5 %all-to-all-start.5 = ((bf16[4,128,1280]{2,1,0:T(8,128)(2,1)}), bf16[4,128,1280]{2,1,0:T(8,128)(2,1)S(1)}, u32[]{:S(2)}, u32[]{:S(2)}) async-start(bf16[4,128,1280]{2,1,0:T(8,128)(2,1)} %bitcast.80), calls=%async_computation.9 | async-start | bytes 2621440 | tf_op jit(solution)/shard_map/all_to_all | solution.py:396
  448.9 3.7 collective-permute-start.29
  452.5 12.3 %collective-permute-start.30 = (f32[16,33]{1,0:T(8,128)S(1)}, f32[16,33]{1,0:T(8,128)S(1)}, u32[]{:S(2)}, u32[]{:S(2)}) collective-permute-start(f32[16,33]{1,0:T(8,128)S(1)} %maximum_select_fusion.4), channel_id=1, source_target_pairs={{0,2},{2,0},{4,6},{6,4},{1,3},{3,1},{5,7},{7,5},{8,10},{10,8},{12,... | collective-permute-start | bytes 6344 | tf_op jit(solution)/shard_map/ppermute | solution.py:597
  464.8 9.6 %collective-permute-start.31 = (f32[16,33]{1,0:T(8,128)S(1)}, f32[16,33]{1,0:T(8,128)S(1)}, u32[]{:S(2)}, u32[]{:S(2)}) collective-permute-start(f32[16,33]{1,0:T(8,128)S(1)} %maximum_select_fusion.3), channel_id=1, source_target_pairs={{0,4},{2,6},{4,0},{6,2},{1,5},{3,7},{5,1},{7,3},{8,12},{10,14},{12... | collective-permute-start | bytes 6344 | tf_op jit(solution)/shard_map/ppermute | solution.py:597
  477.9 2.2 collective-permute-start.27
  481.2 3.7 collective-permute-start.16
  484.3 1.8 collective-permute-start.23
  (54 other events, 400.0 us)
Sparse Core Ops, SparseCore 0:
  45.8 42.0 all-gather.4
  90.1 51.2 all-gather.6
  143.7 48.8 reduce-scatter.4
  197.9 40.3 all-gather.8
  258.2 39.1 reduce-scatter.6
  303.4 36.1 all-gather.10
  341.9 42.6 reduce-scatter.8
  407.6 40.2 reduce-scatter.10

commit v4 on v3

--- a/solution.py
+++ b/solution.py
@@ -252,30 +252,26 @@
     return active, slope
 
 
-def ffn_kernel(
-    place_ref, rows_ref, grad_ref, *refs, count, units, tile
-):
+def ffn_kernel(place_ref, rows_ref, grad_ref, *refs, count, units, tile):
     gates, ups, downs = (refs[n * count : (n + 1) * count] for n in range(3))
-    product_ref, both_ref, terms_ref = refs[3 * count :]
+    product_ref, both_ref, terms_ref, pair_ref, down_ref = refs[3 * count :]
     depth = gates[0].shape[0]
-    spans = [pl.ds(pl.multiple_of((place_ref[0] ^ n) * depth, depth), depth) for n in range(count)]
+    for n in range(count):
+        span = pl.ds(pl.multiple_of((place_ref[0] ^ n) * depth, depth), depth)
+        pair_ref[span, :units] = gates[n][...]
+        pair_ref[span, units:] = ups[n][...]
+        down_ref[span, :] = downs[n][...]
 
     def step(index, carry):
         rows = pl.ds(pl.multiple_of(index * tile, tile), tile)
-        def columns_of(source, pieces):
-            return sum(
-                contract(source[rows, span], piece[...], 1, 0) for span, piece in zip(spans, pieces, strict=True)
-            )
-
-        gate_pre, upward = columns_of(rows_ref, gates), columns_of(rows_ref, ups)
-        grad_product = columns_of(grad_ref, downs)
-        active, slope = gelu_with_slope(gate_pre)
+        pre = contract(rows_ref[rows, :], pair_ref[...], 1, 0)
+        grad_product = contract(grad_ref[rows, :], down_ref[...], 1, 0)
+        upward = pre[:, units:]
+        active, slope = gelu_with_slope(pre[:, :units])
         product_ref[rows, :] = (active * upward).astype(LOW)
         both_ref[rows, :units] = (grad_product * upward * slope).astype(LOW)
         both_ref[rows, units:] = (grad_product * active).astype(LOW)
-        for span, gate, up in zip(spans, gates, ups, strict=True):
-            terms = contract(both_ref[rows, :units], gate[...], 1, 1)
-            terms_ref[rows, span] = (terms + contract(both_ref[rows, units:], up[...], 1, 1)).astype(LOW)
+        terms_ref[rows, :] = contract(both_ref[rows, :], pair_ref[...], 1, 1).astype(LOW)
         return carry
 
     lax.fori_loop(0, rows_ref.shape[0] // tile, step, 0)
@@ -285,7 +281,7 @@
     slots, model = rows_in.shape
     units = downs[0].shape[1]
     return pl.pallas_call(
-        functools.partial(ffn_kernel, count=len(downs), units=units, tile=256),
+        functools.partial(ffn_kernel, count=len(downs), units=units, tile=384),
         out_shape=(
             jax.ShapeDtypeStruct((slots, units), LOW),
             jax.ShapeDtypeStruct((slots, 2 * units), LOW),
@@ -293,6 +289,7 @@
         ),
         in_specs=[whole(pltpu.SMEM)] + [whole()] * (2 + 3 * len(downs)),
         out_specs=(whole(), whole(), whole()),
+        scratch_shapes=[pltpu.VMEM((model, 2 * units), LOW), pltpu.VMEM((model, units), LOW)],
         compiler_params=pltpu.CompilerParams(vmem_limit_bytes=VMEM_LIMIT),
         cost_estimate=lasting(19),
         name="ffn_both_ways",

time: 500 us -> 498 us (level)
  no operation moved by 1% of the time
where the time goes in v4:
time: 498 us; the launch traced here: 492 us
  waiting for transfers between devices  235 us (47%)
  starting transfers between devices  65.4 us (13%)
  Pallas kernels  54.1 us (11%)
  other arithmetic  46.4 us (9%)
  local copies, waits for them, and re-layouts  38.9 us (8%)
  matrix products  35.7 us (7%)
  between operations  16.4 us (3%)
    ppermute x27, waiting for transfers between devices, flip(): return lax.ppermute(value, 'fsdp', [(i, i ^ mask) for i in range(groups)])  110 us
    reduce_scatter x4, waiting for transfers between devices, reduce_rows(): lax.psum_scatter(terms.astype(LOW), ('ctx', 'tp'), scatter_dimension=0, t...  42.1 us
    all_gather x4, waiting for transfers between devices, gather_rows(): return lax.all_gather(piece, ('ctx', 'tp'), axis=0, tiled=True)  36.6 us
    dot_general x9, matrix products, contract(): lax.dot_general(left, right, (((left_dim,), (right_dim,)), ((), ())), pre...  35.7 us
    all_to_all x4, waiting for transfers between devices, spread(): return lax.all_to_all(packed, 'ctx', 0, 0, tiled=True)  32.8 us
    ppermute x27, starting transfers between devices, flip(): return lax.ppermute(value, 'fsdp', [(i, i ^ mask) for i in range(groups)])  31.9 us
    pallas_call x1, Pallas kernels, ffn_both_ways(): pl.pallas_call(functools.partial(ffn_kernel, count=len(downs), units=unit...  17.9 us
    all_to_all x4, starting transfers between devices, spread(): return lax.all_to_all(packed, 'ctx', 0, 0, tiled=True)  16.9 us
  transfers between devices with their start and end apart: 46, of which 25 were waited for; matrix products, arithmetic and copies ran while one was open for 20% of the time, Pallas kernels for 7%

profile of v4, /device:TPU:0, one launch (start us, length us, event | category | flops | bytes accessed | tf_op | source)
XLA Modules:
  0.0 492.3 jit_solution(11870694206172306105)
XLA Ops:
  13.5 6.4 %all-to-all-start = ((bf16[4,128,1024]{2,1,0:T(8,128)(2,1)}), bf16[4,128,1024]{2,1,0:T(8,128)(2,1)S(1)}, u32[]{:S(2)}, u32[]{:S(2)}) async-start(bf16[4,128,1024]{2,1,0:T(8,128)(2,1)} %bitcast.5), calls=%async_computation | async-start | bytes 2097152 | tf_op jit(solution)/shard_map/all_to_all | solution.py:390
  20.8 2.3 bias_master.1.bias_ref
  23.2 2.3 copy-done.16
  26.4 19.3 %all-to-all-done = bf16[4,128,1024]{2,1,0:T(8,128)(2,1)S(1)} async-done(((bf16[4,128,1024]{2,1,0:T(8,128)(2,1)}), bf16[4,128,1024]{2,1,0:T(8,128)(2,1)S(1)}, u32[]{:S(2)}, u32[]{:S(2)}) %all-to-all-start) | async-done | bytes 1048608 | tf_op jit(solution)/shard_map/all_to_all | solution.py:390
  52.7 17.3 %collective-permute-done.1 = bf16[512,1024]{1,0:T(8,128)(2,1)S(1)} collective-permute-done((bf16[512,1024]{1,0:T(8,128)(2,1)S(1)}, bf16[512,1024]{1,0:T(8,128)(2,1)S(1)}, u32[]{:S(2)}, u32[]{:S(2)}) %collective-permute-start.1) | collective-permute-done | bytes 1048608 | tf_op jit(solution)/shard_map/ppermute | solution.py:372
  73.0 3.5 all-to-all-start.1
  81.6 2.6 broadcast_in_dim.76
  85.3 2.4 constant_dynamic-update-slice_fusion.3
  92.8 3.0 all-to-all-done.1
  95.7 2.4 collective-permute-start.6
  100.3 3.5 all-to-all-start.2
  104.0 5.5 %fusion.3.rows_ref = bf16[768,768]{1,0:T(8,128)(2,1)S(1)} fusion(bf16[768,2048]{1,0:T(8,128)(2,1)} %all-gather.5.cloned.1.call-done, bf16[2048,1024]{1,0:T(8,128)(2,1)} %constant_dynamic-update-slice_fusion), kind=kOutput, calls=%fused_computation.23 | convolution fusion | flops 2416508928 | bytes 7471104 | tf_op jit(solution)/shard_map/dot_general | solution.py:35
  109.5 9.6 %attend_forward.1 = (bf16[768,256]{1,0:T(8,128)(2,1)S(1)}, f32[8,768]{1,0:T(8,128)S(1)}, f32[8,128]{1,0:T(8,128)S(1)}) custom-call(s32[2]{0:T(128)S(1)} %pad_add_fusion.meta_ref, bf16[768,768]{1,0:T(8,128)(2,1)S(1)} %fusion.3.rows_ref, f32[4,1280,256]{2,1,0:T(8,128)} %copy-done.16), custom_call_target="tpu_custom_call" | custom-call | flops 11000000512 | bytes 33000000 | tf_op jit(solution)/shard_map/attend_forward/pallas_call | solution.py:205
  119.8 3.9 convolution_convert_fusion.2
  123.7 3.4 collective-permute-done.5.refs_2_
  127.2 10.5 %all-to-all-done.2 = bf16[4,128,640]{2,1,0:T(8,128)(2,1)S(1)} async-done(((bf16[4,128,640]{2,1,0:T(8,128)(2,1)}), bf16[4,128,640]{2,1,0:T(8,128)(2,1)S(1)}, u32[]{:S(2)}, u32[]{:S(2)}) %all-to-all-start.2) | async-done | bytes 655392 | tf_op jit(solution)/shard_map/all_to_all | solution.py:390
  137.8 3.6 all-gather.7.cloned.1.call-done.grad_ref
  143.4 3.5 all-to-all-start.3
  147.0 2.5 collective-permute-start.9
  150.5 42.1 %reduce-scatter.5.cloned.1.call-done = bf16[96,2048]{1,0:T(8,128)(2,1)} async-done(((bf16[768,2048]{1,0:T(8,128)(2,1)}), bf16[96,2048]{1,0:T(8,128)(2,1)}) %reduce-scatter.5.cloned.1.call-update) | async-done | bytes 393232 | tf_op jit(solution)/shard_map/reduce_scatter | solution.py:445
  198.2 2.6 collective-permute-start.12
  201.8 15.1 %collective-permute-done.12.refs_11_.refs_3_ = bf16[512,640]{1,0:T(8,128)(2,1)S(1)} collective-permute-done((bf16[512,640]{1,0:T(8,128)(2,1)S(1)}, bf16[512,640]{1,0:T(8,128)(2,1)S(1)}, u32[]{:S(2)}, u32[]{:S(2)}) %collective-permute-start.12) | collective-permute-done | bytes 655392 | tf_op jit(solution)/shard_map/ppermute | solution.py:372
  216.8 13.8 %collective-permute-done.11.refs_10_.refs_2_ = bf16[512,640]{1,0:T(8,128)(2,1)S(1)} collective-permute-done((bf16[512,640]{1,0:T(8,128)(2,1)S(1)}, bf16[512,640]{1,0:T(8,128)(2,1)S(1)}, u32[]{:S(2)}, u32[]{:S(2)}) %collective-permute-start.11) | collective-permute-done | bytes 655392 | tf_op jit(solution)/shard_map/ppermute | solution.py:372
  231.5 6.8 %all-gather.9.cloned.1.call-done.rows_ref = bf16[768,2048]{1,0:T(8,128)(2,1)} async-done(((bf16[96,2048]{1,0:T(8,128)(2,1)}), bf16[768,2048]{1,0:T(8,128)(2,1)}) %all-gather.9.cloned.1.call-update) | async-done | bytes 3145744 | tf_op jit(solution)/shard_map/all_gather | solution.py:442
  238.3 17.9 %ffn_both_ways.1 = (bf16[768,640]{1,0:T(8,128)(2,1)}, bf16[768,1280]{1,0:T(8,128)(2,1)}, bf16[768,2048]{1,0:T(8,128)(2,1)}) custom-call(s32[1]{0:T(128)} %bitcast.16.place_ref, bf16[768,2048]{1,0:T(8,128)(2,1)} %all-gather.9.cloned.1.call-done.rows_ref, bf16[768,2048]{1,0:T(8,128)(2,1)} %all-gather.7.cloned.1.call-done.grad_ref, ...), custom_call_target="tpu_custom_call" | custom-call | flops 20899999744 | bytes 62700000 | tf_op jit(solution)/shard_map/ffn_both_ways/pallas_call | solution.py:283
  256.2 4.5 convolution_convert_fusion.5
  265.7 3.8 convolution_convert_fusion.4
  269.5 5.4 %ffn_out.1 = bf16[768,2048]{1,0:T(8,128)(2,1)} custom-call(s32[1]{0:T(128)} %bitcast.16.place_ref, bf16[768,640]{1,0:T(8,128)(2,1)S(1)} %copy-done.17, bf16[512,640]{1,0:T(8,128)(2,1)S(1)} %bitcast.75, bf16[512,640]{1,0:T(8,128)(2,1)} %collective-permute-done.10.refs_9_.refs_1_, bf16[512,640]{1,0:T(8,128)(2,1)S(1)} %copy-done.14, bf16[512,640]{1,0:T(8,128)(2,1)S(1)} %copy-done.12), custom_call_target="tpu_custom_call" | custom-call | flops 5500000256 | bytes 16500000 | tf_op jit(solution)/shard_map/ffn_out/pallas_call | solution.py:310
  274.9 5.7 %convolution_convert_fusion.3 = bf16[2048,640]{0,1:T(8,128)(2,1)} fusion(bf16[768,2048]{1,0:T(8,128)(2,1)} %all-gather.7.cloned.1.call-done.grad_ref, bf16[768,640]{1,0:T(8,128)(2,1)S(1)} %copy-done.17), kind=kOutput, calls=%fused_computation.3 | convolution fusion | flops 2014576640 | bytes 6750208 | tf_op jit(solution)/shard_map/dot_general | solution.py:35
  280.6 13.8 %collective-permute-done.15 = bf16[512,640]{0,1:T(8,128)(2,1)} collective-permute-done((bf16[512,640]{0,1:T(8,128)(2,1)}, bf16[512,640]{0,1:T(8,128)(2,1)}, u32[]{:S(2)}, u32[]{:S(2)}) %collective-permute-start.15) | collective-permute-done | bytes 655392 | tf_op jit(solution)/shard_map/ppermute | solution.py:372
  295.8 2.9 add_convert_fusion.2
  311.6 26.2 %all-gather.11.cloned.1.call-done = bf16[768,2048]{1,0:T(8,128)(2,1)} async-done(((bf16[96,2048]{1,0:T(8,128)(2,1)}), bf16[768,2048]{1,0:T(8,128)(2,1)}) %all-gather.11.cloned.1.call-update) | async-done | bytes 3145744 | tf_op jit(solution)/shard_map/all_gather | solution.py:442
  337.8 17.1 %collective-permute-done.18 = bf16[512,1024]{0,1:T(8,128)(2,1)} collective-permute-done((bf16[512,1024]{0,1:T(8,128)(2,1)}, bf16[512,1024]{0,1:T(8,128)(2,1)}, u32[]{:S(2)}, u32[]{:S(2)}) %collective-permute-start.18) | collective-permute-done | bytes 1048608 | tf_op jit(solution)/shard_map/ppermute | solution.py:372
  364.8 2.4 collective-permute-start.22
  368.8 4.4 all-to-all-start.4
  374.5 14.7 %attend_backward.1 = (bf16[768,768]{1,0:T(8,128)(2,1)S(1)}, f32[8,128]{1,0:T(8,128)S(1)}) custom-call(s32[2]{0:T(128)S(1)} %pad_add_fusion.meta_ref, bf16[768,768]{1,0:T(8,128)(2,1)S(1)} %copy-done.19, bf16[768,256]{1,0:T(8,128)(2,1)S(1)} %convolution_convert_fusion.7.grad_ref, f32[8,768]{1,0:T(8,128)S(1)} %get-tuple-element.73.log_ref, ...), custom_call_target="tpu_custom_call" | custom-call | flops 16499999744 | bytes 49500000 | tf_op jit(solution)/shard_map/attend_backward/pallas_call | solution.py:226
  390.6 3.1 convolution_convert_fusion.1
  399.7 5.9 %convolution_convert_fusion = bf16[768,2048]{1,0:T(8,128)(2,1)} fusion(bf16[768,768]{1,0:T(8,128)(2,1)S(1)} %get-tuple-element.79, bf16[2048,1024]{1,0:T(8,128)(2,1)} %constant_dynamic-update-slice_fusion), kind=kOutput, calls=%fused_computation | convolution fusion | flops 2417491968 | bytes 7471104 | tf_op jit(solution)/shard_map/dot_general | solution.py:35
  406.7 10.2 %collective-permute-done.24 = bf16[512,768]{1,0:T(8,128)(2,1)S(1)} collective-permute-done((bf16[512,768]{1,0:T(8,128)(2,1)}, bf16[512,768]{1,0:T(8,128)(2,1)S(1)}, u32[]{:S(2)}, u32[]{:S(2)}) %collective-permute-start.24) | collective-permute-done | bytes 786464 | tf_op jit(solution)/shard_map/ppermute | solution.py:372
  416.9 11.7 %collective-permute-done.26 = bf16[512,768]{1,0:T(8,128)(2,1)S(1)} collective-permute-done((bf16[512,768]{1,0:T(8,128)(2,1)}, bf16[512,768]{1,0:T(8,128)(2,1)S(1)}, u32[]{:S(2)}, u32[]{:S(2)}) %collective-permute-start.26) | collective-permute-done | bytes 786464 | tf_op jit(solution)/shard_map/ppermute | solution.py:372
  430.1 2.7 add_convert_fusion.1
  432.8 2.8 copy.52
  438.1 2.5 pad_maximum_fusion.1
  441.4 4.8 all-to-all-start.5
  447.5 2.4 fusion.7
  454.1 8.9 %collective-permute-done.30 = f32[16,33]{1,0:T(8,128)S(1)} collective-permute-done((f32[16,33]{1,0:T(8,128)S(1)}, f32[16,33]{1,0:T(8,128)S(1)}, u32[]{:S(2)}, u32[]{:S(2)}) %collective-permute-start.30) | collective-permute-done | bytes 2144 | tf_op jit(solution)/shard_map/ppermute | solution.py:594
  463.0 3.6 collective-permute-start.31
  467.7 4.9 collective-permute-done.31
  (268 shorter events, 105.9 us)
Async XLA Ops:
  13.5 32.2 %all-to-all-start = ((bf16[4,128,1024]{2,1,0:T(8,128)(2,1)}), bf16[4,128,1024]{2,1,0:T(8,128)(2,1)S(1)}, u32[]{:S(2)}, u32[]{:S(2)}) async-start(bf16[4,128,1024]{2,1,0:T(8,128)(2,1)} %bitcast.5), calls=%async_computation | async-start | bytes 2097152 | tf_op jit(solution)/shard_map/all_to_all | solution.py:390
  20.0 79.3 %all-gather.5.cloned.1.call-start = ((), (), s32[]{:S(2)}) async-start(), calls=%async_computation.10 | async-start | bytes 3538944 | tf_op jit(solution)/shard_map/all_gather | solution.py:442
  25.5 45.8 %copy-start.51 = (bf16[128]{0:T(256)(128)(2,1)S(1)}, bf16[128]{0:T(256)(128)(2,1)}, u32[]{:S(2)}) copy-start(bf16[128]{0:T(256)(128)(2,1)} %param.25) | copy-start | bytes 772
  25.5 46.4 %copy-start.1 = (bf16[128,2560]{1,0:T(8,128)(2,1)S(1)}, bf16[128,2560]{1,0:T(8,128)(2,1)}, u32[]{:S(2)}) copy-start(bf16[128,2560]{1,0:T(8,128)(2,1)} %refs_0_.2) | copy-start | bytes 1966084
  45.7 95.7 %all-gather.7.cloned.1.call-start = ((), (), s32[]{:S(2)}) async-start(), calls=%async_computation.11 | async-start | bytes 3538944 | tf_op jit(solution)/shard_map/all_gather | solution.py:442
  45.8 24.2 %collective-permute-start.1 = (bf16[512,1024]{1,0:T(8,128)(2,1)S(1)}, bf16[512,1024]{1,0:T(8,128)(2,1)S(1)}, u32[]{:S(2)}, u32[]{:S(2)}) collective-permute-start(bf16[512,1024]{1,0:T(8,128)(2,1)S(1)} %bitcast.81), channel_id=1, source_target_pairs={{0,16},{8,24},{16,0},{24,8},{1,17},{9,25},{17,1},{25,9},{2,18},{10... | collective-permute-start | bytes 3145736 | tf_op jit(solution)/shard_map/ppermute | solution.py:372
  47.4 24.0 %collective-permute-start = (bf16[512,1024]{1,0:T(8,128)(2,1)S(1)}, bf16[512,1024]{1,0:T(8,128)(2,1)}, u32[]{:S(2)}, u32[]{:S(2)}) collective-permute-start(bf16[512,1024]{1,0:T(8,128)(2,1)S(1)} %bitcast.82), channel_id=1, source_target_pairs={{0,8},{8,0},{16,24},{24,16},{1,9},{9,1},{17,25},{25,17},{2,10},{10... | collective-permute-start | bytes 3145736 | tf_op jit(solution)/shard_map/ppermute | solution.py:372
  73.0 22.7 %all-to-all-start.1 = ((bf16[4,128,640]{2,1,0:T(8,128)(2,1)}), bf16[4,128,640]{2,1,0:T(8,128)(2,1)S(1)}, u32[]{:S(2)}, u32[]{:S(2)}) async-start(bf16[4,128,640]{2,1,0:T(8,128)(2,1)} %bitcast.8), calls=%async_computation.1 | async-start | bytes 1310720 | tf_op jit(solution)/shard_map/all_to_all | solution.py:390
  77.6 11.7 %collective-permute-start.2 = (bf16[256,1024]{1,0:T(8,128)(2,1)S(1)}, bf16[256,1024]{1,0:T(8,128)(2,1)S(1)}, u32[]{:S(2)}, u32[]{:S(2)}) collective-permute-start(bf16[256,1024]{1,0:T(8,128)(2,1)S(1)} %slice.227), channel_id=1, source_target_pairs={{0,16},{8,24},{16,0},{24,8},{1,17},{9,25},{17,1},{25,9},{2,18},{10... | collective-permute-start | bytes 1572872 | tf_op jit(solution)/shard_map/ppermute | solution.py:372
  80.1 11.8 %collective-permute-start.3 = (bf16[256,1024]{1,0:T(8,128)(2,1)S(1)}, bf16[256,1024]{1,0:T(8,128)(2,1)S(1)}, u32[]{:S(2)}, u32[]{:S(2)}) collective-permute-start(bf16[256,1024]{1,0:T(8,128)(2,1)S(1)} %slice.228), channel_id=1, source_target_pairs={{0,8},{8,0},{16,24},{24,16},{1,9},{9,1},{17,25},{25,17},{2,10},{10... | collective-permute-start | bytes 1572872 | tf_op jit(solution)/shard_map/ppermute | solution.py:372
  95.7 28.0 %collective-permute-start.6 = (bf16[512,640]{1,0:T(8,128)(2,1)S(1)}, bf16[512,640]{1,0:T(8,128)(2,1)}, u32[]{:S(2)}, u32[]{:S(2)}) collective-permute-start(bf16[512,640]{1,0:T(8,128)(2,1)S(1)} %bitcast.63), channel_id=1, source_target_pairs={{0,24},{8,16},{16,8},{24,0},{1,25},{9,17},{17,9},{25,1},{2,26},{10... | collective-permute-start | bytes 1966088 | tf_op jit(solution)/shard_map/ppermute | solution.py:372
  98.1 29.0 %collective-permute-start.5 = (bf16[512,640]{1,0:T(8,128)(2,1)S(1)}, bf16[512,640]{1,0:T(8,128)(2,1)}, u32[]{:S(2)}, u32[]{:S(2)}) collective-permute-start(bf16[512,640]{1,0:T(8,128)(2,1)S(1)} %bitcast.64), channel_id=1, source_target_pairs={{0,16},{8,24},{16,0},{24,8},{1,17},{9,25},{17,1},{25,9},{2,18},{10... | collective-permute-start | bytes 1966088 | tf_op jit(solution)/shard_map/ppermute | solution.py:372
  98.7 28.6 %collective-permute-start.4 = (bf16[512,640]{1,0:T(8,128)(2,1)S(1)}, bf16[512,640]{1,0:T(8,128)(2,1)}, u32[]{:S(2)}, u32[]{:S(2)}) collective-permute-start(bf16[512,640]{1,0:T(8,128)(2,1)S(1)} %bitcast.65), channel_id=1, source_target_pairs={{0,8},{8,0},{16,24},{24,16},{1,9},{9,1},{17,25},{25,17},{2,10},{10... | collective-permute-start | bytes 1966088 | tf_op jit(solution)/shard_map/ppermute | solution.py:372
  100.3 37.5 %all-to-all-start.2 = ((bf16[4,128,640]{2,1,0:T(8,128)(2,1)}), bf16[4,128,640]{2,1,0:T(8,128)(2,1)S(1)}, u32[]{:S(2)}, u32[]{:S(2)}) async-start(bf16[4,128,640]{2,1,0:T(8,128)(2,1)} %bitcast.12), calls=%async_computation.2 | async-start | bytes 1310720 | tf_op jit(solution)/shard_map/all_to_all | solution.py:390
  103.8 88.8 %reduce-scatter.5.cloned.1.call-start = ((), (), s32[]{:S(2)}) async-start(), calls=%async_computation.12 | async-start | bytes 3538944 | tf_op jit(solution)/shard_map/reduce_scatter | solution.py:445
  143.4 51.1 %all-to-all-start.3 = ((bf16[4,128,640]{2,1,0:T(8,128)(2,1)}), bf16[4,128,640]{2,1,0:T(8,128)(2,1)S(1)}, u32[]{:S(2)}, u32[]{:S(2)}) async-start(bf16[4,128,640]{2,1,0:T(8,128)(2,1)} %bitcast.14), calls=%async_computation.4 | async-start | bytes 1310720 | tf_op jit(solution)/shard_map/all_to_all | solution.py:390
  146.9 91.4 %all-gather.9.cloned.1.call-start = ((), (), s32[]{:S(2)}) async-start(), calls=%async_computation.13 | async-start | bytes 3538944 | tf_op jit(solution)/shard_map/all_gather | solution.py:442
  147.0 47.6 %collective-permute-start.9 = (bf16[512,640]{1,0:T(8,128)(2,1)S(1)}, bf16[512,640]{1,0:T(8,128)(2,1)}, u32[]{:S(2)}, u32[]{:S(2)}) collective-permute-start(bf16[512,640]{1,0:T(8,128)(2,1)S(1)} %bitcast.67), channel_id=1, source_target_pairs={{0,24},{8,16},{16,8},{24,0},{1,25},{9,17},{17,9},{25,1},{2,26},{10... | collective-permute-start | bytes 1966088 | tf_op jit(solution)/shard_map/ppermute | solution.py:372
  149.4 45.1 %collective-permute-start.8 = (bf16[512,640]{1,0:T(8,128)(2,1)S(1)}, bf16[512,640]{1,0:T(8,128)(2,1)}, u32[]{:S(2)}, u32[]{:S(2)}) collective-permute-start(bf16[512,640]{1,0:T(8,128)(2,1)S(1)} %bitcast.68), channel_id=1, source_target_pairs={{0,16},{8,24},{16,0},{24,8},{1,17},{9,25},{17,1},{25,9},{2,18},{10... | collective-permute-start | bytes 1966088 | tf_op jit(solution)/shard_map/ppermute | solution.py:372
  150.0 44.5 %collective-permute-start.7 = (bf16[512,640]{1,0:T(8,128)(2,1)S(1)}, bf16[512,640]{1,0:T(8,128)(2,1)}, u32[]{:S(2)}, u32[]{:S(2)}) collective-permute-start(bf16[512,640]{1,0:T(8,128)(2,1)S(1)} %bitcast.69), channel_id=1, source_target_pairs={{0,8},{8,0},{16,24},{24,16},{1,9},{9,1},{17,25},{25,17},{2,10},{10... | collective-permute-start | bytes 1966088 | tf_op jit(solution)/shard_map/ppermute | solution.py:372
  197.8 100.9 %reduce-scatter.7.cloned.1.call-start = ((), (), s32[]{:S(2)}) async-start(), calls=%async_computation.14 | async-start | bytes 3538944 | tf_op jit(solution)/shard_map/reduce_scatter | solution.py:445
  198.2 18.6 %collective-permute-start.12 = (bf16[512,640]{1,0:T(8,128)(2,1)S(1)}, bf16[512,640]{1,0:T(8,128)(2,1)S(1)}, u32[]{:S(2)}, u32[]{:S(2)}) collective-permute-start(bf16[512,640]{1,0:T(8,128)(2,1)S(1)} %bitcast.71), channel_id=1, source_target_pairs={{0,24},{8,16},{16,8},{24,0},{1,25},{9,17},{17,9},{25,1},{2,26},{10... | collective-permute-start | bytes 1966088 | tf_op jit(solution)/shard_map/ppermute | solution.py:372
  200.8 29.8 %collective-permute-start.11 = (bf16[512,640]{1,0:T(8,128)(2,1)S(1)}, bf16[512,640]{1,0:T(8,128)(2,1)S(1)}, u32[]{:S(2)}, u32[]{:S(2)}) collective-permute-start(bf16[512,640]{1,0:T(8,128)(2,1)S(1)} %bitcast.72), channel_id=1, source_target_pairs={{0,16},{8,24},{16,0},{24,8},{1,17},{9,25},{17,1},{25,9},{2,18},{10... | collective-permute-start | bytes 1966088 | tf_op jit(solution)/shard_map/ppermute | solution.py:372
  201.4 30.1 %collective-permute-start.10 = (bf16[512,640]{1,0:T(8,128)(2,1)S(1)}, bf16[512,640]{1,0:T(8,128)(2,1)}, u32[]{:S(2)}, u32[]{:S(2)}) collective-permute-start(bf16[512,640]{1,0:T(8,128)(2,1)S(1)} %bitcast.73), channel_id=1, source_target_pairs={{0,8},{8,0},{16,24},{24,16},{1,9},{9,1},{17,25},{25,17},{2,10},{10... | collective-permute-start | bytes 1966088 | tf_op jit(solution)/shard_map/ppermute | solution.py:372
  256.2 81.6 %all-gather.11.cloned.1.call-start = ((), (), s32[]{:S(2)}) async-start(), calls=%async_computation.15 | async-start | bytes 3538944 | tf_op jit(solution)/shard_map/all_gather | solution.py:442
  262.2 18.5 %collective-permute-start.13 = (bf16[512,640]{0,1:T(8,128)(2,1)}, bf16[512,640]{0,1:T(8,128)(2,1)}, u32[]{:S(2)}, u32[]{:S(2)}) collective-permute-start(bf16[512,640]{0,1:T(8,128)(2,1)} %get-tuple-element.98), channel_id=1, source_target_pairs={{0,8},{8,0},{16,24},{24,16},{1,9},{9,1},{17,25},{25,17},{2,10},{10... | collective-permute-start | bytes 1966088 | tf_op jit(solution)/shard_map/ppermute | solution.py:372
  263.6 30.8 %collective-permute-start.15 = (bf16[512,640]{0,1:T(8,128)(2,1)}, bf16[512,640]{0,1:T(8,128)(2,1)}, u32[]{:S(2)}, u32[]{:S(2)}) collective-permute-start(bf16[512,640]{0,1:T(8,128)(2,1)} %get-tuple-element.99), channel_id=1, source_target_pairs={{0,24},{8,16},{16,8},{24,0},{1,25},{9,17},{17,9},{25,1},{2,26},{10... | collective-permute-start | bytes 1966088 | tf_op jit(solution)/shard_map/ppermute | solution.py:372
  265.1 30.7 %collective-permute-start.14 = (bf16[512,640]{0,1:T(8,128)(2,1)}, bf16[512,640]{0,1:T(8,128)(2,1)}, u32[]{:S(2)}, u32[]{:S(2)}) collective-permute-start(bf16[512,640]{0,1:T(8,128)(2,1)} %get-tuple-element.100), channel_id=1, source_target_pairs={{0,16},{8,24},{16,0},{24,8},{1,17},{9,25},{17,1},{25,9},{2,18},{10... | collective-permute-start | bytes 1966088 | tf_op jit(solution)/shard_map/ppermute | solution.py:372
  301.4 176.9 %reduce-scatter.9.cloned.1.call-start = ((), (), s32[]{:S(2)}) async-start(), calls=%async_computation.16 | async-start | bytes 3538944 | tf_op jit(solution)/shard_map/reduce_scatter | solution.py:445
  306.0 31.8 %collective-permute-start.17 = (bf16[512,1024]{0,1:T(8,128)(2,1)}, bf16[512,1024]{0,1:T(8,128)(2,1)S(1)}, u32[]{:S(2)}, u32[]{:S(2)}) collective-permute-start(bf16[512,1024]{0,1:T(8,128)(2,1)} %pad_maximum_fusion.2), channel_id=1, source_target_pairs={{0,8},{8,0},{16,24},{24,16},{1,9},{9,1},{17,25},{25,17},{2,10},{10... | collective-permute-start | bytes 3145736 | tf_op jit(solution)/shard_map/ppermute | solution.py:372
  308.5 46.4 %collective-permute-start.18 = (bf16[512,1024]{0,1:T(8,128)(2,1)}, bf16[512,1024]{0,1:T(8,128)(2,1)}, u32[]{:S(2)}, u32[]{:S(2)}) collective-permute-start(bf16[512,1024]{0,1:T(8,128)(2,1)} %pad_maximum_fusion.3), channel_id=1, source_target_pairs={{0,16},{8,24},{16,0},{24,8},{1,17},{9,25},{17,1},{25,9},{2,18},{10... | collective-permute-start | bytes 3145736 | tf_op jit(solution)/shard_map/ppermute | solution.py:372
  310.1 44.7 %collective-permute-start.19 = (bf16[512,1024]{0,1:T(8,128)(2,1)}, bf16[512,1024]{0,1:T(8,128)(2,1)}, u32[]{:S(2)}, u32[]{:S(2)}) collective-permute-start(bf16[512,1024]{0,1:T(8,128)(2,1)} %pad_maximum_fusion.4), channel_id=1, source_target_pairs={{0,24},{8,16},{16,8},{24,0},{1,25},{9,17},{17,9},{25,1},{2,26},{10... | collective-permute-start | bytes 3145736 | tf_op jit(solution)/shard_map/ppermute | solution.py:372
  362.1 27.2 %collective-permute-start.20 = (bf16[512,512]{0,1:T(8,128)(2,1)}, bf16[512,512]{0,1:T(8,128)(2,1)S(1)}, u32[]{:S(2)}, u32[]{:S(2)}) collective-permute-start(bf16[512,512]{0,1:T(8,128)(2,1)} %pad_maximum_fusion.8), channel_id=1, source_target_pairs={{0,8},{8,0},{16,24},{24,16},{1,9},{9,1},{17,25},{25,17},{2,10},{10... | collective-permute-start | bytes 1572872 | tf_op jit(solution)/shard_map/ppermute | solution.py:372
  363.5 25.8 %collective-permute-start.21 = (bf16[512,512]{0,1:T(8,128)(2,1)}, bf16[512,512]{0,1:T(8,128)(2,1)S(1)}, u32[]{:S(2)}, u32[]{:S(2)}) collective-permute-start(bf16[512,512]{0,1:T(8,128)(2,1)} %pad_maximum_fusion.9), channel_id=1, source_target_pairs={{0,16},{8,24},{16,0},{24,8},{1,17},{9,25},{17,1},{25,9},{2,18},{10... | collective-permute-start | bytes 1572872 | tf_op jit(solution)/shard_map/ppermute | solution.py:372
  364.8 24.4 %collective-permute-start.22 = (bf16[512,512]{0,1:T(8,128)(2,1)}, bf16[512,512]{0,1:T(8,128)(2,1)}, u32[]{:S(2)}, u32[]{:S(2)}) collective-permute-start(bf16[512,512]{0,1:T(8,128)(2,1)} %pad_maximum_fusion.10), channel_id=1, source_target_pairs={{0,24},{8,16},{16,8},{24,0},{1,25},{9,17},{17,9},{25,1},{2,26},{10... | collective-permute-start | bytes 1572872 | tf_op jit(solution)/shard_map/ppermute | solution.py:372
  368.8 64.0 %all-to-all-start.4 = ((bf16[4,128,1664]{1,2,0:T(8,128)(2,1)}), bf16[4,128,1664]{1,2,0:T(8,128)(2,1)}, u32[]{:S(2)}, u32[]{:S(2)}) async-start(bf16[4,128,1664]{1,2,0:T(8,128)(2,1)} %copy_bitcast_fusion), calls=%async_computation.8 | async-start | bytes 3407872 | tf_op jit(solution)/shard_map/all_to_all | solution.py:393
  373.2 106.7 %reduce-scatter.11.cloned.1.call-start = ((), (), s32[]{:S(2)}) async-start(), calls=%async_computation.17 | async-start | bytes 3538944 | tf_op jit(solution)/shard_map/reduce_scatter | solution.py:445
  396.2 20.7 %collective-permute-start.24 = (bf16[512,768]{1,0:T(8,128)(2,1)}, bf16[512,768]{1,0:T(8,128)(2,1)S(1)}, u32[]{:S(2)}, u32[]{:S(2)}) collective-permute-start(bf16[512,768]{1,0:T(8,128)(2,1)} %get-tuple-element.91), channel_id=1, source_target_pairs={{0,8},{8,0},{16,24},{24,16},{1,9},{9,1},{17,25},{25,17},{2,10},{10... | collective-permute-start | bytes 2359304 | tf_op jit(solution)/shard_map/ppermute | solution.py:372
  396.8 31.8 %collective-permute-start.26 = (bf16[512,768]{1,0:T(8,128)(2,1)}, bf16[512,768]{1,0:T(8,128)(2,1)S(1)}, u32[]{:S(2)}, u32[]{:S(2)}) collective-permute-start(bf16[512,768]{1,0:T(8,128)(2,1)} %get-tuple-element.92), channel_id=1, source_target_pairs={{0,24},{8,16},{16,8},{24,0},{1,25},{9,17},{17,9},{25,1},{2,26},{10... | collective-permute-start | bytes 2359304 | tf_op jit(solution)/shard_map/ppermute | solution.py:372
  398.3 31.8 %collective-permute-start.25 = (bf16[512,768]{1,0:T(8,128)(2,1)}, bf16[512,768]{1,0:T(8,128)(2,1)}, u32[]{:S(2)}, u32[]{:S(2)}) collective-permute-start(bf16[512,768]{1,0:T(8,128)(2,1)} %get-tuple-element.93), channel_id=1, source_target_pairs={{0,16},{8,24},{16,0},{24,8},{1,17},{9,25},{17,1},{25,9},{2,18},{10... | collective-permute-start | bytes 2359304 | tf_op jit(solution)/shard_map/ppermute | solution.py:372
  436.6 9.7 %collective-permute-start.28 = (f32[16,33]{1,0:T(8,128)}, f32[16,33]{1,0:T(8,128)}, u32[]{:S(2)}, u32[]{:S(2)}) collective-permute-start(f32[16,33]{1,0:T(8,128)} %broadcast_select_fusion), channel_id=1, source_target_pairs={{0,8},{8,0},{16,24},{24,16},{1,9},{9,1},{17,25},{25,17},{2,10},{10... | collective-permute-start | bytes 6344 | tf_op jit(solution)/shard_map/ppermute | solution.py:372
  441.4 31.5 %all-to-all-start.5 = ((bf16[4,128,1280]{2,1,0:T(8,128)(2,1)}), bf16[4,128,1280]{2,1,0:T(8,128)(2,1)S(1)}, u32[]{:S(2)}, u32[]{:S(2)}) async-start(bf16[4,128,1280]{2,1,0:T(8,128)(2,1)} %bitcast.80), calls=%async_computation.9 | async-start | bytes 2621440 | tf_op jit(solution)/shard_map/all_to_all | solution.py:393
  447.0 3.7 collective-permute-start.29
  450.7 12.3 %collective-permute-start.30 = (f32[16,33]{1,0:T(8,128)S(1)}, f32[16,33]{1,0:T(8,128)S(1)}, u32[]{:S(2)}, u32[]{:S(2)}) collective-permute-start(f32[16,33]{1,0:T(8,128)S(1)} %maximum_select_fusion.4), channel_id=1, source_target_pairs={{0,2},{2,0},{4,6},{6,4},{1,3},{3,1},{5,7},{7,5},{8,10},{10,8},{12,... | collective-permute-start | bytes 6344 | tf_op jit(solution)/shard_map/ppermute | solution.py:594
  463.0 9.6 %collective-permute-start.31 = (f32[16,33]{1,0:T(8,128)S(1)}, f32[16,33]{1,0:T(8,128)S(1)}, u32[]{:S(2)}, u32[]{:S(2)}) collective-permute-start(f32[16,33]{1,0:T(8,128)S(1)} %maximum_select_fusion.3), channel_id=1, source_target_pairs={{0,4},{2,6},{4,0},{6,2},{1,5},{3,7},{5,1},{7,3},{8,12},{10,14},{12... | collective-permute-start | bytes 6344 | tf_op jit(solution)/shard_map/ppermute | solution.py:594
  476.0 2.2 collective-permute-start.27
  479.4 3.7 collective-permute-start.16
  482.4 1.8 collective-permute-start.23
  (54 other events, 400.1 us)
Sparse Core Ops, SparseCore 0:
  45.8 42.0 all-gather.4
  90.1 51.2 all-gather.6
  143.7 48.8 reduce-scatter.4
  197.9 40.3 all-gather.8
  256.3 39.2 reduce-scatter.6
  301.5 36.2 all-gather.10
  340.1 42.7 reduce-scatter.8
  405.7 40.2 reduce-scatter.10
